TPU v7x, 32 devices: a whole 2x2x4 slice. The times are simulated.
32 devices in a mesh: alpha: 8 (over z, y), beta: 4 (over x, core).
Axes of the slice: x: 2, y: 2, z: 4, core: 2. Of those that a mesh axis runs over, the one named last changes fastest.
Arguments:
- ci_vector: float32 [1024, 1024], P('alpha', 'beta'), may hold values from -6 to 6
- one_body: float32 [102], replicated, may hold values from -1 to 1
- pair_integrals: bfloat16 [102, 102], replicated, may hold values from -0.15625 to 0.15625
- beta_target: int32 [40, 1024], P(None, 'beta'), may hold values from 0 to 1023
- beta_pair: int32 [40, 1024], P(None, 'beta'), may hold values from 0 to 101
- beta_sign: int32 [40, 1024], P(None, 'beta'), may hold values 0 or 1
- alpha_target: int32 [40, 1024], P(None, 'alpha'), may hold values from 0 to 1023
- alpha_pair: int32 [40, 1024], P(None, 'alpha'), may hold values from 0 to 101
- alpha_sign: int32 [40, 1024], P(None, 'alpha'), may hold values 0 or 1
Outputs:
- sigma_vector: float32 [1024, 1024], P('alpha', 'beta')
All inputs are finite; a program needn't handle non-finite values. No bound on the sum of `beta_sign` or of `alpha_sign` on one device may be relied on, other than what follows from the above.
Results may differ from a plain program's by a relative error of at most 0.0035.
Values may be sent and summed in bfloat16 or wider, within the bound.
No kernel may reach another device: no remote copies, remote signals or barrier semaphores. Data moves between devices by JAX's collectives and lax.ppermute only.
A program may use at most 128 MiB of HBM per device.

v0:
```python
import jax
import jax.numpy as jnp
from jax import lax
from jax.sharding import PartitionSpec as P

precise = lax.Precision.HIGHEST


def shards(
    ci_vector,
    one_body,
    pair_integrals,
    beta_target,
    beta_pair,
    beta_sign,
    alpha_target,
    alpha_pair,
    alpha_sign,
):
    alpha_count = ci_vector.shape[0]
    beta_count = ci_vector.shape[1]
    pair_count = one_body.shape[0]
    total_alpha = alpha_count * lax.axis_size("alpha")
    civec_bf = ci_vector.astype(jnp.bfloat16)
    rows_whole = lax.all_gather(civec_bf, "beta", axis=1, tiled=True)
    total_beta = rows_whole.shape[1]
    pair_ids = jnp.arange(pair_count, dtype=jnp.int32)
    beta_hot = (
        (2 * beta_sign - 1)[:, :, None] * (beta_pair[:, :, None] == pair_ids).astype(jnp.int32)
    ).astype(jnp.bfloat16)
    alpha_signed = (2 * alpha_sign - 1)[:, :, None] * (alpha_pair[:, :, None] == pair_ids).astype(
        jnp.int32
    )
    alpha_hot = alpha_signed.astype(jnp.bfloat16)
    alpha_level = jnp.einsum(
        "eaq,q->ea", alpha_signed.astype(jnp.float32), one_body, precision=precise
    )
    col_block = min(128, beta_count)
    col_blocks = beta_count // col_block
    string_ids = jnp.arange(total_beta, dtype=jnp.int32)

    def beta_block(block_index):
        start = block_index * col_block
        targets = lax.dynamic_slice_in_dim(beta_target, start, col_block, 1)
        hot_cols = lax.dynamic_slice_in_dim(beta_hot, start, col_block, 1)
        coupling = (targets[None, :, :] == string_ids[:, None, None]).astype(jnp.bfloat16)
        picked = jnp.einsum(
            "aj,jei->aei", rows_whole, coupling, preferred_element_type=jnp.float32
        ).astype(jnp.bfloat16)
        return jnp.einsum("aei,eip->pai", picked, hot_cols, preferred_element_type=jnp.float32)

    blocks = lax.map(beta_block, jnp.arange(col_blocks, dtype=jnp.int32))
    density = jnp.transpose(blocks, (1, 2, 0, 3)).reshape(pair_count, alpha_count, beta_count)
    same_beta = jnp.einsum("p,pai->ai", one_body, density, precision=precise)
    density_bf = density.astype(jnp.bfloat16)
    mixed = jnp.einsum(
        "qp,pai->qai", pair_integrals, density_bf, preferred_element_type=jnp.float32
    ).astype(jnp.bfloat16)
    alpha_ids = jnp.arange(total_alpha, dtype=jnp.int32)
    block_rows = 32

    def accumulate(partial_value, block_index):
        offset = block_index * block_rows
        hot_rows = lax.dynamic_slice_in_dim(alpha_hot, offset, block_rows, 1)
        mixed_rows = lax.dynamic_slice_in_dim(mixed, offset, block_rows, 1)
        lifted_bf = jnp.einsum(
            "eaq,qai->aei", hot_rows, mixed_rows, preferred_element_type=jnp.float32
        ).astype(jnp.bfloat16)
        targets = lax.dynamic_slice_in_dim(alpha_target, offset, block_rows, 1)
        matches = targets.T[None, :, :] == alpha_ids[:, None, None]
        spread = matches.astype(jnp.bfloat16)
        partial_value = partial_value + jnp.einsum(
            "bae,aei->bi", spread, lifted_bf, preferred_element_type=jnp.float32
        )
        level_rows = lax.dynamic_slice_in_dim(alpha_level, offset, block_rows, 1)
        level_map = jnp.sum(jnp.where(matches, level_rows.T[None, :, :], jnp.float32(0.0)), axis=2)
        own_block = lax.dynamic_slice_in_dim(civec_bf, offset, block_rows, 0).astype(jnp.float32)
        partial_value = partial_value + jnp.dot(level_map, own_block, precision=precise)
        return (partial_value, None)

    partial_value, unused = lax.scan(
        accumulate,
        jnp.zeros((total_alpha, beta_count), jnp.float32),
        jnp.arange(alpha_count // block_rows, dtype=jnp.int32),
    )
    own_rows = lax.psum_scatter(partial_value, "alpha", scatter_dimension=0, tiled=True)
    return own_rows + same_beta


def solution(mesh):
    placed = (
        P("alpha", "beta"),
        P(),
        P(),
        P(None, "beta"),
        P(None, "beta"),
        P(None, "beta"),
        P(None, "alpha"),
        P(None, "alpha"),
        P(None, "alpha"),
    )
    return jax.shard_map(
        shards, mesh=mesh, in_specs=placed, out_specs=P("alpha", "beta"), check_vma=False
    )
```

profile of v0, /device:TPU:0, one launch (start us, length us, event | category | flops | bytes accessed | tf_op | source)
XLA Modules:
  0.0 234.7 jit_solution(6492165012831663588)
XLA Ops:
  6.5 0.0 copy-start
  6.5 0.0 reduce-scatter.2.cloned.1.call-start
  6.5 0.9 convert_element_type.37
  7.5 7.2 %all_gather.3 = bf16[128,1024]{1,0:T(8,128)(2,1)S(1)} all-gather(bf16[128,256]{1,0:T(8,128)(2,1)S(1)} %convert_element_type.37), channel_id=1, replica_groups=mesh['alpha'=8,'beta'=4] {'beta'}, dimensions={1}, use_global_device_ids=true | all-gather | bytes 327680 | tf_op jit(solution)/shard_map/all_gather | solution.py:25
  14.7 0.8 multiply_add_fusion
  15.4 0.1 copy.16
  15.5 0.9 copy.15
  16.4 4.0 %select_convert_fusion = bf16[40,256,102]{2,0,1:T(8,128)(2,1)S(1)} fusion(s32[40,256]{0,1:T(8,128)S(1)} %copy.16, s32[40,256]{0,1:T(8,128)S(1)} %copy.15), kind=kLoop, calls=%fused_computation.31 | loop fusion | flops 3133440 | bytes 2170880 | tf_op jit(solution)/shard_map/convert_element_type | solution.py:30
  20.4 65.6 %while.22 = (s32[]{:T(128)}, f32[2,102,128,128]{2,1,3,0:T(8,128)}, s32[2]{0:T(128)S(1)}, bf16[40,256,102]{2,0,1:T(8,128)(2,1)S(1)}, s32[40,256]{1,0:T(8,128)}, /...) while((s32[]{:T(128)}, f32[2,102,128,128]{2,1,3,0:T(8,128)}, ...), condition=%wide.region_1.2_spmd.clone, body=%wide.region_0.1_spmd.clone.sunk | while | flops 1481768960 | bytes 29422248 | solution.py:52
  20.4 0.7 dynamic_slice.58
  21.8 0.7 constant_dynamic-slice_fusion.6
  22.5 5.0 %iota_compare_fusion.12 = pred[1024,40,128]{2,1,0:T(8,128)(4,1)} fusion(s32[40,128]{1,0:T(8,128)S(1)} %constant_dynamic-slice_fusion.6), kind=kLoop, calls=%fused_computation.2.clone.1 | loop fusion | flops 5242880 | bytes 5263360 | tf_op jit(solution)/shard_map/while/body/eval_jaxpr/eq | solution.py:46
  27.5 15.0 %copy.37 = pred[1024,40,128]{0,1,2:T(8,128)(4,1)} copy(pred[1024,40,128]{2,1,0:T(8,128)(4,1)} %iota_compare_fusion.12) | data formatting | bytes 10485760 | tf_op jit(solution)/shard_map/while/body/eval_jaxpr/eq | solution.py:46
  42.5 10.7 %bitcast_dynamic-update-slice_fusion.2 = f32[2,102,128,128]{2,1,3,0:T(8,128)} fusion(f32[2,102,128,128]{2,1,3,0:T(8,128)} %get-tuple-element.275, s32[]{:T(128)} %get-tuple-element.274, pred[1024,40,128]{0,1,2:T(8,128)(4,1)} %copy.37, bf16[40,256,102]{2,0,1:T(8,128)(2,1)S(1)} %get-tuple-element.287, s32[]{:T(128)S(6)} %select_n.24, ...), kind=kOutput, calls=%fused_computation.3.clone.1 | convolution fusion | flops 1476526080 | bytes 13632004 | tf_op jit(solution)/shard_map/while/body/eval_jaxpr/aei,eip->pai/dot_general | solution.py:50
  53.2 0.6 dynamic_slice.58
  54.6 0.7 constant_dynamic-slice_fusion.6
  55.3 5.0 %iota_compare_fusion.12 = pred[1024,40,128]{2,1,0:T(8,128)(4,1)} fusion(s32[40,128]{1,0:T(8,128)S(1)} %constant_dynamic-slice_fusion.6), kind=kLoop, calls=%fused_computation.2.clone.1 | loop fusion | flops 5242880 | bytes 5263360 | tf_op jit(solution)/shard_map/while/body/eval_jaxpr/eq | solution.py:46
  60.3 15.0 %copy.37 = pred[1024,40,128]{0,1,2:T(8,128)(4,1)} copy(pred[1024,40,128]{2,1,0:T(8,128)(4,1)} %iota_compare_fusion.12) | data formatting | bytes 10485760 | tf_op jit(solution)/shard_map/while/body/eval_jaxpr/eq | solution.py:46
  75.3 10.8 %bitcast_dynamic-update-slice_fusion.2 = f32[2,102,128,128]{2,1,3,0:T(8,128)} fusion(f32[2,102,128,128]{2,1,3,0:T(8,128)} %get-tuple-element.275, s32[]{:T(128)} %get-tuple-element.274, pred[1024,40,128]{0,1,2:T(8,128)(4,1)} %copy.37, bf16[40,256,102]{2,0,1:T(8,128)(2,1)S(1)} %get-tuple-element.287, s32[]{:T(128)S(6)} %select_n.24, ...), kind=kOutput, calls=%fused_computation.3.clone.1 | convolution fusion | flops 1476526080 | bytes 13632004 | tf_op jit(solution)/shard_map/while/body/eval_jaxpr/aei,eip->pai/dot_general | solution.py:50
  86.1 12.9 %copy.17 = bf16[102,128,256]{2,0,1:T(8,128)(2,1)} copy(f32[102,128,256]{1,0,2:T(8,128)} %bitcast.63) | data formatting | bytes 20054016 | tf_op jit(solution)/shard_map/reshape | solution.py:53
  98.9 0.0 copy-done
  98.9 4.9 %fusion.27 = bf16[102,128,256]{2,0,1:T(8,128)(2,1)S(1)} fusion(bf16[102,128,256]{2,0,1:T(8,128)(2,1)} %copy.17, bf16[102,102]{1,0:T(8,128)(2,1)S(1)} %copy-done), kind=kOutput, calls=%fused_computation.30 | convolution fusion | flops 685178880 | bytes 13390152 | tf_op jit(solution)/shard_map/qp,pai->qai/dot_general | solution.py:56
  103.8 0.0 copy-start.1
  103.8 0.0 copy-start.3
  103.8 0.0 copy-start.4
  103.8 0.0 copy-start.2
  103.8 4.2 %copy.19 = bf16[102,128,256]{2,1,0:T(8,128)(2,1)} copy(bf16[102,128,256]{2,0,1:T(8,128)(2,1)S(1)} %fusion.27) | data formatting | bytes 13369344
  108.1 0.0 copy-done.1
  108.1 0.0 copy-done.3
  108.1 3.9 %select_convert_fusion.2 = bf16[40,128,102]{2,1,0:T(8,128)(2,1)} fusion(s32[40,128]{1,0:T(8,128)S(1)} %multiply_add_fusion.1, s32[40,128]{1,0:T(8,128)S(1)} %copy-done.3), kind=kLoop, calls=%fused_computation.34 | loop fusion | flops 1566720 | bytes 1085440 | tf_op jit(solution)/shard_map/convert_element_type | solution.py:34
  111.9 4.8 %fusion.30 = f32[1,40,128]{2,0,1:T(1,128)S(1)} fusion(s32[40,128]{1,0:T(8,128)S(1)} %multiply_add_fusion.1, s32[40,128]{1,0:T(8,128)S(1)} %copy-done.3, f32[102]{0:T(128)S(1)} %copy-done.4), kind=kOutput, calls=%fused_computation.35 | convolution fusion | flops 7833600 | bytes 61848 | tf_op jit(solution)/shard_map/eaq,q->ea/dot_general | solution.py:35
  116.7 0.1 copy.23
  116.8 0.0 copy-done.2
  116.8 0.1 copy.18
  117.0 44.5 %while.23 = (s32[]{:T(128)}, f32[1024,256]{1,0:T(8,128)}, s32[4]{0:T(128)S(1)}, s32[40,128]{0,1:T(8,128)S(1)}, bf16[40,128,102]{2,1,0:T(8,128)(2,1)}, /*index=5*...) while((s32[]{:T(128)}, f32[1024,256]{1,0:T(8,128)}, ...), condition=%wide.region_4.5_spmd.clone, body=%wide.region_2.4_spmd.clone.sunk | while | flops 844922880 | bytes 10305741 | solution.py:81
  117.1 0.6 dynamic_slice.64
  118.3 1.6 constant_dynamic-slice_fusion.7
  119.9 1.0 constant_dynamic-slice_fusion.8
  121.0 3.6 %fusion.59 = f32[1024,256]{1,0:T(8,128)S(1)} fusion(s32[32,40]{1,0:T(8,128)S(1)} %dynamic-slice_bitcast_fusion.4, bf16[102,32,256]{2,1,0:T(8,128)(2,1)S(1)} %constant_dynamic-slice_fusion.7, f32[1024,256]{1,0:T(8,128)} %get-tuple-element.307, pred[]{:T(512)S(6)} %compare.3, bf16[40,32,102]{2,1,0:T(8,128)(2,1)S(1)} %constant_dynamic-slice_fusion.8), kind=kOutput, calls=%fused_computation.20.clone.1 | convolution fusion | flops 740098048 | bytes 4034561 | tf_op jit(solution)/shard_map/while/body/eval_jaxpr/bae,aei->bi/dot_general | solution.py:72
  124.6 1.1 fusion.60
  125.7 1.6 convolution_add_fusion.2
  127.3 0.6 dynamic_slice.64
  128.5 1.6 constant_dynamic-slice_fusion.7
  130.1 1.0 constant_dynamic-slice_fusion.8
  131.1 4.8 %fusion.59 = f32[1024,256]{1,0:T(8,128)S(1)} fusion(s32[32,40]{1,0:T(8,128)S(1)} %dynamic-slice_bitcast_fusion.4, bf16[102,32,256]{2,1,0:T(8,128)(2,1)S(1)} %constant_dynamic-slice_fusion.7, f32[1024,256]{1,0:T(8,128)} %get-tuple-element.307, pred[]{:T(512)S(6)} %compare.3, bf16[40,32,102]{2,1,0:T(8,128)(2,1)S(1)} %constant_dynamic-slice_fusion.8), kind=kOutput, calls=%fused_computation.20.clone.1 | convolution fusion | flops 740098048 | bytes 4034561 | tf_op jit(solution)/shard_map/while/body/eval_jaxpr/bae,aei->bi/dot_general | solution.py:72
  136.0 1.1 fusion.60
  137.1 1.6 convolution_add_fusion.2
  138.7 0.6 dynamic_slice.64
  139.9 1.6 constant_dynamic-slice_fusion.7
  141.5 1.0 constant_dynamic-slice_fusion.8
  142.5 4.8 %fusion.59 = f32[1024,256]{1,0:T(8,128)S(1)} fusion(s32[32,40]{1,0:T(8,128)S(1)} %dynamic-slice_bitcast_fusion.4, bf16[102,32,256]{2,1,0:T(8,128)(2,1)S(1)} %constant_dynamic-slice_fusion.7, f32[1024,256]{1,0:T(8,128)} %get-tuple-element.307, pred[]{:T(512)S(6)} %compare.3, bf16[40,32,102]{2,1,0:T(8,128)(2,1)S(1)} %constant_dynamic-slice_fusion.8), kind=kOutput, calls=%fused_computation.20.clone.1 | convolution fusion | flops 740098048 | bytes 4034561 | tf_op jit(solution)/shard_map/while/body/eval_jaxpr/bae,aei->bi/dot_general | solution.py:72
  147.3 1.1 fusion.60
  148.4 1.6 convolution_add_fusion.2
  150.1 0.6 dynamic_slice.64
  151.3 1.6 constant_dynamic-slice_fusion.7
  152.9 1.0 constant_dynamic-slice_fusion.8
  153.9 4.8 %fusion.59 = f32[1024,256]{1,0:T(8,128)S(1)} fusion(s32[32,40]{1,0:T(8,128)S(1)} %dynamic-slice_bitcast_fusion.4, bf16[102,32,256]{2,1,0:T(8,128)(2,1)S(1)} %constant_dynamic-slice_fusion.7, f32[1024,256]{1,0:T(8,128)} %get-tuple-element.307, pred[]{:T(512)S(6)} %compare.3, bf16[40,32,102]{2,1,0:T(8,128)(2,1)S(1)} %constant_dynamic-slice_fusion.8), kind=kOutput, calls=%fused_computation.20.clone.1 | convolution fusion | flops 740098048 | bytes 4034561 | tf_op jit(solution)/shard_map/while/body/eval_jaxpr/bae,aei->bi/dot_general | solution.py:72
  158.7 1.1 fusion.60
  159.8 1.6 convolution_add_fusion.2
  161.4 0.0 reduce-scatter.2.cloned.1.call-update
  161.5 10.7 %fusion.35 = f32[1,128,256]{1,0,2:T(1,128)S(1)} fusion(f32[102,128,256]{1,0,2:T(8,128)} %bitcast.64, f32[102]{0:T(128)S(1)} %copy-done.4), kind=kOutput, calls=%fused_computation.44 | convolution fusion | flops 40108032 | bytes 13500824 | tf_op jit(solution)/shard_map/p,pai->ai/dot_general | solution.py:54
  172.2 0.1 copy.24
  172.3 54.0 %reduce-scatter.2.cloned.1.call-done = f32[128,256]{1,0:T(8,128)} async-done(((f32[1024,256]{1,0:T(8,128)}), f32[128,256]{1,0:T(8,128)}) %reduce-scatter.2.cloned.1.call-update) | async-done | bytes 131088 | tf_op jit(solution)/shard_map/reduce_scatter | solution.py:86
  226.3 1.6 bitcast_add_fusion
  (14 shorter events, 0.1 us)
Async XLA Ops:
  6.5 92.4 %copy-start = (bf16[102,102]{1,0:T(8,128)(2,1)S(1)}, bf16[102,102]{1,0:T(8,128)(2,1)}, u32[]{:S(2)}) copy-start(bf16[102,102]{1,0:T(8,128)(2,1)} %param.15) | copy-start | bytes 62428
  6.5 219.7 %reduce-scatter.2.cloned.1.call-start = ((), (), s32[]{:S(2)}) async-start(), calls=%async_computation.1 | async-start | bytes 1179648 | tf_op jit(solution)/shard_map/reduce_scatter | solution.py:86
  103.8 4.3 %copy-start.1 = (s32[40,128]{1,0:T(8,128)S(1)}, s32[40,128]{1,0:T(8,128)}, u32[]{:S(2)}) copy-start(s32[40,128]{1,0:T(8,128)} %param.21) | copy-start | bytes 61444
  103.8 4.3 %copy-start.3 = (s32[40,128]{1,0:T(8,128)S(1)}, s32[40,128]{1,0:T(8,128)}, u32[]{:S(2)}) copy-start(s32[40,128]{1,0:T(8,128)} %param.20) | copy-start | bytes 61444
  103.8 8.1 %copy-start.4 = (f32[102]{0:T(128)S(1)}, f32[102]{0:T(128)}, u32[]{:S(2)}) copy-start(f32[102]{0:T(128)} %param.14) | copy-start | bytes 1228
  103.8 13.0 %copy-start.2 = (s32[40,128]{1,0:T(8,128)S(1)}, s32[40,128]{1,0:T(8,128)}, u32[]{:S(2)}) copy-start(s32[40,128]{1,0:T(8,128)} %param.19) | copy-start | bytes 61444
Sparse Core Ops, SparseCore 0:
  161.6 64.6 reduce-scatter.1
where the time goes:
time: 236 us; the launch traced here: 235 us
  matrix products  66.4 us (28%)
  local copies, waits for them, and re-layouts  64 us (27%)
  waiting for transfers between devices  54 us (23%)
  other arithmetic  25.5 us (11%)
  between operations  13.5 us (6%)
  blocking collectives  7.19 us (3%)
  loops' own time  4.09 us (2%)
    reduce_scatter x1, waiting for transfers between devices, shards(): lax.psum_scatter(partial_value, 'alpha', scatter_dimension=0, tiled=True)  54 us
    eq x2, local copies, waits for them, and re-layouts, beta_block(): targets[None, :, :] == string_ids[:, None, None]  29.9 us
    dot_general x2, matrix products, beta_block(): jnp.einsum('aei,eip->pai', picked, hot_cols, preferred_element_type=jnp.f...  21.5 us
    dot_general x4, matrix products, accumulate(): jnp.einsum('bae,aei->bi', spread, lifted_bf, preferred_element_type=jnp.f...  18.1 us
    reshape x1, local copies, waits for them, and re-layouts, shards(): jnp.transpose(blocks, (1, 2, 0, 3))  12.9 us
    dot_general x1, matrix products, shards(): same_beta = jnp.einsum('p,pai->ai', one_body, density, precision=precise)  10.7 us
    eq x2, other arithmetic, beta_block(): targets[None, :, :] == string_ids[:, None, None]  10 us
    all_gather x1, blocking collectives, shards(): rows_whole = lax.all_gather(civec_bf, 'beta', axis=1, tiled=True)  7.19 us
  transfers between devices with their start and end apart: 1, of which 1 were waited for; matrix products, arithmetic and copies ran while one was open for 5% of the time, Pallas kernels for 0%

commit v1 on v0

v1 whole, which is shorter than its diff:
```python
import functools

import jax
import jax.numpy as jnp
from jax import lax
from jax.experimental import pallas as pl
from jax.experimental.pallas import tpu as pltpu
from jax.sharding import PartitionSpec as P

LANES = 128
GROUP = 3
NT = (((1,), (1,)), ((), ()))


def high_low(values):
    high = lax.reduce_precision(values, 8, 7)
    return high, values - high


def local_kernel(
    sizes, me_ref, c_ref, beta_ref, alpha_ref, vt_ref, h_ref, own_ref, *rest
):
    chunks, rows, cols, nexc, blocks = sizes
    out_refs = rest[: blocks - 1]
    density, lifted, weights, same = rest[blocks - 1 :]
    per_tile = LANES // GROUP
    bf16, f32 = jnp.bfloat16, jnp.float32

    def weight_step(t, carry):
        code = alpha_ref[t]
        pair = (code >> 1) & 127
        sign = (2 * (code & 1) - 1).astype(f32)
        q_ids = lax.broadcasted_iota(jnp.int32, (LANES, LANES), 0)
        hot = jnp.where(q_ids == pair, sign, 0.0).astype(bf16)
        u_t = jnp.dot(vt_ref[...], hot, preferred_element_type=f32)
        weights[pl.ds(pl.multiple_of(t * LANES, LANES), LANES), :] = u_t.T
        return carry

    lax.fori_loop(0, rows * nexc // LANES, weight_step, 0)

    groups = beta_ref.shape[0]

    def beta_step(g, carry):
        code = beta_ref[g]
        target = code >> 8
        low = lax.rem(target, cols)
        high = lax.div(target, cols)
        j_ids = lax.broadcasted_iota(jnp.int32, (cols, 2 * LANES), 0)
        hot = jnp.where(j_ids == low, 1.0, 0.0).astype(bf16)
        picked = jnp.dot(c_ref[0], hot, preferred_element_type=f32)
        for k in range(1, chunks):
            picked = jnp.where(
                high == k, jnp.dot(c_ref[k], hot, preferred_element_type=f32), picked
            )
        picked = picked.astype(bf16)
        pair = (code >> 1) & 127
        sign = (2 * (code & 1) - 1).astype(f32)
        lane = lax.broadcasted_iota(jnp.int32, (1, 2 * LANES), 1)
        member = lax.div(lane & (LANES - 1), per_tile)
        slot = pair + LANES * member
        for half in range(2):
            span = slice(half * LANES, (half + 1) * LANES)
            p_ids = lax.broadcasted_iota(jnp.int32, (GROUP * LANES, LANES), 0)
            h_t = jnp.where(p_ids == slot[:, span], sign[:, span], 0.0).astype(bf16)
            d = lax.dot_general(picked[:, span], h_t, NT, preferred_element_type=f32)
            for m in range(GROUP):
                i = (2 * g + half) * GROUP + m
                density[pl.ds(pl.multiple_of(i * rows, rows), rows), :] = d[
                    :, m * LANES : (m + 1) * LANES
                ]
        return carry

    lax.fori_loop(0, groups, beta_step, 0)

    def alpha_step(t, carry):
        parts = []
        for m in range(2):
            a = 2 * t + m
            d = density[pl.ds(a, cols, stride=rows), :].astype(bf16)
            u = weights[pl.ds(pl.multiple_of(a * nexc, 8), nexc), :]
            u = jnp.concatenate([u, h_ref[...]], axis=0).astype(bf16)
            l = lax.dot_general(u, d, NT, preferred_element_type=f32)
            same[pl.ds(a, 1), :] = l[nexc : nexc + 1] + l[nexc + 1 : nexc + 2]
            parts.append(l[:nexc])
        lifted[pl.ds(pl.multiple_of(t * 2 * nexc, 2 * nexc), 2 * nexc), :] = (
            jnp.concatenate(parts, axis=0).astype(bf16)
        )
        return carry

    lax.fori_loop(0, rows // 2, alpha_step, 0)

    me = me_ref[0]
    for s in range(blocks):
        base = (me ^ s) * rows
        total = jnp.zeros((rows, cols), f32)
        for t in range(rows * nexc // LANES // 8):
            hots = []
            for w in range(8):
                target = (alpha_ref[8 * t + w] >> 8) - base
                b_ids = lax.broadcasted_iota(jnp.int32, (rows, LANES), 0)
                hots.append(jnp.where(b_ids == target, 1.0, 0.0).astype(bf16))
            total += jnp.dot(
                jnp.concatenate(hots, axis=1),
                lifted[8 * t * LANES : 8 * (t + 1) * LANES, :],
                preferred_element_type=f32,
            )
        if s == 0:
            own_ref[...] = total + same[...]
        else:
            out_refs[s - 1][...] = total.astype(bf16)


def shards(
    ci_vector,
    one_body,
    pair_integrals,
    beta_target,
    beta_pair,
    beta_sign,
    alpha_target,
    alpha_pair,
    alpha_sign,
):
    rows, cols = ci_vector.shape
    pairs = one_body.shape[0]
    nexc = beta_target.shape[0]
    blocks = lax.axis_size("alpha")
    chunks = lax.axis_size("beta")
    per_tile = LANES // GROUP
    me = lax.axis_index("alpha")
    bf16 = jnp.bfloat16

    civec_bf = ci_vector.astype(bf16)
    gathered = lax.all_gather(civec_bf, "beta", axis=0)

    beta_code = beta_target * 256 + beta_pair * 2 + beta_sign
    own = (lax.axis_index("beta") * cols + jnp.arange(cols, dtype=jnp.int32)) * 256 + 1
    extra = jnp.stack([own + 2 * (pairs + 2), own + 2 * (pairs + 3)])
    beta_code = jnp.concatenate([beta_code, extra]).T
    tiles = -(-cols // (2 * GROUP)) * 2
    beta_code = jnp.pad(beta_code, ((0, tiles * GROUP - cols), (0, 0)))
    beta_code = beta_code.reshape(tiles, GROUP * (nexc + 2))
    beta_code = jnp.pad(beta_code, ((0, 0), (0, LANES - GROUP * (nexc + 2))))
    beta_code = beta_code.reshape(tiles // 2, 1, 2 * LANES)
    alpha_code = (alpha_target * 256 + alpha_pair * 2 + alpha_sign).T
    alpha_code = alpha_code.reshape(rows * nexc // LANES, 1, LANES)

    h_high, h_low = high_low(one_body)
    vt = jnp.zeros((LANES, LANES), bf16)
    vt = vt.at[:pairs, :pairs].set(pair_integrals.T)
    vt = vt.at[pairs + 2, :pairs].set(h_high.astype(bf16))
    vt = vt.at[pairs + 3, :pairs].set(h_low.astype(bf16))
    h_rows = jnp.pad(jnp.stack([h_high, h_low]), ((0, 6), (0, LANES - pairs)))

    sizes = (chunks, rows, cols, nexc, blocks)
    vmem = pl.BlockSpec(memory_space=pltpu.VMEM)
    outs = pl.pallas_call(
        functools.partial(local_kernel, sizes),
        out_shape=[jax.ShapeDtypeStruct((rows, cols), jnp.float32)]
        + [jax.ShapeDtypeStruct((rows, cols), bf16)] * (blocks - 1),
        in_specs=[pl.BlockSpec(memory_space=pltpu.SMEM)] + [vmem] * 5,
        out_specs=[vmem] * blocks,
        scratch_shapes=[
            pltpu.VMEM((tiles * GROUP * rows, LANES), jnp.float32),
            pltpu.VMEM((rows * nexc, cols), bf16),
            pltpu.VMEM((rows * nexc, LANES), jnp.float32),
            pltpu.VMEM((rows, cols), jnp.float32),
        ],
        compiler_params=pltpu.CompilerParams(vmem_limit_bytes=56 * 1024 * 1024),
        name="sigma_local",
    )(me.reshape(1), gathered, beta_code, alpha_code, vt, h_rows)
    total = outs[0]
    for s in range(1, blocks):
        got = lax.ppermute(outs[s], "alpha", [(d, d ^ s) for d in range(blocks)])
        total = total + got.astype(jnp.float32)
    return total


def solution(mesh):
    placed = (
        P("alpha", "beta"),
        P(),
        P(),
        P(None, "beta"),
        P(None, "beta"),
        P(None, "beta"),
        P(None, "alpha"),
        P(None, "alpha"),
        P(None, "alpha"),
    )
    return jax.shard_map(
        shards, mesh=mesh, in_specs=placed, out_specs=P("alpha", "beta"), check_vma=False
    )
```

time: 236 us -> 82.6 us (0.35)
  matrix products: 66.4 us -> 0 us
  local copies, waits for them, and re-layouts: 64 us -> 5.02 us
  Pallas kernels: 0 us -> 48.9 us
  waiting for transfers between devices: 54 us -> 7.16 us
  other arithmetic: 25.5 us -> 2.28 us
  between operations: 13.5 us -> 0.12 us
  starting transfers between devices: 0.01 us -> 11.1 us
  loops' own time: 4.09 us -> 0 us
    dot_general x13 -> x0, matrix products: 66.4 us -> none  [the longest x2 21.5 us: beta_block(): jnp.einsum('aei,eip->pai', picked, hot_cols, preferred_element_type=jnp.f...]
    reduce_scatter x1 -> x0, waiting for transfers between devices: 54 us -> none  [shards(): lax.psum_scatter(partial_value, 'alpha', scatter_dimension=0, tiled=True)]
    pallas_call x0 -> x1, Pallas kernels: none -> 48.9 us  [shards(): pl.pallas_call(functools.partial(local_kernel, sizes), out_shape=[jax.Sha...]
    eq x2 -> x0, local copies, waits for them, and re-layouts: 29.9 us -> none  [beta_block(): targets[None, :, :] == string_ids[:, None, None]]
    dynamic_slice x16 -> x0, local copies, waits for them, and re-layouts: 15.6 us -> none  [the longest x4 6.38 us: accumulate(): mixed_rows = lax.dynamic_slice_in_dim(mixed, offset, block_rows, 1)]
    reshape x1 -> x3, local copies, waits for them, and re-layouts: 12.9 us -> 1.44 us  [the longest x1 0.71 us: shards(): alpha_code = alpha_code.reshape(rows * nexc // LANES, 1, LANES)]
    ppermute x0 -> x7, starting transfers between devices: none -> 11.1 us  [shards(): got = lax.ppermute(outs[s], 'alpha', [(d, d ^ s) for d in range(blocks)])]
    eq x2 -> x0, other arithmetic: 10 us -> none  [beta_block(): targets[None, :, :] == string_ids[:, None, None]]
  transfers between devices with their start and end apart: 1 -> 7, of which waited for: 1 -> 2; matrix products, arithmetic and copies ran while one was open for 5% -> 0% of each run, Pallas kernels for 0% -> 0%
where the time goes in v1:
time: 82.6 us; the launch traced here: 82.3 us
  Pallas kernels  48.9 us (59%)
  starting transfers between devices  11.1 us (13%)
  blocking collectives  7.63 us (9%)
  waiting for transfers between devices  7.16 us (9%)
  local copies, waits for them, and re-layouts  5.02 us (6%)
  other arithmetic  2.28 us (3%)
    pallas_call x1, Pallas kernels, shards(): pl.pallas_call(functools.partial(local_kernel, sizes), out_shape=[jax.Sha...  48.9 us
    ppermute x7, starting transfers between devices, shards(): got = lax.ppermute(outs[s], 'alpha', [(d, d ^ s) for d in range(blocks)])  11.1 us
    all_gather x1, blocking collectives, shards(): gathered = lax.all_gather(civec_bf, 'beta', axis=0)  7.63 us
    ppermute x7, waiting for transfers between devices, shards(): got = lax.ppermute(outs[s], 'alpha', [(d, d ^ s) for d in range(blocks)])  7.16 us
    unnamed x20, local copies, waits for them, and re-layouts  3.13 us
  transfers between devices with their start and end apart: 7, of which 2 were waited for; matrix products, arithmetic and copies ran while one was open for 0% of the time, Pallas kernels for 0%

profile of v1, /device:TPU:0, one launch (start us, length us, event | category | flops | bytes accessed | tf_op | source)
XLA Modules:
  0.0 82.3 jit_solution(10751532305040415573)
XLA Ops:
  0.0 0.0 copy-start.8
  0.0 0.0 copy-start.7
  0.0 0.6 copy-done.8
  0.7 0.0 copy-start.5
  0.7 0.0 copy-start.6
  0.7 0.9 %copy.14 = bf16[102,102]{0,1:T(8,128)(2,1)S(1)} copy(bf16[102,102]{1,0:T(8,128)(2,1)} %param.17) | data formatting | bytes 41616 | tf_op args[2]
  1.5 0.0 copy-done.7
  1.6 0.0 copy-done.5
  1.6 0.0 copy-done.6
  1.6 0.0 copy-start.1
  1.6 0.1 copy.13
  1.7 0.7 reshape.121
  2.4 0.1 copy-done.1
  2.5 0.0 copy-start.2
  2.5 0.0 copy-start.3
  2.5 0.0 copy-start.4
  2.5 0.8 copy-done.2
  3.3 0.0 copy-done.3
  3.3 0.0 copy-done.4
  3.3 0.1 copy.16
  3.5 0.1 reshape.119
  3.6 0.6 reshape.120.beta_ref
  4.2 7.6 %all-gather = bf16[512,256]{1,0:T(8,128)(2,1)} all-gather(bf16[128,256]{1,0:T(8,128)(2,1)S(1)} %convert_element_type.32), channel_id=2, replica_groups=mesh['alpha'=8,'beta'=4] {'beta'}, dimensions={0}, use_global_device_ids=true | all-gather | bytes 327680 | tf_op jit(solution)/shard_map/all_gather | solution.py:134
  11.8 0.6 select_maximum_fusion.h_ref
  12.5 0.2 scatter.11
  12.6 0.2 scatter.14.vt_ref
  12.8 0.0 copy-start
  12.8 0.6 copy-done
  13.4 48.9 %sigma_local.1 = (f32[128,256]{1,0:T(8,128)}, bf16[128,256]{1,0:T(8,128)(2,1)}, bf16[128,256]{1,0:T(8,128)(2,1)}, bf16[128,256]{1,0:T(8,128)(2,1)}, bf16[128,256...) custom-call(s32[1]{0:T(128)} %bitcast.me_ref, ...), custom_call_target="tpu_custom_call" | custom-call | tf_op jit(solution)/shard_map/sigma_local/pallas_call | solution.py:157
  62.3 1.6 %collective-permute-start = (bf16[128,256]{1,0:T(8,128)(2,1)}, bf16[128,256]{1,0:T(8,128)(2,1)S(1)}, u32[]{:S(2)}, u32[]{:S(2)}) collective-permute-start(bf16[128,256]{1,0:T(8,128)(2,1)} %get-tuple-element.50), channel_id=1, source_target_pairs={{0,4},{4,0},{8,12},{12,8},{16,20},{20,16},{24,28},{28,24},{1,5},{5... | collective-permute-start | bytes 196616 | tf_op jit(solution)/shard_map/ppermute | solution.py:174
  63.9 1.6 %collective-permute-start.1 = (bf16[128,256]{1,0:T(8,128)(2,1)}, bf16[128,256]{1,0:T(8,128)(2,1)S(1)}, u32[]{:S(2)}, u32[]{:S(2)}) collective-permute-start(bf16[128,256]{1,0:T(8,128)(2,1)} %get-tuple-element.51), channel_id=1, source_target_pairs={{0,8},{4,12},{8,0},{12,4},{16,24},{20,28},{24,16},{28,20},{1,9},{5... | collective-permute-start | bytes 196616 | tf_op jit(solution)/shard_map/ppermute | solution.py:174
  65.5 0.3 collective-permute-start.2
  65.8 2.6 %collective-permute-start.3 = (bf16[128,256]{1,0:T(8,128)(2,1)}, bf16[128,256]{1,0:T(8,128)(2,1)S(1)}, u32[]{:S(2)}, u32[]{:S(2)}) collective-permute-start(bf16[128,256]{1,0:T(8,128)(2,1)} %get-tuple-element.53), channel_id=1, source_target_pairs={{0,16},{4,20},{8,24},{12,28},{16,0},{20,4},{24,8},{28,12},{1,17},{... | collective-permute-start | bytes 196616 | tf_op jit(solution)/shard_map/ppermute | solution.py:174
  68.5 1.3 %collective-permute-start.4 = (bf16[128,256]{1,0:T(8,128)(2,1)}, bf16[128,256]{1,0:T(8,128)(2,1)S(1)}, u32[]{:S(2)}, u32[]{:S(2)}) collective-permute-start(bf16[128,256]{1,0:T(8,128)(2,1)} %get-tuple-element.54), channel_id=1, source_target_pairs={{0,20},{4,16},{8,28},{12,24},{16,4},{20,0},{24,12},{28,8},{1,21},{... | collective-permute-start | bytes 196616 | tf_op jit(solution)/shard_map/ppermute | solution.py:174
  69.8 0.0 collective-permute-done
  69.8 3.6 %collective-permute-start.5 = (bf16[128,256]{1,0:T(8,128)(2,1)}, bf16[128,256]{1,0:T(8,128)(2,1)S(1)}, u32[]{:S(2)}, u32[]{:S(2)}) collective-permute-start(bf16[128,256]{1,0:T(8,128)(2,1)} %get-tuple-element.55), channel_id=1, source_target_pairs={{0,24},{4,28},{8,16},{12,20},{16,8},{20,12},{24,0},{28,4},{1,25},{... | collective-permute-start | bytes 196616 | tf_op jit(solution)/shard_map/ppermute | solution.py:174
  73.4 0.0 collective-permute-done.1
  73.4 0.1 collective-permute-start.6
  73.5 0.0 collective-permute-done.2
  73.5 0.0 collective-permute-done.3
  73.5 5.4 %collective-permute-done.4 = bf16[128,256]{1,0:T(8,128)(2,1)S(1)} collective-permute-done((bf16[128,256]{1,0:T(8,128)(2,1)}, bf16[128,256]{1,0:T(8,128)(2,1)S(1)}, u32[]{:S(2)}, u32[]{:S(2)}) %collective-permute-start.4) | collective-permute-done | bytes 65568 | tf_op jit(solution)/shard_map/ppermute | solution.py:174
  78.9 0.0 collective-permute-done.5
  78.9 1.7 %collective-permute-done.6 = bf16[128,256]{1,0:T(8,128)(2,1)S(1)} collective-permute-done((bf16[128,256]{1,0:T(8,128)(2,1)}, bf16[128,256]{1,0:T(8,128)(2,1)S(1)}, u32[]{:S(2)}, u32[]{:S(2)}) %collective-permute-start.6) | collective-permute-done | bytes 65568 | tf_op jit(solution)/shard_map/ppermute | solution.py:174
  80.6 1.6 %convert_add_fusion = f32[128,256]{1,0:T(8,128)} fusion(bf16[128,256]{1,0:T(8,128)(2,1)S(1)} %collective-permute-done.6, bf16[128,256]{1,0:T(8,128)(2,1)S(1)} %collective-permute-done.5, bf16[128,256]{1,0:T(8,128)(2,1)S(1)} %collective-permute-done.4, bf16[128,256]{1,0:T(8,128)(2,1)S(1)} %collective-permute-done.3, ...), kind=kLoop, calls=%fused_computation | loop fusion | flops 458752 | bytes 720896 | tf_op jit(solution)/shard_map/add | solution.py:175
  (9 shorter events, 0.1 us)
Async XLA Ops:
  0.0 0.7 copy-start.8
  0.0 1.5 %copy-start.7 = (s32[40,128]{1,0:T(8,128)S(1)}, s32[40,128]{1,0:T(8,128)}, u32[]{:S(2)}) copy-start(s32[40,128]{1,0:T(8,128)} %param.21) | copy-start | bytes 61444
  0.7 0.9 %copy-start.5 = (s32[40,128]{1,0:T(8,128)S(1)}, s32[40,128]{1,0:T(8,128)}, u32[]{:S(2)}) copy-start(s32[40,128]{1,0:T(8,128)} %param.23) | copy-start | bytes 61444
  0.7 0.9 %copy-start.6 = (s32[40,128]{1,0:T(8,128)S(1)}, s32[40,128]{1,0:T(8,128)}, u32[]{:S(2)}) copy-start(s32[40,128]{1,0:T(8,128)} %param.22) | copy-start | bytes 61444
  1.6 0.9 %copy-start.1 = (f32[128,256]{1,0:T(8,128)S(1)}, f32[128,256]{1,0:T(8,128)}, u32[]{:S(2)}) copy-start(f32[128,256]{1,0:T(8,128)} %param.15) | copy-start | bytes 393220
  2.5 0.8 copy-start.2
  2.5 0.8 copy-start.3
  2.5 0.8 copy-start.4
  12.8 0.6 copy-start
  62.3 7.4 %collective-permute-start = (bf16[128,256]{1,0:T(8,128)(2,1)}, bf16[128,256]{1,0:T(8,128)(2,1)S(1)}, u32[]{:S(2)}, u32[]{:S(2)}) collective-permute-start(bf16[128,256]{1,0:T(8,128)(2,1)} %get-tuple-element.50), channel_id=1, source_target_pairs={{0,4},{4,0},{8,12},{12,8},{16,20},{20,16},{24,28},{28,24},{1,5},{5... | collective-permute-start | bytes 196616 | tf_op jit(solution)/shard_map/ppermute | solution.py:174
  63.9 9.5 %collective-permute-start.1 = (bf16[128,256]{1,0:T(8,128)(2,1)}, bf16[128,256]{1,0:T(8,128)(2,1)S(1)}, u32[]{:S(2)}, u32[]{:S(2)}) collective-permute-start(bf16[128,256]{1,0:T(8,128)(2,1)} %get-tuple-element.51), channel_id=1, source_target_pairs={{0,8},{4,12},{8,0},{12,4},{16,24},{20,28},{24,16},{28,20},{1,9},{5... | collective-permute-start | bytes 196616 | tf_op jit(solution)/shard_map/ppermute | solution.py:174
  65.5 8.0 %collective-permute-start.2 = (bf16[128,256]{1,0:T(8,128)(2,1)}, bf16[128,256]{1,0:T(8,128)(2,1)S(1)}, u32[]{:S(2)}, u32[]{:S(2)}) collective-permute-start(bf16[128,256]{1,0:T(8,128)(2,1)} %get-tuple-element.52), channel_id=1, source_target_pairs={{0,12},{4,8},{8,4},{12,0},{16,28},{20,24},{24,20},{28,16},{1,13},{... | collective-permute-start | bytes 196616 | tf_op jit(solution)/shard_map/ppermute | solution.py:174
  65.8 7.7 %collective-permute-start.3 = (bf16[128,256]{1,0:T(8,128)(2,1)}, bf16[128,256]{1,0:T(8,128)(2,1)S(1)}, u32[]{:S(2)}, u32[]{:S(2)}) collective-permute-start(bf16[128,256]{1,0:T(8,128)(2,1)} %get-tuple-element.53), channel_id=1, source_target_pairs={{0,16},{4,20},{8,24},{12,28},{16,0},{20,4},{24,8},{28,12},{1,17},{... | collective-permute-start | bytes 196616 | tf_op jit(solution)/shard_map/ppermute | solution.py:174
  68.5 10.5 %collective-permute-start.4 = (bf16[128,256]{1,0:T(8,128)(2,1)}, bf16[128,256]{1,0:T(8,128)(2,1)S(1)}, u32[]{:S(2)}, u32[]{:S(2)}) collective-permute-start(bf16[128,256]{1,0:T(8,128)(2,1)} %get-tuple-element.54), channel_id=1, source_target_pairs={{0,20},{4,16},{8,28},{12,24},{16,4},{20,0},{24,12},{28,8},{1,21},{... | collective-permute-start | bytes 196616 | tf_op jit(solution)/shard_map/ppermute | solution.py:174
  69.8 9.2 %collective-permute-start.5 = (bf16[128,256]{1,0:T(8,128)(2,1)}, bf16[128,256]{1,0:T(8,128)(2,1)S(1)}, u32[]{:S(2)}, u32[]{:S(2)}) collective-permute-start(bf16[128,256]{1,0:T(8,128)(2,1)} %get-tuple-element.55), channel_id=1, source_target_pairs={{0,24},{4,28},{8,16},{12,20},{16,8},{20,12},{24,0},{28,4},{1,25},{... | collective-permute-start | bytes 196616 | tf_op jit(solution)/shard_map/ppermute | solution.py:174
  73.4 7.3 %collective-permute-start.6 = (bf16[128,256]{1,0:T(8,128)(2,1)}, bf16[128,256]{1,0:T(8,128)(2,1)S(1)}, u32[]{:S(2)}, u32[]{:S(2)}) collective-permute-start(bf16[128,256]{1,0:T(8,128)(2,1)} %get-tuple-element.56), channel_id=1, source_target_pairs={{0,28},{4,24},{8,20},{12,16},{16,12},{20,8},{24,4},{28,0},{1,29},{... | collective-permute-start | bytes 196616 | tf_op jit(solution)/shard_map/ppermute | solution.py:174

commit v2 on v1

v2 whole, which is shorter than its diff:
```python
import functools

import jax
import jax.numpy as jnp
from jax import lax
from jax.experimental import pallas as pl
from jax.experimental.pallas import tpu as pltpu
from jax.sharding import PartitionSpec as P

LANES = 128
UNROLL = 11
GROUP = 3
NT = (((1,), (1,)), ((), ()))


def high_low(values):
    high = lax.reduce_precision(values, 8, 7)
    return high, values - high


def weight_kernel(tiles, alpha_ref, vt_ref, weights_ref):
    for t in range(tiles):
        code = alpha_ref[t]
        pair = (code >> 1) & 127
        sign = (2 * (code & 1) - 1).astype(jnp.float32)
        q_ids = lax.broadcasted_iota(jnp.int32, (LANES, LANES), 0)
        hot = jnp.where(q_ids == pair, sign, 0.0).astype(jnp.bfloat16)
        u_t = jnp.dot(vt_ref[...], hot, preferred_element_type=jnp.float32)
        weights_ref[t * LANES : (t + 1) * LANES, :] = u_t.T.astype(jnp.bfloat16)


def local_kernel(sizes, place_ref, beta_ref, alpha_ref, weights, *rest):
    chunks, rows, cols, nexc, depth, blocks, stride = sizes
    c_refs, rest = rest[:chunks], rest[chunks:]
    own_ref, out_refs, rest = rest[0], rest[1:blocks], rest[blocks:]
    density, lifted, same, picked = rest
    per_tile = LANES // GROUP
    bf16, f32 = jnp.bfloat16, jnp.float32
    groups = beta_ref.shape[0]
    my_alpha, my_beta = place_ref[0], place_ref[1]

    def gather_step(g, carry):
        target = beta_ref[g] >> 8
        low = lax.rem(target, cols)
        high = lax.div(target, cols) ^ my_beta
        j_ids = lax.broadcasted_iota(jnp.int32, (cols, 2 * LANES), 0)
        hot = jnp.where(j_ids == low, 1.0, 0.0).astype(bf16)
        found = jnp.dot(c_refs[0][...], hot, preferred_element_type=f32)
        for k in range(1, chunks):
            found = jnp.where(
                high == k, jnp.dot(c_refs[k][...], hot, preferred_element_type=f32), found
            )
        picked[g] = found.astype(bf16)
        return carry

    lax.fori_loop(0, groups, gather_step, 0, unroll=UNROLL)

    def density_step(g, carry):
        code = beta_ref[g]
        pair = (code >> 1) & 127
        sign = (2 * (code & 1) - 1).astype(f32)
        lane = lax.broadcasted_iota(jnp.int32, (1, 2 * LANES), 1)
        slot = pair + LANES * lax.div(lane & (LANES - 1), per_tile)
        for half in range(2):
            span = slice(half * LANES, (half + 1) * LANES)
            p_ids = lax.broadcasted_iota(jnp.int32, (GROUP * LANES, LANES), 0)
            h_t = jnp.where(p_ids == slot[:, span], sign[:, span], 0.0).astype(bf16)
            d = lax.dot_general(picked[g, :, span], h_t, NT, preferred_element_type=f32)
            for m in range(GROUP):
                i = (2 * g + half) * GROUP + m
                density[pl.ds(pl.multiple_of(i * stride, 8), rows), :] = d[
                    :, m * LANES : (m + 1) * LANES
                ]
        return carry

    lax.fori_loop(0, groups, density_step, 0, unroll=UNROLL)

    def alpha_step(t, carry):
        parts = []
        for m in range(2):
            a = 2 * t + m
            d = density[pl.ds(a, cols, stride=stride), :].astype(bf16)
            u = weights[pl.ds(pl.multiple_of(a * depth, 16), depth), :]
            l = lax.dot_general(u, d, NT, preferred_element_type=f32)
            same[pl.ds(a, 1), :] = l[nexc : nexc + 1] + l[nexc + 1 : nexc + 2]
            parts.append(l[:nexc])
        lifted[pl.ds(pl.multiple_of(t * 2 * nexc, 2 * nexc), 2 * nexc), :] = (
            jnp.concatenate(parts, axis=0).astype(bf16)
        )
        return carry

    lax.fori_loop(0, rows // 2, alpha_step, 0, unroll=8)

    for s in range(blocks):
        base = (my_alpha ^ s) * rows
        total = jnp.zeros((rows, cols), f32)
        for t in range(rows * nexc // LANES // 8):
            hots = []
            for w in range(8):
                target = (alpha_ref[8 * t + w] >> 8) - base
                b_ids = lax.broadcasted_iota(jnp.int32, (rows, LANES), 0)
                hots.append(jnp.where(b_ids == target, 1.0, 0.0).astype(bf16))
            total += jnp.dot(
                jnp.concatenate(hots, axis=1),
                lifted[8 * t * LANES : 8 * (t + 1) * LANES, :],
                preferred_element_type=f32,
            )
        if s == 0:
            own_ref[...] = total + same[...]
        else:
            out_refs[s - 1][...] = total.astype(bf16)


def shards(
    ci_vector,
    one_body,
    pair_integrals,
    beta_target,
    beta_pair,
    beta_sign,
    alpha_target,
    alpha_pair,
    alpha_sign,
):
    rows, cols = ci_vector.shape
    pairs = one_body.shape[0]
    nexc = beta_target.shape[0]
    blocks = lax.axis_size("alpha")
    chunks = lax.axis_size("beta")
    place = jnp.stack([lax.axis_index("alpha"), lax.axis_index("beta")])
    bf16 = jnp.bfloat16

    civec_bf = ci_vector.astype(bf16)
    gathered = [civec_bf] + [
        lax.ppermute(civec_bf, "beta", [(d, d ^ s) for d in range(chunks)])
        for s in range(1, chunks)
    ]

    beta_code = beta_target * 256 + beta_pair * 2 + beta_sign
    own = (lax.axis_index("beta") * cols + jnp.arange(cols, dtype=jnp.int32)) * 256 + 1
    extra = jnp.stack([own + 2 * (pairs + 2), own + 2 * (pairs + 3)])
    beta_code = jnp.concatenate([beta_code, extra]).T
    tiles = -(-cols // (2 * GROUP * UNROLL)) * 2 * UNROLL
    beta_code = jnp.pad(beta_code, ((0, tiles * GROUP - cols), (0, 0)))
    beta_code = beta_code.reshape(tiles, GROUP * (nexc + 2))
    beta_code = jnp.pad(beta_code, ((0, 0), (0, LANES - GROUP * (nexc + 2))))
    beta_code = beta_code.reshape(tiles // 2, 1, 2 * LANES)
    alpha_code = alpha_target * 256 + alpha_pair * 2 + alpha_sign
    depth = nexc + 8
    one_rows = jnp.arange(depth - nexc, dtype=jnp.int32)[:, None] * 2 + 2 * pairs + 1
    one_rows = jnp.broadcast_to(one_rows, (depth - nexc, rows))
    weight_code = jnp.concatenate([alpha_code, one_rows]).T
    weight_code = weight_code.reshape(rows * depth // LANES, 1, LANES)
    alpha_code = alpha_code.T.reshape(rows * nexc // LANES, 1, LANES)

    h_high, h_low = high_low(one_body)
    halves = jnp.stack([h_high, h_low]).astype(bf16)
    corner = jnp.zeros((2, 2), bf16)
    vt = jnp.concatenate(
        [
            jnp.concatenate([pair_integrals.T, halves.T], axis=1),
            jnp.zeros((2, pairs + 2), bf16),
            jnp.concatenate([halves, corner], axis=1),
        ]
    )
    vt = jnp.pad(vt, ((0, LANES - pairs - 4), (0, LANES - pairs - 2)))

    vmem = pl.BlockSpec(memory_space=pltpu.VMEM)
    weights = pl.pallas_call(
        functools.partial(weight_kernel, rows * depth // LANES),
        out_shape=jax.ShapeDtypeStruct((rows * depth, LANES), bf16),
        in_specs=[vmem] * 2,
        out_specs=vmem,
        name="weights",
    )(weight_code, vt)

    stride = rows + 8
    sizes = (chunks, rows, cols, nexc, depth, blocks, stride)
    outs = pl.pallas_call(
        functools.partial(local_kernel, sizes),
        out_shape=[jax.ShapeDtypeStruct((rows, cols), jnp.float32)]
        + [jax.ShapeDtypeStruct((rows, cols), bf16)] * (blocks - 1),
        in_specs=[pl.BlockSpec(memory_space=pltpu.SMEM)] + [vmem] * (3 + chunks),
        out_specs=[vmem] * blocks,
        scratch_shapes=[
            pltpu.VMEM((tiles * GROUP * stride, LANES), jnp.float32),
            pltpu.VMEM((rows * nexc, cols), bf16),
            pltpu.VMEM((rows, cols), jnp.float32),
            pltpu.VMEM((tiles // 2, rows, 2 * LANES), bf16),
        ],
        compiler_params=pltpu.CompilerParams(vmem_limit_bytes=56 * 1024 * 1024),
        name="sigma_local",
    )(place, beta_code, alpha_code, weights, *gathered)
    total = outs[0]
    for s in range(1, blocks):
        got = lax.ppermute(outs[s], "alpha", [(d, d ^ s) for d in range(blocks)])
        total = total + got.astype(jnp.float32)
    return total


def solution(mesh):
    placed = (
        P("alpha", "beta"),
        P(),
        P(),
        P(None, "beta"),
        P(None, "beta"),
        P(None, "beta"),
        P(None, "alpha"),
        P(None, "alpha"),
        P(None, "alpha"),
    )
    return jax.shard_map(
        shards, mesh=mesh, in_specs=placed, out_specs=P("alpha", "beta"), check_vma=False
    )
```

time: 82.6 us -> 51.9 us (0.63)
  Pallas kernels: 48.9 us -> 19.3 us
  blocking collectives: 7.63 us -> 0 us
  other arithmetic: 2.28 us -> 5.59 us
  starting transfers between devices: 11.1 us -> 14.4 us
    pallas_call x1, Pallas kernels: 48.9 us -> 16.6 us  [shards(): pl.pallas_call(functools.partial(local_kernel, sizes), out_shape=[jax.Sha...]
    all_gather x1 -> x0, blocking collectives: 7.63 us -> none  [shards(): gathered = lax.all_gather(civec_bf, 'beta', axis=0)]
    ppermute x0 -> x3, starting transfers between devices: none -> 3.12 us  [shards(): lax.ppermute(civec_bf, 'beta', [(d, d ^ s) for d in range(chunks)])]
    pallas_call x0 -> x1, Pallas kernels: none -> 2.69 us  [shards(): pl.pallas_call(functools.partial(weight_kernel, rows * depth // LANES), o...]
    unnamed x20 -> x10, local copies, waits for them, and re-layouts: 3.13 us -> 1.63 us
    convert_element_type x1, other arithmetic: 0.01 us -> 0.91 us  [shards(): civec_bf = ci_vector.astype(bf16)]
  transfers between devices with their start and end apart: 7 -> 10, of which waited for: 2 -> 2; matrix products, arithmetic and copies ran while one was open for 0% -> 14% of each run, Pallas kernels for 0% -> 5%
where the time goes in v2:
time: 51.9 us; the launch traced here: 51.5 us
  Pallas kernels  19.3 us (37%)
  starting transfers between devices  14.4 us (28%)
  waiting for transfers between devices  7.27 us (14%)
  other arithmetic  5.59 us (11%)
  local copies, waits for them, and re-layouts  4.87 us (9%)
    pallas_call x1, Pallas kernels, shards(): pl.pallas_call(functools.partial(local_kernel, sizes), out_shape=[jax.Sha...  16.6 us
    ppermute x7, starting transfers between devices, shards(): got = lax.ppermute(outs[s], 'alpha', [(d, d ^ s) for d in range(blocks)])  11.2 us
    ppermute x7, waiting for transfers between devices, shards(): got = lax.ppermute(outs[s], 'alpha', [(d, d ^ s) for d in range(blocks)])  7.26 us
    ppermute x3, starting transfers between devices, shards(): lax.ppermute(civec_bf, 'beta', [(d, d ^ s) for d in range(chunks)])  3.12 us
    pallas_call x1, Pallas kernels, shards(): pl.pallas_call(functools.partial(weight_kernel, rows * depth // LANES), o...  2.69 us
    unnamed x10, local copies, waits for them, and re-layouts  1.63 us
    add x1, other arithmetic, shards(): total = total + got.astype(jnp.float32)  1.63 us
  transfers between devices with their start and end apart: 10, of which 2 were waited for; matrix products, arithmetic and copies ran while one was open for 14% of the time, Pallas kernels for 5%

profile of v2, /device:TPU:0, one launch (start us, length us, event | category | flops | bytes accessed | tf_op | source)
XLA Modules:
  0.0 51.5 jit_solution(8264490807742921277)
XLA Ops:
  0.0 0.9 %convert_element_type.27.rest_0_ = bf16[128,256]{1,0:T(8,128)(2,1)S(1)} convert(f32[128,256]{1,0:T(8,128)} %param.9) | non-fusion elementwise | flops 32768 | bytes 196608 | tf_op jit(solution)/shard_map/convert_element_type | solution.py:133
  0.9 0.0 copy-start
  0.9 2.4 %collective-permute-start.2 = (bf16[128,256]{1,0:T(8,128)(2,1)S(1)}, bf16[128,256]{1,0:T(8,128)(2,1)S(1)}, u32[]{:S(2)}, u32[]{:S(2)}) collective-permute-start(bf16[128,256]{1,0:T(8,128)(2,1)S(1)} %convert_element_type.27.rest_0_), channel_id=1, source_target_pairs={{0,3},{1,2},{2,1},{3,0},{4,7},{5,6},{6,5},{7,4},{8,11},{9,10},{10,... | collective-permute-start | bytes 196616 | tf_op jit(solution)/shard_map/ppermute | solution.py:135
  3.4 0.6 %collective-permute-start.1 = (bf16[128,256]{1,0:T(8,128)(2,1)S(1)}, bf16[128,256]{1,0:T(8,128)(2,1)S(1)}, u32[]{:S(2)}, u32[]{:S(2)}) collective-permute-start(bf16[128,256]{1,0:T(8,128)(2,1)S(1)} %convert_element_type.27.rest_0_), channel_id=1, source_target_pairs={{0,2},{1,3},{2,0},{3,1},{4,6},{5,7},{6,4},{7,5},{8,10},{9,11},{10,... | collective-permute-start | bytes 196616 | tf_op jit(solution)/shard_map/ppermute | solution.py:135
  4.0 0.0 collective-permute-start
  4.0 0.7 %fusion.4 = (bf16[1,102]{1,0:T(2,128)(2,1)S(1)}, bf16[1,102]{1,0:T(2,128)(2,1)S(1)}) fusion(f32[102]{0:T(128)} %param.10), kind=kLoop, calls=%fused_computation.13 | loop fusion | flops 408 | bytes 816 | tf_op jit(solution)/shard_map/stack | solution.py:157
  4.8 0.1 copy.18
  4.9 0.9 %copy.17 = bf16[102,102]{0,1:T(8,128)(2,1)S(1)} copy(bf16[102,102]{1,0:T(8,128)(2,1)} %param.11) | data formatting | bytes 41616 | tf_op args[2]
  5.8 0.1 pad.18.clone
  5.8 0.1 fusion.1
  5.9 0.6 %pad.15.vt_ref = bf16[128,128]{1,0:T(8,128)(2,1)} pad(bf16[106,104]{1,0:T(8,128)(2,1)S(1)} %fusion.1, bf16[]{:T(256)} %constant.8.clone.1), padding=0_22x0_24 | pad | bytes 54818 | tf_op jit(solution)/shard_map/jit(_pad)/pad | solution.py:166
  6.6 0.1 pad.23.clone
  6.6 0.8 %add_add_fusion.1 = s32[40,128]{1,0:T(8,128)S(1)} fusion(s32[40,128]{1,0:T(8,128)} %param.17, s32[40,128]{1,0:T(8,128)} %param.16, s32[40,128]{1,0:T(8,128)} %param.15), kind=kLoop, calls=%fused_computation.7 | loop fusion | flops 20480 | bytes 81920 | tf_op jit(solution)/shard_map/add | solution.py:148
  7.4 0.1 add_bitcast_fusion.1
  7.5 0.1 copy.16
  7.6 0.7 %reshape.39 = s32[48,1,128]{2,0,1:T(8,128)} reshape(s32[128,48]{1,0:T(8,128)S(1)} %copy.16) | data formatting | bytes 49152 | tf_op jit(solution)/shard_map/reshape | solution.py:153
  8.3 0.1 copy.15
  8.4 0.7 %reshape.38 = s32[40,1,128]{2,0,1:T(8,128)} reshape(s32[128,40]{1,0:T(8,128)S(1)} %copy.15) | data formatting | bytes 40960 | tf_op jit(solution)/shard_map/reshape | solution.py:154
  9.1 0.8 %add_add_fusion = s32[40,256]{1,0:T(8,128)S(1)} fusion(s32[40,256]{1,0:T(8,128)} %param.14, s32[40,256]{1,0:T(8,128)} %param.13, s32[40,256]{1,0:T(8,128)} %param.12), kind=kLoop, calls=%fused_computation.4 | loop fusion | flops 40960 | bytes 163840 | tf_op jit(solution)/shard_map/add | solution.py:139
  9.9 0.1 copy.21
  10.1 0.1 reshape.36
  10.2 0.6 %pad.14 = s32[88,128]{1,0:T(8,128)} pad(s32[88,126]{1,0:T(8,128)S(1)} %reshape.36, s32[]{:T(128)} %constant.17.clone.1), padding=0_0x0_2 | pad | bytes 89412 | tf_op jit(solution)/shard_map/jit(_pad)/pad | solution.py:146
  10.8 2.7 %weights.1 = bf16[6144,128]{1,0:T(8,128)(2,1)} custom-call(s32[48,1,128]{2,1,0:T(1,128)} %bitcast.20, bf16[128,128]{1,0:T(8,128)(2,1)} %pad.15.vt_ref), custom_call_target="tpu_custom_call" | custom-call | tf_op jit(solution)/shard_map/weights/pallas_call | solution.py:169
  13.5 0.0 copy-done
  13.5 0.6 %pad_add_fusion.place_ref = s32[2]{0:T(128)} fusion(s32[1]{0:T(128)} %bitcast.1, s32[1]{0:T(128)} %bitcast), kind=kLoop, calls=%fused_computation.16 | loop fusion | flops 2 | bytes 16 | tf_op jit(solution)/shard_map/stack | solution.py:130
  14.1 0.0 collective-permute-done.2.rest_3_
  14.1 0.0 copy-start.1
  14.1 0.0 collective-permute-done.1.rest_2_
  14.1 0.0 copy-start.2
  14.1 0.0 collective-permute-done.rest_1_
  14.1 0.0 copy-start.3
  14.1 0.6 %copy-done.1 = bf16[128,256]{1,0:T(8,128)(2,1)} copy-done((bf16[128,256]{1,0:T(8,128)(2,1)}, bf16[128,256]{1,0:T(8,128)(2,1)S(1)}, u32[]{:S(2)}) %copy-start.1) | copy-done | bytes 65560
  14.7 0.0 copy-done.2
  14.7 0.0 copy-done.3
  14.8 16.6 %sigma_local.1 = (f32[128,256]{1,0:T(8,128)}, bf16[128,256]{1,0:T(8,128)(2,1)}, bf16[128,256]{1,0:T(8,128)(2,1)}, bf16[128,256]{1,0:T(8,128)(2,1)}, bf16[128,256...) custom-call(s32[2]{0:T(128)} %pad_add_fusion.place_ref, ...), custom_call_target="tpu_custom_call" | custom-call | tf_op jit(solution)/shard_map/sigma_local/pallas_call | solution.py:179
  31.4 1.8 %collective-permute-start.3 = (bf16[128,256]{1,0:T(8,128)(2,1)}, bf16[128,256]{1,0:T(8,128)(2,1)S(1)}, u32[]{:S(2)}, u32[]{:S(2)}) collective-permute-start(bf16[128,256]{1,0:T(8,128)(2,1)} %get-tuple-element.14), channel_id=1, source_target_pairs={{0,4},{4,0},{8,12},{12,8},{16,20},{20,16},{24,28},{28,24},{1,5},{5... | collective-permute-start | bytes 196616 | tf_op jit(solution)/shard_map/ppermute | solution.py:196
  33.1 1.6 %collective-permute-start.4 = (bf16[128,256]{1,0:T(8,128)(2,1)}, bf16[128,256]{1,0:T(8,128)(2,1)S(1)}, u32[]{:S(2)}, u32[]{:S(2)}) collective-permute-start(bf16[128,256]{1,0:T(8,128)(2,1)} %get-tuple-element.15), channel_id=1, source_target_pairs={{0,8},{4,12},{8,0},{12,4},{16,24},{20,28},{24,16},{28,20},{1,9},{5... | collective-permute-start | bytes 196616 | tf_op jit(solution)/shard_map/ppermute | solution.py:196
  34.7 0.1 collective-permute-start.5
  34.9 2.8 %collective-permute-start.6 = (bf16[128,256]{1,0:T(8,128)(2,1)}, bf16[128,256]{1,0:T(8,128)(2,1)S(1)}, u32[]{:S(2)}, u32[]{:S(2)}) collective-permute-start(bf16[128,256]{1,0:T(8,128)(2,1)} %get-tuple-element.17), channel_id=1, source_target_pairs={{0,16},{4,20},{8,24},{12,28},{16,0},{20,4},{24,8},{28,12},{1,17},{... | collective-permute-start | bytes 196616 | tf_op jit(solution)/shard_map/ppermute | solution.py:196
  37.7 1.3 %collective-permute-start.7 = (bf16[128,256]{1,0:T(8,128)(2,1)}, bf16[128,256]{1,0:T(8,128)(2,1)S(1)}, u32[]{:S(2)}, u32[]{:S(2)}) collective-permute-start(bf16[128,256]{1,0:T(8,128)(2,1)} %get-tuple-element.18), channel_id=1, source_target_pairs={{0,20},{4,16},{8,28},{12,24},{16,4},{20,0},{24,12},{28,8},{1,21},{... | collective-permute-start | bytes 196616 | tf_op jit(solution)/shard_map/ppermute | solution.py:196
  39.0 0.0 collective-permute-done.3
  39.0 3.6 %collective-permute-start.8 = (bf16[128,256]{1,0:T(8,128)(2,1)}, bf16[128,256]{1,0:T(8,128)(2,1)S(1)}, u32[]{:S(2)}, u32[]{:S(2)}) collective-permute-start(bf16[128,256]{1,0:T(8,128)(2,1)} %get-tuple-element.19), channel_id=1, source_target_pairs={{0,24},{4,28},{8,16},{12,20},{16,8},{20,12},{24,0},{28,4},{1,25},{... | collective-permute-start | bytes 196616 | tf_op jit(solution)/shard_map/ppermute | solution.py:196
  42.6 0.0 collective-permute-done.4
  42.6 0.0 collective-permute-start.9
  42.6 0.0 collective-permute-done.5
  42.6 0.0 collective-permute-done.6
  42.6 5.7 %collective-permute-done.7 = bf16[128,256]{1,0:T(8,128)(2,1)S(1)} collective-permute-done((bf16[128,256]{1,0:T(8,128)(2,1)}, bf16[128,256]{1,0:T(8,128)(2,1)S(1)}, u32[]{:S(2)}, u32[]{:S(2)}) %collective-permute-start.7) | collective-permute-done | bytes 65568 | tf_op jit(solution)/shard_map/ppermute | solution.py:196
  48.3 0.0 collective-permute-done.8
  48.3 1.6 %collective-permute-done.9 = bf16[128,256]{1,0:T(8,128)(2,1)S(1)} collective-permute-done((bf16[128,256]{1,0:T(8,128)(2,1)}, bf16[128,256]{1,0:T(8,128)(2,1)S(1)}, u32[]{:S(2)}, u32[]{:S(2)}) %collective-permute-start.9) | collective-permute-done | bytes 65568 | tf_op jit(solution)/shard_map/ppermute | solution.py:196
  49.9 1.6 %convert_add_fusion = f32[128,256]{1,0:T(8,128)} fusion(bf16[128,256]{1,0:T(8,128)(2,1)S(1)} %collective-permute-done.9, bf16[128,256]{1,0:T(8,128)(2,1)S(1)} %collective-permute-done.8, bf16[128,256]{1,0:T(8,128)(2,1)S(1)} %collective-permute-done.7, bf16[128,256]{1,0:T(8,128)(2,1)S(1)} %collective-permute-done.6, ...), kind=kLoop, calls=%fused_computation | loop fusion | flops 458752 | bytes 720896 | tf_op jit(solution)/shard_map/add | solution.py:197
  (7 shorter events, 0.1 us)
Async XLA Ops:
  0.9 12.6 %copy-start = (bf16[128,256]{1,0:T(8,128)(2,1)}, bf16[128,256]{1,0:T(8,128)(2,1)S(1)}, u32[]{:S(2)}) copy-start(bf16[128,256]{1,0:T(8,128)(2,1)S(1)} %convert_element_type.27.rest_0_) | copy-start | bytes 196612
  0.9 13.1 %collective-permute-start.2 = (bf16[128,256]{1,0:T(8,128)(2,1)S(1)}, bf16[128,256]{1,0:T(8,128)(2,1)S(1)}, u32[]{:S(2)}, u32[]{:S(2)}) collective-permute-start(bf16[128,256]{1,0:T(8,128)(2,1)S(1)} %convert_element_type.27.rest_0_), channel_id=1, source_target_pairs={{0,3},{1,2},{2,1},{3,0},{4,7},{5,6},{6,5},{7,4},{8,11},{9,10},{10,... | collective-permute-start | bytes 196616 | tf_op jit(solution)/shard_map/ppermute | solution.py:135
  3.4 10.7 %collective-permute-start.1 = (bf16[128,256]{1,0:T(8,128)(2,1)S(1)}, bf16[128,256]{1,0:T(8,128)(2,1)S(1)}, u32[]{:S(2)}, u32[]{:S(2)}) collective-permute-start(bf16[128,256]{1,0:T(8,128)(2,1)S(1)} %convert_element_type.27.rest_0_), channel_id=1, source_target_pairs={{0,2},{1,3},{2,0},{3,1},{4,6},{5,7},{6,4},{7,5},{8,10},{9,11},{10,... | collective-permute-start | bytes 196616 | tf_op jit(solution)/shard_map/ppermute | solution.py:135
  4.0 10.1 %collective-permute-start = (bf16[128,256]{1,0:T(8,128)(2,1)S(1)}, bf16[128,256]{1,0:T(8,128)(2,1)S(1)}, u32[]{:S(2)}, u32[]{:S(2)}) collective-permute-start(bf16[128,256]{1,0:T(8,128)(2,1)S(1)} %convert_element_type.27.rest_0_), channel_id=1, source_target_pairs={{0,1},{1,0},{2,3},{3,2},{4,5},{5,4},{6,7},{7,6},{8,9},{9,8},{10,11... | collective-permute-start | bytes 196616 | tf_op jit(solution)/shard_map/ppermute | solution.py:135
  14.1 0.6 %copy-start.1 = (bf16[128,256]{1,0:T(8,128)(2,1)}, bf16[128,256]{1,0:T(8,128)(2,1)S(1)}, u32[]{:S(2)}) copy-start(bf16[128,256]{1,0:T(8,128)(2,1)S(1)} %collective-permute-done.2.rest_3_) | copy-start | bytes 196612
  14.1 0.6 %copy-start.2 = (bf16[128,256]{1,0:T(8,128)(2,1)}, bf16[128,256]{1,0:T(8,128)(2,1)S(1)}, u32[]{:S(2)}) copy-start(bf16[128,256]{1,0:T(8,128)(2,1)S(1)} %collective-permute-done.1.rest_2_) | copy-start | bytes 196612
  14.1 0.7 %copy-start.3 = (bf16[128,256]{1,0:T(8,128)(2,1)}, bf16[128,256]{1,0:T(8,128)(2,1)S(1)}, u32[]{:S(2)}) copy-start(bf16[128,256]{1,0:T(8,128)(2,1)S(1)} %collective-permute-done.rest_1_) | copy-start | bytes 196612
  31.4 7.6 %collective-permute-start.3 = (bf16[128,256]{1,0:T(8,128)(2,1)}, bf16[128,256]{1,0:T(8,128)(2,1)S(1)}, u32[]{:S(2)}, u32[]{:S(2)}) collective-permute-start(bf16[128,256]{1,0:T(8,128)(2,1)} %get-tuple-element.14), channel_id=1, source_target_pairs={{0,4},{4,0},{8,12},{12,8},{16,20},{20,16},{24,28},{28,24},{1,5},{5... | collective-permute-start | bytes 196616 | tf_op jit(solution)/shard_map/ppermute | solution.py:196
  33.1 9.5 %collective-permute-start.4 = (bf16[128,256]{1,0:T(8,128)(2,1)}, bf16[128,256]{1,0:T(8,128)(2,1)S(1)}, u32[]{:S(2)}, u32[]{:S(2)}) collective-permute-start(bf16[128,256]{1,0:T(8,128)(2,1)} %get-tuple-element.15), channel_id=1, source_target_pairs={{0,8},{4,12},{8,0},{12,4},{16,24},{20,28},{24,16},{28,20},{1,9},{5... | collective-permute-start | bytes 196616 | tf_op jit(solution)/shard_map/ppermute | solution.py:196
  34.7 7.9 %collective-permute-start.5 = (bf16[128,256]{1,0:T(8,128)(2,1)}, bf16[128,256]{1,0:T(8,128)(2,1)S(1)}, u32[]{:S(2)}, u32[]{:S(2)}) collective-permute-start(bf16[128,256]{1,0:T(8,128)(2,1)} %get-tuple-element.16), channel_id=1, source_target_pairs={{0,12},{4,8},{8,4},{12,0},{16,28},{20,24},{24,20},{28,16},{1,13},{... | collective-permute-start | bytes 196616 | tf_op jit(solution)/shard_map/ppermute | solution.py:196
  34.9 7.8 %collective-permute-start.6 = (bf16[128,256]{1,0:T(8,128)(2,1)}, bf16[128,256]{1,0:T(8,128)(2,1)S(1)}, u32[]{:S(2)}, u32[]{:S(2)}) collective-permute-start(bf16[128,256]{1,0:T(8,128)(2,1)} %get-tuple-element.17), channel_id=1, source_target_pairs={{0,16},{4,20},{8,24},{12,28},{16,0},{20,4},{24,8},{28,12},{1,17},{... | collective-permute-start | bytes 196616 | tf_op jit(solution)/shard_map/ppermute | solution.py:196
  37.7 10.6 %collective-permute-start.7 = (bf16[128,256]{1,0:T(8,128)(2,1)}, bf16[128,256]{1,0:T(8,128)(2,1)S(1)}, u32[]{:S(2)}, u32[]{:S(2)}) collective-permute-start(bf16[128,256]{1,0:T(8,128)(2,1)} %get-tuple-element.18), channel_id=1, source_target_pairs={{0,20},{4,16},{8,28},{12,24},{16,4},{20,0},{24,12},{28,8},{1,21},{... | collective-permute-start | bytes 196616 | tf_op jit(solution)/shard_map/ppermute | solution.py:196
  39.0 9.3 %collective-permute-start.8 = (bf16[128,256]{1,0:T(8,128)(2,1)}, bf16[128,256]{1,0:T(8,128)(2,1)S(1)}, u32[]{:S(2)}, u32[]{:S(2)}) collective-permute-start(bf16[128,256]{1,0:T(8,128)(2,1)} %get-tuple-element.19), channel_id=1, source_target_pairs={{0,24},{4,28},{8,16},{12,20},{16,8},{20,12},{24,0},{28,4},{1,25},{... | collective-permute-start | bytes 196616 | tf_op jit(solution)/shard_map/ppermute | solution.py:196
  42.6 7.3 %collective-permute-start.9 = (bf16[128,256]{1,0:T(8,128)(2,1)}, bf16[128,256]{1,0:T(8,128)(2,1)S(1)}, u32[]{:S(2)}, u32[]{:S(2)}) collective-permute-start(bf16[128,256]{1,0:T(8,128)(2,1)} %get-tuple-element.20), channel_id=1, source_target_pairs={{0,28},{4,24},{8,20},{12,16},{16,12},{20,8},{24,4},{28,0},{1,29},{... | collective-permute-start | bytes 196616 | tf_op jit(solution)/shard_map/ppermute | solution.py:196

commit v3 on v2

--- a/solution.py
+++ b/solution.py
@@ -13,20 +13,85 @@
 NT = (((1,), (1,)), ((), ()))
 
 
-def high_low(values):
-    high = lax.reduce_precision(values, 8, 7)
-    return high, values - high
-
-
-def weight_kernel(tiles, alpha_ref, vt_ref, weights_ref):
-    for t in range(tiles):
-        code = alpha_ref[t]
-        pair = (code >> 1) & 127
-        sign = (2 * (code & 1) - 1).astype(jnp.float32)
-        q_ids = lax.broadcasted_iota(jnp.int32, (LANES, LANES), 0)
-        hot = jnp.where(q_ids == pair, sign, 0.0).astype(jnp.bfloat16)
-        u_t = jnp.dot(vt_ref[...], hot, preferred_element_type=jnp.float32)
-        weights_ref[t * LANES : (t + 1) * LANES, :] = u_t.T.astype(jnp.bfloat16)
+def index_kernel(
+    sizes,
+    own_ref,
+    beta_target,
+    beta_pair,
+    beta_sign,
+    alpha_target,
+    alpha_pair,
+    alpha_sign,
+    one_body,
+    integrals,
+    beta_ref,
+    alpha_ref,
+    weights_ref,
+    table,
+    turned,
+):
+    rows, cols, nexc, depth, tiles, pairs = sizes
+    bf16, f32 = jnp.bfloat16, jnp.float32
+    per_tile = LANES // GROUP
+    lane = lax.broadcasted_iota(jnp.int32, (8, LANES), 1)
+
+    h = one_body[...]
+    h_high = h.astype(bf16).astype(f32)
+    halves = jnp.concatenate([h_high, h - h_high], axis=0)
+    table[...] = jnp.zeros_like(table)
+    table[pairs + 2 : pairs + 4, :pairs] = halves
+    columns = table[...].T
+    table[...] = jnp.zeros_like(table)
+    table[:pairs, :pairs] = integrals[...].astype(f32)
+    table[pairs : pairs + 2, :pairs] = halves
+    rows_of = (table[...] + columns).astype(bf16)
+
+    signed = (2 * alpha_sign[...] - 1) * (alpha_pair[...] + 1)
+    after = lax.broadcasted_iota(jnp.int32, (depth - nexc, rows), 0) + pairs + 1
+    signed = jnp.concatenate([signed, after], axis=0)
+    q_ids = lax.broadcasted_iota(jnp.int32, (depth, LANES), 1) + 1
+    batch = 16
+    for b in range(rows // batch):
+        hots = []
+        for a in range(b * batch, (b + 1) * batch):
+            column = jnp.broadcast_to(signed[:, a : a + 1], (depth, LANES))
+            value = jnp.where(column > 0, 1.0, -1.0)
+            hots.append(jnp.where(jnp.abs(column) == q_ids, value, 0.0).astype(bf16))
+        u = jnp.dot(jnp.concatenate(hots, axis=0), rows_of, preferred_element_type=f32)
+        weights_ref[b * batch * depth : (b + 1) * batch * depth, :] = u.astype(bf16)
+
+    code = beta_target[...] * 256 + beta_pair[...] * 2 + beta_sign[...]
+    own = own_ref[0] * cols + lax.broadcasted_iota(jnp.int32, (2, cols), 1)
+    extra = lax.broadcasted_iota(jnp.int32, (2, cols), 0) + pairs + 2
+    extra = own * 256 + extra * 2 + 1
+    blank = jnp.zeros((LANES - nexc - 2, cols), jnp.int32)
+    code = jnp.concatenate([code, extra, blank], axis=0).astype(f32)
+    turned[...] = jnp.zeros_like(turned)
+    for c in range(cols // LANES):
+        turned[c * LANES : (c + 1) * LANES, :] = code[:, c * LANES : (c + 1) * LANES].T
+    total = jnp.zeros((tiles, LANES), f32)
+    for m in range(GROUP):
+        part = turned[pl.ds(m, tiles, stride=GROUP), :]
+        total += pltpu.roll(part, m * per_tile, 1) if m else part
+    total = total.astype(jnp.int32)
+    beta_ref[...] = total
+
+    code = jnp.concatenate(
+        [alpha_target[...], jnp.zeros((LANES - nexc, rows), jnp.int32)], axis=0
+    )
+    turned[:rows, :] = code.astype(f32).T
+    period = rows * nexc // LANES // 8
+    step = period * LANES // nexc
+    found = [jnp.zeros((8, LANES), f32) for w in range(period)]
+    for j in range(step):
+        part = turned[pl.ds(j, 8, stride=step), :]
+        w, shift = divmod(j * nexc, LANES)
+        part = pltpu.roll(part, shift, 1) if shift else part
+        found[w] += jnp.where(lane >= shift, part, 0.0)
+        if shift + nexc > LANES:
+            found[w + 1] += jnp.where(lane < shift + nexc - LANES, part, 0.0)
+    for w in range(period):
+        alpha_ref[8 * w : 8 * w + 8, :] = found[w].astype(jnp.int32)
 
 
 def local_kernel(sizes, place_ref, beta_ref, alpha_ref, weights, *rest):
@@ -36,11 +101,14 @@
     density, lifted, same, picked = rest
     per_tile = LANES // GROUP
     bf16, f32 = jnp.bfloat16, jnp.float32
-    groups = beta_ref.shape[0]
+    groups = beta_ref.shape[0] // 2
     my_alpha, my_beta = place_ref[0], place_ref[1]
 
+    def beta_code(g):
+        return jnp.concatenate([beta_ref[pl.ds(2 * g, 1), :], beta_ref[pl.ds(2 * g + 1, 1), :]], axis=1)
+
     def gather_step(g, carry):
-        target = beta_ref[g] >> 8
+        target = beta_code(g) >> 8
         low = lax.rem(target, cols)
         high = lax.div(target, cols) ^ my_beta
         j_ids = lax.broadcasted_iota(jnp.int32, (cols, 2 * LANES), 0)
@@ -56,7 +124,7 @@
     lax.fori_loop(0, groups, gather_step, 0, unroll=UNROLL)
 
     def density_step(g, carry):
-        code = beta_ref[g]
+        code = beta_code(g)
         pair = (code >> 1) & 127
         sign = (2 * (code & 1) - 1).astype(f32)
         lane = lax.broadcasted_iota(jnp.int32, (1, 2 * LANES), 1)
@@ -94,15 +162,16 @@
     for s in range(blocks):
         base = (my_alpha ^ s) * rows
         total = jnp.zeros((rows, cols), f32)
-        for t in range(rows * nexc // LANES // 8):
+        period = rows * nexc // LANES // 8
+        for t in range(8):
             hots = []
-            for w in range(8):
-                target = (alpha_ref[8 * t + w] >> 8) - base
+            for w in range(period):
+                target = alpha_ref[8 * w + t : 8 * w + t + 1, :] - base
                 b_ids = lax.broadcasted_iota(jnp.int32, (rows, LANES), 0)
                 hots.append(jnp.where(b_ids == target, 1.0, 0.0).astype(bf16))
             total += jnp.dot(
                 jnp.concatenate(hots, axis=1),
-                lifted[8 * t * LANES : 8 * (t + 1) * LANES, :],
+                lifted[period * t * LANES : period * (t + 1) * LANES, :],
                 preferred_element_type=f32,
             )
         if s == 0:
@@ -136,43 +205,34 @@
         for s in range(1, chunks)
     ]
 
-    beta_code = beta_target * 256 + beta_pair * 2 + beta_sign
-    own = (lax.axis_index("beta") * cols + jnp.arange(cols, dtype=jnp.int32)) * 256 + 1
-    extra = jnp.stack([own + 2 * (pairs + 2), own + 2 * (pairs + 3)])
-    beta_code = jnp.concatenate([beta_code, extra]).T
+    depth = nexc + 8
     tiles = -(-cols // (2 * GROUP * UNROLL)) * 2 * UNROLL
-    beta_code = jnp.pad(beta_code, ((0, tiles * GROUP - cols), (0, 0)))
-    beta_code = beta_code.reshape(tiles, GROUP * (nexc + 2))
-    beta_code = jnp.pad(beta_code, ((0, 0), (0, LANES - GROUP * (nexc + 2))))
-    beta_code = beta_code.reshape(tiles // 2, 1, 2 * LANES)
-    alpha_code = alpha_target * 256 + alpha_pair * 2 + alpha_sign
-    depth = nexc + 8
-    one_rows = jnp.arange(depth - nexc, dtype=jnp.int32)[:, None] * 2 + 2 * pairs + 1
-    one_rows = jnp.broadcast_to(one_rows, (depth - nexc, rows))
-    weight_code = jnp.concatenate([alpha_code, one_rows]).T
-    weight_code = weight_code.reshape(rows * depth // LANES, 1, LANES)
-    alpha_code = alpha_code.T.reshape(rows * nexc // LANES, 1, LANES)
-
-    h_high, h_low = high_low(one_body)
-    halves = jnp.stack([h_high, h_low]).astype(bf16)
-    corner = jnp.zeros((2, 2), bf16)
-    vt = jnp.concatenate(
-        [
-            jnp.concatenate([pair_integrals.T, halves.T], axis=1),
-            jnp.zeros((2, pairs + 2), bf16),
-            jnp.concatenate([halves, corner], axis=1),
-        ]
-    )
-    vt = jnp.pad(vt, ((0, LANES - pairs - 4), (0, LANES - pairs - 2)))
-
     vmem = pl.BlockSpec(memory_space=pltpu.VMEM)
-    weights = pl.pallas_call(
-        functools.partial(weight_kernel, rows * depth // LANES),
-        out_shape=jax.ShapeDtypeStruct((rows * depth, LANES), bf16),
-        in_specs=[vmem] * 2,
-        out_specs=vmem,
-        name="weights",
-    )(weight_code, vt)
+    beta_code, alpha_code, weights = pl.pallas_call(
+        functools.partial(index_kernel, (rows, cols, nexc, depth, tiles, pairs)),
+        out_shape=[
+            jax.ShapeDtypeStruct((tiles, LANES), jnp.int32),
+            jax.ShapeDtypeStruct((rows * nexc // LANES, LANES), jnp.int32),
+            jax.ShapeDtypeStruct((rows * depth, LANES), bf16),
+        ],
+        in_specs=[pl.BlockSpec(memory_space=pltpu.SMEM)] + [vmem] * 8,
+        out_specs=[vmem] * 3,
+        scratch_shapes=[
+            pltpu.VMEM((LANES, LANES), jnp.float32),
+            pltpu.VMEM((tiles * GROUP, LANES), jnp.float32),
+        ],
+        name="index_lists",
+    )(
+        place[1:],
+        beta_target,
+        beta_pair,
+        beta_sign,
+        alpha_target,
+        alpha_pair,
+        alpha_sign,
+        one_body.reshape(1, pairs),
+        pair_integrals,
+    )
 
     stride = rows + 8
     sizes = (chunks, rows, cols, nexc, depth, blocks, stride)

time: 51.9 us -> 46.3 us (0.89)
  local copies, waits for them, and re-layouts: 4.87 us -> 0.65 us
  other arithmetic: 5.59 us -> 3.19 us
  Pallas kernels: 19.3 us -> 20.5 us
    add x4 -> x0, other arithmetic: 1.61 us -> none  [the longest x1 0.83 us: shards(): beta_code = beta_target * 256 + beta_pair * 2 + beta_sign]
    reshape x3 -> x0, local copies, waits for them, and re-layouts: 1.49 us -> none  [the longest x1 0.71 us: shards(): weight_code = weight_code.reshape(rows * depth // LANES, 1, LANES)]
    pad x3 -> x0, local copies, waits for them, and re-layouts: 1.26 us -> none  [the longest x1 0.63 us: shards(): vt = jnp.pad(vt, ((0, LANES - pairs - 4), (0, LANES - pairs - 2)))]
    unnamed x10 -> x8, local copies, waits for them, and re-layouts: 1.63 us -> 0.65 us
    pallas_call x1, Pallas kernels: 2.69 us -> 3.39 us  [shards(): pl.pallas_call(functools.partial(index_kernel, (rows, cols, nexc, depth,...]
    another operation x2 -> x0, other arithmetic: 0.67 us -> none  [shards(): halves = jnp.stack([h_high, h_low]).astype(bf16)]
  transfers between devices with their start and end apart: 10 -> 10, of which waited for: 2 -> 2; matrix products, arithmetic and copies ran while one was open for 14% -> 1% of each run, Pallas kernels for 5% -> 7%
where the time goes in v3:
time: 46.3 us; the launch traced here: 46 us
  Pallas kernels  20.5 us (44%)
  starting transfers between devices  14.4 us (31%)
  waiting for transfers between devices  7.26 us (16%)
  other arithmetic  3.19 us (7%)
  local copies, waits for them, and re-layouts  0.65 us (1%)
    pallas_call x1, Pallas kernels, shards(): pl.pallas_call(functools.partial(local_kernel, sizes), out_shape=[jax.Sha...  17.1 us
    ppermute x7, starting transfers between devices, shards(): got = lax.ppermute(outs[s], 'alpha', [(d, d ^ s) for d in range(blocks)])  11.2 us
    ppermute x7, waiting for transfers between devices, shards(): got = lax.ppermute(outs[s], 'alpha', [(d, d ^ s) for d in range(blocks)])  7.26 us
    pallas_call x1, Pallas kernels, shards(): pl.pallas_call(functools.partial(index_kernel, (rows, cols, nexc, depth,...  3.39 us
    ppermute x3, starting transfers between devices, shards(): lax.ppermute(civec_bf, 'beta', [(d, d ^ s) for d in range(chunks)])  3.12 us
    add x1, other arithmetic, shards(): total = total + got.astype(jnp.float32)  1.63 us
  transfers between devices with their start and end apart: 10, of which 2 were waited for; matrix products, arithmetic and copies ran while one was open for 1% of the time, Pallas kernels for 7%

profile of v3, /device:TPU:0, one launch (start us, length us, event | category | flops | bytes accessed | tf_op | source)
XLA Modules:
  0.0 46.0 jit_solution(5063384036804721429)
XLA Ops:
  0.0 0.9 %convert_element_type.24.rest_0_ = bf16[128,256]{1,0:T(8,128)(2,1)S(1)} convert(f32[128,256]{1,0:T(8,128)} %param.9) | non-fusion elementwise | flops 32768 | bytes 196608 | tf_op jit(solution)/shard_map/convert_element_type | solution.py:202
  0.9 0.0 copy-start
  0.9 2.4 %collective-permute-start.2 = (bf16[128,256]{1,0:T(8,128)(2,1)S(1)}, bf16[128,256]{1,0:T(8,128)(2,1)S(1)}, u32[]{:S(2)}, u32[]{:S(2)}) collective-permute-start(bf16[128,256]{1,0:T(8,128)(2,1)S(1)} %convert_element_type.24.rest_0_), channel_id=1, source_target_pairs={{0,3},{1,2},{2,1},{3,0},{4,7},{5,6},{6,5},{7,4},{8,11},{9,10},{10,... | collective-permute-start | bytes 196616 | tf_op jit(solution)/shard_map/ppermute | solution.py:204
  3.4 0.6 %collective-permute-start.1 = (bf16[128,256]{1,0:T(8,128)(2,1)S(1)}, bf16[128,256]{1,0:T(8,128)(2,1)S(1)}, u32[]{:S(2)}, u32[]{:S(2)}) collective-permute-start(bf16[128,256]{1,0:T(8,128)(2,1)S(1)} %convert_element_type.24.rest_0_), channel_id=1, source_target_pairs={{0,2},{1,3},{2,0},{3,1},{4,6},{5,7},{6,4},{7,5},{8,10},{9,11},{10,... | collective-permute-start | bytes 196616 | tf_op jit(solution)/shard_map/ppermute | solution.py:204
  4.0 0.0 collective-permute-start
  4.0 3.4 %index_lists.1 = (s32[88,128]{1,0:T(8,128)}, s32[40,128]{1,0:T(8,128)}, bf16[6144,128]{1,0:T(8,128)(2,1)}) custom-call(s32[1]{0:T(128)} %bitcast.1.own_ref, s32[40,256]{1,0:T(8,128)} %beta_target.1, s32[40,256]{1,0:T(8,128)} %beta_pair.1, s32[40,256]{1,0:T(8,128)} %beta_sign.1, s32[40,128]{1,0:T(8,128)} %alpha_target.1, s32[40,128]{1,0:T(8,128)} %alpha_pair.1, ...), custom_call_target="tpu_custom_call" | custom-call | tf_op jit(solution)/shard_map/index_lists/pallas_call | solution.py:211
  7.4 0.7 %pad_add_fusion.place_ref = s32[2]{0:T(128)} fusion(s32[1]{0:T(128)} %bitcast.1.own_ref, s32[1]{0:T(128)} %bitcast), kind=kLoop, calls=%fused_computation.1 | loop fusion | flops 2 | bytes 16 | tf_op jit(solution)/shard_map/stack | solution.py:199
  8.1 0.0 collective-permute-done.2.rest_3_
  8.1 0.0 copy-start.1
  8.1 0.0 collective-permute-done.1.rest_2_
  8.1 0.0 copy-start.2
  8.1 0.0 collective-permute-done.rest_1_
  8.1 0.0 copy-start.3
  8.1 0.0 copy-done
  8.1 0.6 %copy-done.1 = bf16[128,256]{1,0:T(8,128)(2,1)} copy-done((bf16[128,256]{1,0:T(8,128)(2,1)}, bf16[128,256]{1,0:T(8,128)(2,1)S(1)}, u32[]{:S(2)}) %copy-start.1) | copy-done | bytes 65560
  8.7 0.0 copy-done.2
  8.7 0.0 copy-done.3
  8.8 17.1 %sigma_local.1 = (f32[128,256]{1,0:T(8,128)}, bf16[128,256]{1,0:T(8,128)(2,1)}, bf16[128,256]{1,0:T(8,128)(2,1)}, bf16[128,256]{1,0:T(8,128)(2,1)}, bf16[128,256...) custom-call(s32[2]{0:T(128)} %pad_add_fusion.place_ref, ...), custom_call_target="tpu_custom_call" | custom-call | tf_op jit(solution)/shard_map/sigma_local/pallas_call | solution.py:239
  25.9 1.8 %collective-permute-start.3 = (bf16[128,256]{1,0:T(8,128)(2,1)}, bf16[128,256]{1,0:T(8,128)(2,1)S(1)}, u32[]{:S(2)}, u32[]{:S(2)}) collective-permute-start(bf16[128,256]{1,0:T(8,128)(2,1)} %get-tuple-element.20), channel_id=1, source_target_pairs={{0,4},{4,0},{8,12},{12,8},{16,20},{20,16},{24,28},{28,24},{1,5},{5... | collective-permute-start | bytes 196616 | tf_op jit(solution)/shard_map/ppermute | solution.py:256
  27.6 1.6 %collective-permute-start.4 = (bf16[128,256]{1,0:T(8,128)(2,1)}, bf16[128,256]{1,0:T(8,128)(2,1)S(1)}, u32[]{:S(2)}, u32[]{:S(2)}) collective-permute-start(bf16[128,256]{1,0:T(8,128)(2,1)} %get-tuple-element.21), channel_id=1, source_target_pairs={{0,8},{4,12},{8,0},{12,4},{16,24},{20,28},{24,16},{28,20},{1,9},{5... | collective-permute-start | bytes 196616 | tf_op jit(solution)/shard_map/ppermute | solution.py:256
  29.2 0.1 collective-permute-start.5
  29.4 2.8 %collective-permute-start.6 = (bf16[128,256]{1,0:T(8,128)(2,1)}, bf16[128,256]{1,0:T(8,128)(2,1)S(1)}, u32[]{:S(2)}, u32[]{:S(2)}) collective-permute-start(bf16[128,256]{1,0:T(8,128)(2,1)} %get-tuple-element.23), channel_id=1, source_target_pairs={{0,16},{4,20},{8,24},{12,28},{16,0},{20,4},{24,8},{28,12},{1,17},{... | collective-permute-start | bytes 196616 | tf_op jit(solution)/shard_map/ppermute | solution.py:256
  32.2 1.3 %collective-permute-start.7 = (bf16[128,256]{1,0:T(8,128)(2,1)}, bf16[128,256]{1,0:T(8,128)(2,1)S(1)}, u32[]{:S(2)}, u32[]{:S(2)}) collective-permute-start(bf16[128,256]{1,0:T(8,128)(2,1)} %get-tuple-element.24), channel_id=1, source_target_pairs={{0,20},{4,16},{8,28},{12,24},{16,4},{20,0},{24,12},{28,8},{1,21},{... | collective-permute-start | bytes 196616 | tf_op jit(solution)/shard_map/ppermute | solution.py:256
  33.5 0.0 collective-permute-done.3
  33.5 3.6 %collective-permute-start.8 = (bf16[128,256]{1,0:T(8,128)(2,1)}, bf16[128,256]{1,0:T(8,128)(2,1)S(1)}, u32[]{:S(2)}, u32[]{:S(2)}) collective-permute-start(bf16[128,256]{1,0:T(8,128)(2,1)} %get-tuple-element.25), channel_id=1, source_target_pairs={{0,24},{4,28},{8,16},{12,20},{16,8},{20,12},{24,0},{28,4},{1,25},{... | collective-permute-start | bytes 196616 | tf_op jit(solution)/shard_map/ppermute | solution.py:256
  37.1 0.0 collective-permute-done.4
  37.1 0.0 collective-permute-start.9
  37.1 0.0 collective-permute-done.5
  37.1 0.0 collective-permute-done.6
  37.1 5.7 %collective-permute-done.7 = bf16[128,256]{1,0:T(8,128)(2,1)S(1)} collective-permute-done((bf16[128,256]{1,0:T(8,128)(2,1)}, bf16[128,256]{1,0:T(8,128)(2,1)S(1)}, u32[]{:S(2)}, u32[]{:S(2)}) %collective-permute-start.7) | collective-permute-done | bytes 65568 | tf_op jit(solution)/shard_map/ppermute | solution.py:256
  42.8 0.0 collective-permute-done.8
  42.8 1.6 %collective-permute-done.9 = bf16[128,256]{1,0:T(8,128)(2,1)S(1)} collective-permute-done((bf16[128,256]{1,0:T(8,128)(2,1)}, bf16[128,256]{1,0:T(8,128)(2,1)S(1)}, u32[]{:S(2)}, u32[]{:S(2)}) %collective-permute-start.9) | collective-permute-done | bytes 65568 | tf_op jit(solution)/shard_map/ppermute | solution.py:256
  44.4 1.6 %convert_add_fusion = f32[128,256]{1,0:T(8,128)} fusion(bf16[128,256]{1,0:T(8,128)(2,1)S(1)} %collective-permute-done.9, bf16[128,256]{1,0:T(8,128)(2,1)S(1)} %collective-permute-done.8, bf16[128,256]{1,0:T(8,128)(2,1)S(1)} %collective-permute-done.7, bf16[128,256]{1,0:T(8,128)(2,1)S(1)} %collective-permute-done.6, ...), kind=kLoop, calls=%fused_computation | loop fusion | flops 458752 | bytes 720896 | tf_op jit(solution)/shard_map/add | solution.py:257
Async XLA Ops:
  0.9 7.2 %copy-start = (bf16[128,256]{1,0:T(8,128)(2,1)}, bf16[128,256]{1,0:T(8,128)(2,1)S(1)}, u32[]{:S(2)}) copy-start(bf16[128,256]{1,0:T(8,128)(2,1)S(1)} %convert_element_type.24.rest_0_) | copy-start | bytes 196612
  0.9 7.2 %collective-permute-start.2 = (bf16[128,256]{1,0:T(8,128)(2,1)S(1)}, bf16[128,256]{1,0:T(8,128)(2,1)S(1)}, u32[]{:S(2)}, u32[]{:S(2)}) collective-permute-start(bf16[128,256]{1,0:T(8,128)(2,1)S(1)} %convert_element_type.24.rest_0_), channel_id=1, source_target_pairs={{0,3},{1,2},{2,1},{3,0},{4,7},{5,6},{6,5},{7,4},{8,11},{9,10},{10,... | collective-permute-start | bytes 196616 | tf_op jit(solution)/shard_map/ppermute | solution.py:204
  3.4 4.7 %collective-permute-start.1 = (bf16[128,256]{1,0:T(8,128)(2,1)S(1)}, bf16[128,256]{1,0:T(8,128)(2,1)S(1)}, u32[]{:S(2)}, u32[]{:S(2)}) collective-permute-start(bf16[128,256]{1,0:T(8,128)(2,1)S(1)} %convert_element_type.24.rest_0_), channel_id=1, source_target_pairs={{0,2},{1,3},{2,0},{3,1},{4,6},{5,7},{6,4},{7,5},{8,10},{9,11},{10,... | collective-permute-start | bytes 196616 | tf_op jit(solution)/shard_map/ppermute | solution.py:204
  4.0 4.1 %collective-permute-start = (bf16[128,256]{1,0:T(8,128)(2,1)S(1)}, bf16[128,256]{1,0:T(8,128)(2,1)S(1)}, u32[]{:S(2)}, u32[]{:S(2)}) collective-permute-start(bf16[128,256]{1,0:T(8,128)(2,1)S(1)} %convert_element_type.24.rest_0_), channel_id=1, source_target_pairs={{0,1},{1,0},{2,3},{3,2},{4,5},{5,4},{6,7},{7,6},{8,9},{9,8},{10,11... | collective-permute-start | bytes 196616 | tf_op jit(solution)/shard_map/ppermute | solution.py:204
  8.1 0.6 %copy-start.1 = (bf16[128,256]{1,0:T(8,128)(2,1)}, bf16[128,256]{1,0:T(8,128)(2,1)S(1)}, u32[]{:S(2)}) copy-start(bf16[128,256]{1,0:T(8,128)(2,1)S(1)} %collective-permute-done.2.rest_3_) | copy-start | bytes 196612
  8.1 0.6 %copy-start.2 = (bf16[128,256]{1,0:T(8,128)(2,1)}, bf16[128,256]{1,0:T(8,128)(2,1)S(1)}, u32[]{:S(2)}) copy-start(bf16[128,256]{1,0:T(8,128)(2,1)S(1)} %collective-permute-done.1.rest_2_) | copy-start | bytes 196612
  8.1 0.7 %copy-start.3 = (bf16[128,256]{1,0:T(8,128)(2,1)}, bf16[128,256]{1,0:T(8,128)(2,1)S(1)}, u32[]{:S(2)}) copy-start(bf16[128,256]{1,0:T(8,128)(2,1)S(1)} %collective-permute-done.rest_1_) | copy-start | bytes 196612
  25.9 7.6 %collective-permute-start.3 = (bf16[128,256]{1,0:T(8,128)(2,1)}, bf16[128,256]{1,0:T(8,128)(2,1)S(1)}, u32[]{:S(2)}, u32[]{:S(2)}) collective-permute-start(bf16[128,256]{1,0:T(8,128)(2,1)} %get-tuple-element.20), channel_id=1, source_target_pairs={{0,4},{4,0},{8,12},{12,8},{16,20},{20,16},{24,28},{28,24},{1,5},{5... | collective-permute-start | bytes 196616 | tf_op jit(solution)/shard_map/ppermute | solution.py:256
  27.6 9.5 %collective-permute-start.4 = (bf16[128,256]{1,0:T(8,128)(2,1)}, bf16[128,256]{1,0:T(8,128)(2,1)S(1)}, u32[]{:S(2)}, u32[]{:S(2)}) collective-permute-start(bf16[128,256]{1,0:T(8,128)(2,1)} %get-tuple-element.21), channel_id=1, source_target_pairs={{0,8},{4,12},{8,0},{12,4},{16,24},{20,28},{24,16},{28,20},{1,9},{5... | collective-permute-start | bytes 196616 | tf_op jit(solution)/shard_map/ppermute | solution.py:256
  29.2 7.9 %collective-permute-start.5 = (bf16[128,256]{1,0:T(8,128)(2,1)}, bf16[128,256]{1,0:T(8,128)(2,1)S(1)}, u32[]{:S(2)}, u32[]{:S(2)}) collective-permute-start(bf16[128,256]{1,0:T(8,128)(2,1)} %get-tuple-element.22), channel_id=1, source_target_pairs={{0,12},{4,8},{8,4},{12,0},{16,28},{20,24},{24,20},{28,16},{1,13},{... | collective-permute-start | bytes 196616 | tf_op jit(solution)/shard_map/ppermute | solution.py:256
  29.4 7.8 %collective-permute-start.6 = (bf16[128,256]{1,0:T(8,128)(2,1)}, bf16[128,256]{1,0:T(8,128)(2,1)S(1)}, u32[]{:S(2)}, u32[]{:S(2)}) collective-permute-start(bf16[128,256]{1,0:T(8,128)(2,1)} %get-tuple-element.23), channel_id=1, source_target_pairs={{0,16},{4,20},{8,24},{12,28},{16,0},{20,4},{24,8},{28,12},{1,17},{... | collective-permute-start | bytes 196616 | tf_op jit(solution)/shard_map/ppermute | solution.py:256
  32.2 10.6 %collective-permute-start.7 = (bf16[128,256]{1,0:T(8,128)(2,1)}, bf16[128,256]{1,0:T(8,128)(2,1)S(1)}, u32[]{:S(2)}, u32[]{:S(2)}) collective-permute-start(bf16[128,256]{1,0:T(8,128)(2,1)} %get-tuple-element.24), channel_id=1, source_target_pairs={{0,20},{4,16},{8,28},{12,24},{16,4},{20,0},{24,12},{28,8},{1,21},{... | collective-permute-start | bytes 196616 | tf_op jit(solution)/shard_map/ppermute | solution.py:256
  33.5 9.3 %collective-permute-start.8 = (bf16[128,256]{1,0:T(8,128)(2,1)}, bf16[128,256]{1,0:T(8,128)(2,1)S(1)}, u32[]{:S(2)}, u32[]{:S(2)}) collective-permute-start(bf16[128,256]{1,0:T(8,128)(2,1)} %get-tuple-element.25), channel_id=1, source_target_pairs={{0,24},{4,28},{8,16},{12,20},{16,8},{20,12},{24,0},{28,4},{1,25},{... | collective-permute-start | bytes 196616 | tf_op jit(solution)/shard_map/ppermute | solution.py:256
  37.1 7.3 %collective-permute-start.9 = (bf16[128,256]{1,0:T(8,128)(2,1)}, bf16[128,256]{1,0:T(8,128)(2,1)S(1)}, u32[]{:S(2)}, u32[]{:S(2)}) collective-permute-start(bf16[128,256]{1,0:T(8,128)(2,1)} %get-tuple-element.26), channel_id=1, source_target_pairs={{0,28},{4,24},{8,20},{12,16},{16,12},{20,8},{24,4},{28,0},{1,29},{... | collective-permute-start | bytes 196616 | tf_op jit(solution)/shard_map/ppermute | solution.py:256

commit v4 on v3

--- a/solution.py
+++ b/solution.py
@@ -15,7 +15,6 @@
 
 def index_kernel(
     sizes,
-    own_ref,
     beta_target,
     beta_pair,
     beta_sign,
@@ -61,7 +60,7 @@
         weights_ref[b * batch * depth : (b + 1) * batch * depth, :] = u.astype(bf16)
 
     code = beta_target[...] * 256 + beta_pair[...] * 2 + beta_sign[...]
-    own = own_ref[0] * cols + lax.broadcasted_iota(jnp.int32, (2, cols), 1)
+    own = lax.axis_index("beta") * cols + lax.broadcasted_iota(jnp.int32, (2, cols), 1)
     extra = lax.broadcasted_iota(jnp.int32, (2, cols), 0) + pairs + 2
     extra = own * 256 + extra * 2 + 1
     blank = jnp.zeros((LANES - nexc - 2, cols), jnp.int32)
@@ -94,15 +93,33 @@
         alpha_ref[8 * w : 8 * w + 8, :] = found[w].astype(jnp.int32)
 
 
-def local_kernel(sizes, place_ref, beta_ref, alpha_ref, weights, *rest):
+def scatter(s, rows, nexc, alpha_ref, lifted):
+    base = (lax.axis_index("alpha") ^ s) * rows
+    total = jnp.zeros((rows, lifted.shape[1]), jnp.float32)
+    period = rows * nexc // LANES // 8
+    for t in range(8):
+        hots = []
+        for w in range(period):
+            target = alpha_ref[8 * w + t : 8 * w + t + 1, :] - base
+            b_ids = lax.broadcasted_iota(jnp.int32, (rows, LANES), 0)
+            hots.append(jnp.where(b_ids == target, 1.0, 0.0).astype(jnp.bfloat16))
+        total += jnp.dot(
+            jnp.concatenate(hots, axis=1),
+            lifted[period * t * LANES : period * (t + 1) * LANES, :],
+            preferred_element_type=jnp.float32,
+        )
+    return total
+
+
+def far_kernel(sizes, beta_ref, alpha_ref, weights, *rest):
     chunks, rows, cols, nexc, depth, blocks, stride = sizes
     c_refs, rest = rest[:chunks], rest[chunks:]
-    own_ref, out_refs, rest = rest[0], rest[1:blocks], rest[blocks:]
-    density, lifted, same, picked = rest
+    lifted, same = rest[:2]
+    out_refs, (density, picked) = rest[2:-2], rest[-2:]
     per_tile = LANES // GROUP
     bf16, f32 = jnp.bfloat16, jnp.float32
     groups = beta_ref.shape[0] // 2
-    my_alpha, my_beta = place_ref[0], place_ref[1]
+    my_beta = lax.axis_index("beta")
 
     def beta_code(g):
         return jnp.concatenate([beta_ref[pl.ds(2 * g, 1), :], beta_ref[pl.ds(2 * g + 1, 1), :]], axis=1)
@@ -159,25 +176,17 @@
 
     lax.fori_loop(0, rows // 2, alpha_step, 0, unroll=8)
 
-    for s in range(blocks):
-        base = (my_alpha ^ s) * rows
-        total = jnp.zeros((rows, cols), f32)
-        period = rows * nexc // LANES // 8
-        for t in range(8):
-            hots = []
-            for w in range(period):
-                target = alpha_ref[8 * w + t : 8 * w + t + 1, :] - base
-                b_ids = lax.broadcasted_iota(jnp.int32, (rows, LANES), 0)
-                hots.append(jnp.where(b_ids == target, 1.0, 0.0).astype(bf16))
-            total += jnp.dot(
-                jnp.concatenate(hots, axis=1),
-                lifted[period * t * LANES : period * (t + 1) * LANES, :],
-                preferred_element_type=f32,
-            )
-        if s == 0:
-            own_ref[...] = total + same[...]
-        else:
-            out_refs[s - 1][...] = total.astype(bf16)
+    for s in range(blocks // 2, blocks):
+        total = scatter(s, rows, nexc, alpha_ref, lifted)
+        out_refs[s - blocks // 2][...] = total.astype(bf16)
+
+
+def near_kernel(sizes, alpha_ref, lifted, same, own_ref, *out_refs):
+    rows, nexc, blocks = sizes
+    for s in range(1, blocks // 2):
+        total = scatter(s, rows, nexc, alpha_ref, lifted)
+        out_refs[s - 1][...] = total.astype(jnp.bfloat16)
+    own_ref[...] = scatter(0, rows, nexc, alpha_ref, lifted) + same[...]
 
 
 def shards(
@@ -196,7 +205,6 @@
     nexc = beta_target.shape[0]
     blocks = lax.axis_size("alpha")
     chunks = lax.axis_size("beta")
-    place = jnp.stack([lax.axis_index("alpha"), lax.axis_index("beta")])
     bf16 = jnp.bfloat16
 
     civec_bf = ci_vector.astype(bf16)
@@ -215,15 +223,17 @@
             jax.ShapeDtypeStruct((rows * nexc // LANES, LANES), jnp.int32),
             jax.ShapeDtypeStruct((rows * depth, LANES), bf16),
         ],
-        in_specs=[pl.BlockSpec(memory_space=pltpu.SMEM)] + [vmem] * 8,
+        in_specs=[vmem] * 8,
         out_specs=[vmem] * 3,
         scratch_shapes=[
             pltpu.VMEM((LANES, LANES), jnp.float32),
             pltpu.VMEM((tiles * GROUP, LANES), jnp.float32),
         ],
+        cost_estimate=pl.CostEstimate(
+            flops=4 * rows * depth * LANES * LANES, bytes_accessed=0, transcendentals=0
+        ),
         name="index_lists",
     )(
-        place[1:],
         beta_target,
         beta_pair,
         beta_sign,
@@ -236,24 +246,40 @@
 
     stride = rows + 8
     sizes = (chunks, rows, cols, nexc, depth, blocks, stride)
-    outs = pl.pallas_call(
-        functools.partial(local_kernel, sizes),
-        out_shape=[jax.ShapeDtypeStruct((rows, cols), jnp.float32)]
-        + [jax.ShapeDtypeStruct((rows, cols), bf16)] * (blocks - 1),
-        in_specs=[pl.BlockSpec(memory_space=pltpu.SMEM)] + [vmem] * (3 + chunks),
-        out_specs=[vmem] * blocks,
+    block = jax.ShapeDtypeStruct((rows, cols), bf16)
+    block_f32 = jax.ShapeDtypeStruct((rows, cols), jnp.float32)
+    lifted, same, *far = pl.pallas_call(
+        functools.partial(far_kernel, sizes),
+        out_shape=[jax.ShapeDtypeStruct((rows * nexc, cols), bf16), block_f32]
+        + [block] * (blocks // 2),
+        in_specs=[vmem] * (3 + chunks),
+        out_specs=[vmem] * (2 + blocks // 2),
         scratch_shapes=[
             pltpu.VMEM((tiles * GROUP * stride, LANES), jnp.float32),
-            pltpu.VMEM((rows * nexc, cols), bf16),
-            pltpu.VMEM((rows, cols), jnp.float32),
             pltpu.VMEM((tiles // 2, rows, 2 * LANES), bf16),
         ],
-        compiler_params=pltpu.CompilerParams(vmem_limit_bytes=56 * 1024 * 1024),
-        name="sigma_local",
-    )(place, beta_code, alpha_code, weights, *gathered)
-    total = outs[0]
-    for s in range(1, blocks):
-        got = lax.ppermute(outs[s], "alpha", [(d, d ^ s) for d in range(blocks)])
+        compiler_params=pltpu.CompilerParams(vmem_limit_bytes=36 * 1024 * 1024),
+        name="sigma_far",
+    )(beta_code, alpha_code, weights, *gathered)
+
+    def send(s, value):
+        return lax.ppermute(value, "alpha", [(d, d ^ s) for d in range(blocks)])
+
+    far_got = [send(blocks // 2 + s, far[s]) for s in range(blocks // 2)]
+    own, *near = pl.pallas_call(
+        functools.partial(near_kernel, (rows, nexc, blocks)),
+        out_shape=[block_f32] + [block] * (blocks // 2 - 1),
+        in_specs=[vmem] * 3,
+        out_specs=[vmem] * (blocks // 2),
+        compiler_params=pltpu.CompilerParams(vmem_limit_bytes=8 * 1024 * 1024),
+        cost_estimate=pl.CostEstimate(
+            flops=blocks * rows * rows * nexc * cols, bytes_accessed=0, transcendentals=0
+        ),
+        name="sigma_near",
+    )(alpha_code, lifted, same)
+    *near, far_got[0] = lax.optimization_barrier((*near, far_got[0]))
+    total = own
+    for got in [send(s + 1, near[s]) for s in range(blocks // 2 - 1)] + far_got:
         total = total + got.astype(jnp.float32)
     return total
 

time: 46.3 us -> 43.5 us (0.940)
  local copies, waits for them, and re-layouts: 0.65 us -> 2.92 us
  Pallas kernels: 20.5 us -> 18.4 us
  waiting for transfers between devices: 7.26 us -> 5.19 us
  other arithmetic: 3.19 us -> 1.63 us
  starting transfers between devices: 14.4 us -> 15 us
    ppermute x7, waiting for transfers between devices: 7.26 us -> 4.56 us  [send(): return lax.ppermute(value, 'alpha', [(d, d ^ s) for d in range(blocks)])]
    unnamed x8 -> x6, local copies, waits for them, and re-layouts: 0.65 us -> 2.92 us
    pallas_call x1 -> x2, Pallas kernels: 17.1 us -> 15.1 us  [the longest x1 13.3 us: shards(): pl.pallas_call(functools.partial(far_kernel, sizes), out_shape=[jax.Shape...]
    add x1, other arithmetic: 1.63 us -> 0.72 us  [shards(): total = total + got.astype(jnp.float32)]
    another operation x1 -> x0, other arithmetic: 0.65 us -> none  [shards(): place = jnp.stack([lax.axis_index('alpha'), lax.axis_index('beta')])]
    ppermute x7, starting transfers between devices: 11.2 us -> 11.9 us  [send(): return lax.ppermute(value, 'alpha', [(d, d ^ s) for d in range(blocks)])]
    ppermute x3, waiting for transfers between devices: 0.01 us -> 0.63 us  [shards(): lax.ppermute(civec_bf, 'beta', [(d, d ^ s) for d in range(chunks)])]
  transfers between devices with their start and end apart: 10 -> 10, of which waited for: 2 -> 5; matrix products, arithmetic and copies ran while one was open for 1% -> 0% of each run, Pallas kernels for 7% -> 12%
where the time goes in v4:
time: 43.5 us; the launch traced here: 43.2 us
  Pallas kernels  18.4 us (42%)
  starting transfers between devices  15 us (34%)
  waiting for transfers between devices  5.19 us (12%)
  local copies, waits for them, and re-layouts  2.92 us (7%)
  other arithmetic  1.63 us (4%)
    pallas_call x1, Pallas kernels, shards(): pl.pallas_call(functools.partial(far_kernel, sizes), out_shape=[jax.Shape...  13.3 us
    ppermute x7, starting transfers between devices, send(): return lax.ppermute(value, 'alpha', [(d, d ^ s) for d in range(blocks)])  11.9 us
    ppermute x7, waiting for transfers between devices, send(): return lax.ppermute(value, 'alpha', [(d, d ^ s) for d in range(blocks)])  4.56 us
    pallas_call x1, Pallas kernels, shards(): pl.pallas_call(functools.partial(index_kernel, (rows, cols, nexc, depth,...  3.37 us
    ppermute x3, starting transfers between devices, shards(): lax.ppermute(civec_bf, 'beta', [(d, d ^ s) for d in range(chunks)])  3.12 us
    unnamed x6, local copies, waits for them, and re-layouts  2.92 us
    pallas_call x1, Pallas kernels, shards(): pl.pallas_call(functools.partial(near_kernel, (rows, nexc, blocks)), out_...  1.79 us
    convert_element_type x1, other arithmetic, shards(): civec_bf = ci_vector.astype(bf16)  0.91 us
  transfers between devices with their start and end apart: 10, of which 5 were waited for; matrix products, arithmetic and copies ran while one was open for 0% of the time, Pallas kernels for 12%

profile of v4, /device:TPU:0, one launch (start us, length us, event | category | flops | bytes accessed | tf_op | source)
XLA Modules:
  0.0 43.2 jit_solution(15940347737762375003)
XLA Ops:
  0.0 0.9 %convert_element_type.24.rest_0_ = bf16[128,256]{1,0:T(8,128)(2,1)S(1)} convert(f32[128,256]{1,0:T(8,128)} %param.9) | non-fusion elementwise | flops 32768 | bytes 196608 | tf_op jit(solution)/shard_map/convert_element_type | solution.py:210
  0.9 2.4 %collective-permute-start.2 = (bf16[128,256]{1,0:T(8,128)(2,1)S(1)}, bf16[128,256]{1,0:T(8,128)(2,1)S(1)}, u32[]{:S(2)}, u32[]{:S(2)}) collective-permute-start(bf16[128,256]{1,0:T(8,128)(2,1)S(1)} %convert_element_type.24.rest_0_), channel_id=1, source_target_pairs={{0,3},{1,2},{2,1},{3,0},{4,7},{5,6},{6,5},{7,4},{8,11},{9,10},{10,... | collective-permute-start | bytes 196616 | tf_op jit(solution)/shard_map/ppermute | solution.py:212
  3.4 0.6 %collective-permute-start.1 = (bf16[128,256]{1,0:T(8,128)(2,1)S(1)}, bf16[128,256]{1,0:T(8,128)(2,1)S(1)}, u32[]{:S(2)}, u32[]{:S(2)}) collective-permute-start(bf16[128,256]{1,0:T(8,128)(2,1)S(1)} %convert_element_type.24.rest_0_), channel_id=1, source_target_pairs={{0,2},{1,3},{2,0},{3,1},{4,6},{5,7},{6,4},{7,5},{8,10},{9,11},{10,... | collective-permute-start | bytes 196616 | tf_op jit(solution)/shard_map/ppermute | solution.py:212
  4.0 0.0 collective-permute-start
  4.0 3.4 %index_lists.1 = (s32[88,128]{1,0:T(8,128)}, s32[40,128]{1,0:T(8,128)}, bf16[6144,128]{1,0:T(8,128)(2,1)}) custom-call(s32[40,256]{1,0:T(8,128)} %beta_target.1, s32[40,256]{1,0:T(8,128)} %beta_pair.1, s32[40,256]{1,0:T(8,128)} %beta_sign.1, s32[40,128]{1,0:T(8,128)} %alpha_target.1, s32[40,128]{1,0:T(8,128)} %alpha_pair.1, s32[40,128]{1,0:T(8,128)} %alpha_sign.1, ...), custom_call_target="tpu_custom_call" | custom-call | flops 402653184 | tf_op jit(solution)/shard_map/index_lists/pallas_call | solution.py:219
  7.4 0.0 collective-permute-done.2.rest_3_
  7.4 0.6 %collective-permute-done.1.rest_2_ = bf16[128,256]{1,0:T(8,128)(2,1)S(1)} collective-permute-done((bf16[128,256]{1,0:T(8,128)(2,1)S(1)}, bf16[128,256]{1,0:T(8,128)(2,1)S(1)}, u32[]{:S(2)}, u32[]{:S(2)}) %collective-permute-start.1) | collective-permute-done | bytes 65568 | tf_op jit(solution)/shard_map/ppermute | solution.py:212
  8.0 0.0 collective-permute-done.rest_1_
  8.0 0.0 copy-start
  8.0 1.4 %copy-done = bf16[6144,128]{1,0:T(8,128)(2,1)S(1)} copy-done((bf16[6144,128]{1,0:T(8,128)(2,1)S(1)}, bf16[6144,128]{1,0:T(8,128)(2,1)}, u32[]{:S(2)}) %copy-start) | copy-done | bytes 1572888
  9.4 0.0 copy-start.1
  9.4 0.8 %copy-done.1 = s32[88,128]{1,0:T(8,128)S(1)} copy-done((s32[88,128]{1,0:T(8,128)S(1)}, s32[88,128]{1,0:T(8,128)}, u32[]{:S(2)}) %copy-start.1) | copy-done | bytes 45080
  10.2 0.0 copy-start.2
  10.2 0.7 %copy-done.2 = s32[40,128]{1,0:T(8,128)S(1)} copy-done((s32[40,128]{1,0:T(8,128)S(1)}, s32[40,128]{1,0:T(8,128)}, u32[]{:S(2)}) %copy-start.2) | copy-done | bytes 20504
  11.0 13.3 %sigma_far.1 = (bf16[5120,256]{1,0:T(8,128)(2,1)S(1)}, f32[128,256]{1,0:T(8,128)S(1)}, bf16[128,256]{1,0:T(8,128)(2,1)S(1)}, bf16[128,256]{1,0:T(8,128)(2,1)S(1)...) custom-call(s32[88,128]{1,0:T(8,128)S(1)} %copy-done.1, s32[40,128]{1,0:T(8,128)S(1)} %copy-done.2, ...), custom_call_target="tpu_custom_call" | custom-call | tf_op jit(solution)/shard_map/sigma_far/pallas_call | solution.py:251
  24.2 2.8 %collective-permute-start.3 = (bf16[128,256]{1,0:T(8,128)(2,1)S(1)}, bf16[128,256]{1,0:T(8,128)(2,1)S(1)}, u32[]{:S(2)}, u32[]{:S(2)}) collective-permute-start(bf16[128,256]{1,0:T(8,128)(2,1)S(1)} %get-tuple-element.31), channel_id=1, source_target_pairs={{0,16},{4,20},{8,24},{12,28},{16,0},{20,4},{24,8},{28,12},{1,17},{... | collective-permute-start | bytes 196616 | tf_op jit(solution)/shard_map/ppermute | solution.py:266
  27.1 1.3 %collective-permute-start.7 = (bf16[128,256]{1,0:T(8,128)(2,1)S(1)}, bf16[128,256]{1,0:T(8,128)(2,1)S(1)}, u32[]{:S(2)}, u32[]{:S(2)}) collective-permute-start(bf16[128,256]{1,0:T(8,128)(2,1)S(1)} %get-tuple-element.36), channel_id=1, source_target_pairs={{0,20},{4,16},{8,28},{12,24},{16,4},{20,0},{24,12},{28,8},{1,21},{... | collective-permute-start | bytes 196616 | tf_op jit(solution)/shard_map/ppermute | solution.py:266
  28.4 3.6 %collective-permute-start.8 = (bf16[128,256]{1,0:T(8,128)(2,1)S(1)}, bf16[128,256]{1,0:T(8,128)(2,1)S(1)}, u32[]{:S(2)}, u32[]{:S(2)}) collective-permute-start(bf16[128,256]{1,0:T(8,128)(2,1)S(1)} %get-tuple-element.37), channel_id=1, source_target_pairs={{0,24},{4,28},{8,16},{12,20},{16,8},{20,12},{24,0},{28,4},{1,25},{... | collective-permute-start | bytes 196616 | tf_op jit(solution)/shard_map/ppermute | solution.py:266
  32.0 0.0 collective-permute-start.9
  32.0 1.8 %sigma_near.1 = (f32[128,256]{1,0:T(8,128)S(1)}, bf16[128,256]{1,0:T(8,128)(2,1)S(1)}, bf16[128,256]{1,0:T(8,128)(2,1)S(1)}, bf16[128,256]{1,0:T(8,128)(2,1)S(1)}) custom-call(s32[40,128]{1,0:T(8,128)S(1)} %copy-done.2, bf16[5120,256]{1,0:T(8,128)(2,1)S(1)} %get-tuple-element.25.lifted, f32[128,256]{1,0:T(8,128)S(1)} %get-tuple-element.26.same), custom_call_target="tpu_custom_call" | custom-call | flops 1342177280 | tf_op jit(solution)/shard_map/sigma_near/pallas_call | solution.py:269
  33.8 0.0 collective-permute-done.3
  33.8 2.0 %collective-permute-start.4 = (bf16[128,256]{1,0:T(8,128)(2,1)S(1)}, bf16[128,256]{1,0:T(8,128)(2,1)S(1)}, u32[]{:S(2)}, u32[]{:S(2)}) collective-permute-start(bf16[128,256]{1,0:T(8,128)(2,1)S(1)} %get-tuple-element.32), channel_id=1, source_target_pairs={{0,4},{4,0},{8,12},{12,8},{16,20},{20,16},{24,28},{28,24},{1,5},{5... | collective-permute-start | bytes 196616 | tf_op jit(solution)/shard_map/ppermute | solution.py:266
  35.8 1.4 %collective-permute-start.5 = (bf16[128,256]{1,0:T(8,128)(2,1)S(1)}, bf16[128,256]{1,0:T(8,128)(2,1)S(1)}, u32[]{:S(2)}, u32[]{:S(2)}) collective-permute-start(bf16[128,256]{1,0:T(8,128)(2,1)S(1)} %get-tuple-element.33), channel_id=1, source_target_pairs={{0,8},{4,12},{8,0},{12,4},{16,24},{20,28},{24,16},{28,20},{1,9},{5... | collective-permute-start | bytes 196616 | tf_op jit(solution)/shard_map/ppermute | solution.py:266
  37.2 0.1 collective-permute-done.7
  37.3 0.8 %collective-permute-start.6 = (bf16[128,256]{1,0:T(8,128)(2,1)S(1)}, bf16[128,256]{1,0:T(8,128)(2,1)S(1)}, u32[]{:S(2)}, u32[]{:S(2)}) collective-permute-start(bf16[128,256]{1,0:T(8,128)(2,1)S(1)} %get-tuple-element.34), channel_id=1, source_target_pairs={{0,12},{4,8},{8,4},{12,0},{16,28},{20,24},{24,20},{28,16},{1,13},{... | collective-permute-start | bytes 196616 | tf_op jit(solution)/shard_map/ppermute | solution.py:266
  38.1 0.0 collective-permute-done.8
  38.1 1.0 %collective-permute-done.9 = bf16[128,256]{1,0:T(8,128)(2,1)S(1)} collective-permute-done((bf16[128,256]{1,0:T(8,128)(2,1)S(1)}, bf16[128,256]{1,0:T(8,128)(2,1)S(1)}, u32[]{:S(2)}, u32[]{:S(2)}) %collective-permute-start.9) | collective-permute-done | bytes 65568 | tf_op jit(solution)/shard_map/ppermute | solution.py:266
  39.0 0.0 collective-permute-done.4
  39.1 1.0 %collective-permute-done.5 = bf16[128,256]{1,0:T(8,128)(2,1)S(1)} collective-permute-done((bf16[128,256]{1,0:T(8,128)(2,1)S(1)}, bf16[128,256]{1,0:T(8,128)(2,1)S(1)}, u32[]{:S(2)}, u32[]{:S(2)}) %collective-permute-start.5) | collective-permute-done | bytes 65568 | tf_op jit(solution)/shard_map/ppermute | solution.py:266
  40.0 2.5 %collective-permute-done.6 = bf16[128,256]{1,0:T(8,128)(2,1)S(1)} collective-permute-done((bf16[128,256]{1,0:T(8,128)(2,1)S(1)}, bf16[128,256]{1,0:T(8,128)(2,1)S(1)}, u32[]{:S(2)}, u32[]{:S(2)}) %collective-permute-start.6) | collective-permute-done | bytes 65568 | tf_op jit(solution)/shard_map/ppermute | solution.py:266
  42.5 0.7 %convert_add_fusion = f32[128,256]{1,0:T(8,128)} fusion(bf16[128,256]{1,0:T(8,128)(2,1)S(1)} %collective-permute-done.9, bf16[128,256]{1,0:T(8,128)(2,1)S(1)} %collective-permute-done.8, bf16[128,256]{1,0:T(8,128)(2,1)S(1)} %collective-permute-done.7, bf16[128,256]{1,0:T(8,128)(2,1)S(1)} %collective-permute-done.3, ...), kind=kLoop, calls=%fused_computation | loop fusion | flops 458752 | bytes 720896 | tf_op jit(solution)/shard_map/add | solution.py:283
Async XLA Ops:
  0.9 6.5 %collective-permute-start.2 = (bf16[128,256]{1,0:T(8,128)(2,1)S(1)}, bf16[128,256]{1,0:T(8,128)(2,1)S(1)}, u32[]{:S(2)}, u32[]{:S(2)}) collective-permute-start(bf16[128,256]{1,0:T(8,128)(2,1)S(1)} %convert_element_type.24.rest_0_), channel_id=1, source_target_pairs={{0,3},{1,2},{2,1},{3,0},{4,7},{5,6},{6,5},{7,4},{8,11},{9,10},{10,... | collective-permute-start | bytes 196616 | tf_op jit(solution)/shard_map/ppermute | solution.py:212
  3.4 4.7 %collective-permute-start.1 = (bf16[128,256]{1,0:T(8,128)(2,1)S(1)}, bf16[128,256]{1,0:T(8,128)(2,1)S(1)}, u32[]{:S(2)}, u32[]{:S(2)}) collective-permute-start(bf16[128,256]{1,0:T(8,128)(2,1)S(1)} %convert_element_type.24.rest_0_), channel_id=1, source_target_pairs={{0,2},{1,3},{2,0},{3,1},{4,6},{5,7},{6,4},{7,5},{8,10},{9,11},{10,... | collective-permute-start | bytes 196616 | tf_op jit(solution)/shard_map/ppermute | solution.py:212
  4.0 4.0 %collective-permute-start = (bf16[128,256]{1,0:T(8,128)(2,1)S(1)}, bf16[128,256]{1,0:T(8,128)(2,1)S(1)}, u32[]{:S(2)}, u32[]{:S(2)}) collective-permute-start(bf16[128,256]{1,0:T(8,128)(2,1)S(1)} %convert_element_type.24.rest_0_), channel_id=1, source_target_pairs={{0,1},{1,0},{2,3},{3,2},{4,5},{5,4},{6,7},{7,6},{8,9},{9,8},{10,11... | collective-permute-start | bytes 196616 | tf_op jit(solution)/shard_map/ppermute | solution.py:212
  8.0 1.4 %copy-start = (bf16[6144,128]{1,0:T(8,128)(2,1)S(1)}, bf16[6144,128]{1,0:T(8,128)(2,1)}, u32[]{:S(2)}) copy-start(bf16[6144,128]{1,0:T(8,128)(2,1)} %get-tuple-element.24.weights) | copy-start | bytes 4718596
  9.4 0.8 %copy-start.1 = (s32[88,128]{1,0:T(8,128)S(1)}, s32[88,128]{1,0:T(8,128)}, u32[]{:S(2)}) copy-start(s32[88,128]{1,0:T(8,128)} %get-tuple-element.23.beta_ref) | copy-start | bytes 135172
  10.2 0.7 %copy-start.2 = (s32[40,128]{1,0:T(8,128)S(1)}, s32[40,128]{1,0:T(8,128)}, u32[]{:S(2)}) copy-start(s32[40,128]{1,0:T(8,128)} %get-tuple-element.22.alpha_ref) | copy-start | bytes 61444
  24.2 9.5 %collective-permute-start.3 = (bf16[128,256]{1,0:T(8,128)(2,1)S(1)}, bf16[128,256]{1,0:T(8,128)(2,1)S(1)}, u32[]{:S(2)}, u32[]{:S(2)}) collective-permute-start(bf16[128,256]{1,0:T(8,128)(2,1)S(1)} %get-tuple-element.31), channel_id=1, source_target_pairs={{0,16},{4,20},{8,24},{12,28},{16,0},{20,4},{24,8},{28,12},{1,17},{... | collective-permute-start | bytes 196616 | tf_op jit(solution)/shard_map/ppermute | solution.py:266
  27.1 10.2 %collective-permute-start.7 = (bf16[128,256]{1,0:T(8,128)(2,1)S(1)}, bf16[128,256]{1,0:T(8,128)(2,1)S(1)}, u32[]{:S(2)}, u32[]{:S(2)}) collective-permute-start(bf16[128,256]{1,0:T(8,128)(2,1)S(1)} %get-tuple-element.36), channel_id=1, source_target_pairs={{0,20},{4,16},{8,28},{12,24},{16,4},{20,0},{24,12},{28,8},{1,21},{... | collective-permute-start | bytes 196616 | tf_op jit(solution)/shard_map/ppermute | solution.py:266
  28.4 9.7 %collective-permute-start.8 = (bf16[128,256]{1,0:T(8,128)(2,1)S(1)}, bf16[128,256]{1,0:T(8,128)(2,1)S(1)}, u32[]{:S(2)}, u32[]{:S(2)}) collective-permute-start(bf16[128,256]{1,0:T(8,128)(2,1)S(1)} %get-tuple-element.37), channel_id=1, source_target_pairs={{0,24},{4,28},{8,16},{12,20},{16,8},{20,12},{24,0},{28,4},{1,25},{... | collective-permute-start | bytes 196616 | tf_op jit(solution)/shard_map/ppermute | solution.py:266
  32.0 7.1 %collective-permute-start.9 = (bf16[128,256]{1,0:T(8,128)(2,1)S(1)}, bf16[128,256]{1,0:T(8,128)(2,1)S(1)}, u32[]{:S(2)}, u32[]{:S(2)}) collective-permute-start(bf16[128,256]{1,0:T(8,128)(2,1)S(1)} %get-tuple-element.38), channel_id=1, source_target_pairs={{0,28},{4,24},{8,20},{12,16},{16,12},{20,8},{24,4},{28,0},{1,29},{... | collective-permute-start | bytes 196616 | tf_op jit(solution)/shard_map/ppermute | solution.py:266
  33.8 5.3 %collective-permute-start.4 = (bf16[128,256]{1,0:T(8,128)(2,1)S(1)}, bf16[128,256]{1,0:T(8,128)(2,1)S(1)}, u32[]{:S(2)}, u32[]{:S(2)}) collective-permute-start(bf16[128,256]{1,0:T(8,128)(2,1)S(1)} %get-tuple-element.32), channel_id=1, source_target_pairs={{0,4},{4,0},{8,12},{12,8},{16,20},{20,16},{24,28},{28,24},{1,5},{5... | collective-permute-start | bytes 196616 | tf_op jit(solution)/shard_map/ppermute | solution.py:266
  35.8 4.3 %collective-permute-start.5 = (bf16[128,256]{1,0:T(8,128)(2,1)S(1)}, bf16[128,256]{1,0:T(8,128)(2,1)S(1)}, u32[]{:S(2)}, u32[]{:S(2)}) collective-permute-start(bf16[128,256]{1,0:T(8,128)(2,1)S(1)} %get-tuple-element.33), channel_id=1, source_target_pairs={{0,8},{4,12},{8,0},{12,4},{16,24},{20,28},{24,16},{28,20},{1,9},{5... | collective-permute-start | bytes 196616 | tf_op jit(solution)/shard_map/ppermute | solution.py:266
  37.3 5.2 %collective-permute-start.6 = (bf16[128,256]{1,0:T(8,128)(2,1)S(1)}, bf16[128,256]{1,0:T(8,128)(2,1)S(1)}, u32[]{:S(2)}, u32[]{:S(2)}) collective-permute-start(bf16[128,256]{1,0:T(8,128)(2,1)S(1)} %get-tuple-element.34), channel_id=1, source_target_pairs={{0,12},{4,8},{8,4},{12,0},{16,28},{20,24},{24,20},{28,16},{1,13},{... | collective-permute-start | bytes 196616 | tf_op jit(solution)/shard_map/ppermute | solution.py:266

commit v5 on v4

--- a/solution.py
+++ b/solution.py
@@ -13,23 +13,20 @@
 NT = (((1,), (1,)), ((), ()))
 
 
-def index_kernel(
-    sizes,
-    beta_target,
-    beta_pair,
-    beta_sign,
-    alpha_target,
-    alpha_pair,
-    alpha_sign,
-    one_body,
-    integrals,
-    beta_ref,
-    alpha_ref,
-    weights_ref,
-    table,
-    turned,
-):
+def index_kernel(sizes, *refs):
     rows, cols, nexc, depth, tiles, pairs = sizes
+    sources, (beta_ref, alpha_ref, weights_ref) = refs[:8], refs[8:11]
+    staged, (table, turned, arrived) = refs[11:19], refs[19:]
+    copies = [
+        pltpu.make_async_copy(source, target, arrived.at[n])
+        for n, (source, target) in enumerate(zip(sources, staged))
+    ]
+    for copy in copies:
+        copy.start()
+    for copy in copies:
+        copy.wait()
+    beta_target, beta_pair, beta_sign, alpha_target, alpha_pair, alpha_sign = staged[:6]
+    one_body, integrals = staged[6:]
     bf16, f32 = jnp.bfloat16, jnp.float32
     per_tile = LANES // GROUP
     lane = lax.broadcasted_iota(jnp.int32, (8, LANES), 1)
@@ -216,24 +213,7 @@
     depth = nexc + 8
     tiles = -(-cols // (2 * GROUP * UNROLL)) * 2 * UNROLL
     vmem = pl.BlockSpec(memory_space=pltpu.VMEM)
-    beta_code, alpha_code, weights = pl.pallas_call(
-        functools.partial(index_kernel, (rows, cols, nexc, depth, tiles, pairs)),
-        out_shape=[
-            jax.ShapeDtypeStruct((tiles, LANES), jnp.int32),
-            jax.ShapeDtypeStruct((rows * nexc // LANES, LANES), jnp.int32),
-            jax.ShapeDtypeStruct((rows * depth, LANES), bf16),
-        ],
-        in_specs=[vmem] * 8,
-        out_specs=[vmem] * 3,
-        scratch_shapes=[
-            pltpu.VMEM((LANES, LANES), jnp.float32),
-            pltpu.VMEM((tiles * GROUP, LANES), jnp.float32),
-        ],
-        cost_estimate=pl.CostEstimate(
-            flops=4 * rows * depth * LANES * LANES, bytes_accessed=0, transcendentals=0
-        ),
-        name="index_lists",
-    )(
+    lists = (
         beta_target,
         beta_pair,
         beta_sign,
@@ -243,6 +223,27 @@
         one_body.reshape(1, pairs),
         pair_integrals,
     )
+    beta_code, alpha_code, weights = pl.pallas_call(
+        functools.partial(index_kernel, (rows, cols, nexc, depth, tiles, pairs)),
+        out_shape=[
+            pltpu.VMEM((tiles, LANES), jnp.int32),
+            pltpu.VMEM((rows * nexc // LANES, LANES), jnp.int32),
+            pltpu.VMEM((rows * depth, LANES), bf16),
+        ],
+        in_specs=[pl.BlockSpec(memory_space=pltpu.HBM)] * 8,
+        out_specs=[vmem] * 3,
+        scratch_shapes=[pltpu.VMEM(x.shape, x.dtype) for x in lists]
+        + [
+            pltpu.VMEM((LANES, LANES), jnp.float32),
+            pltpu.VMEM((tiles * GROUP, LANES), jnp.float32),
+            pltpu.SemaphoreType.DMA((len(lists),)),
+        ],
+        cost_estimate=pl.CostEstimate(
+            flops=4 * rows * depth * LANES * LANES, bytes_accessed=0, transcendentals=0
+        ),
+        compiler_params=pltpu.CompilerParams(vmem_limit_bytes=16 * 1024 * 1024),
+        name="index_lists",
+    )(*[pltpu.with_memory_space_constraint(x, pltpu.HBM) for x in lists])
 
     stride = rows + 8
     sizes = (chunks, rows, cols, nexc, depth, blocks, stride)
@@ -265,7 +266,10 @@
     def send(s, value):
         return lax.ppermute(value, "alpha", [(d, d ^ s) for d in range(blocks)])
 
-    far_got = [send(blocks // 2 + s, far[s]) for s in range(blocks // 2)]
+    far_sum = far[0].astype(jnp.float32)
+    for s in range(1, blocks // 2):
+        far_sum = far_sum + send(s, far[s]).astype(jnp.float32)
+    far_sum = far_sum.astype(bf16)
     own, *near = pl.pallas_call(
         functools.partial(near_kernel, (rows, nexc, blocks)),
         out_shape=[block_f32] + [block] * (blocks // 2 - 1),
@@ -277,9 +281,9 @@
         ),
         name="sigma_near",
     )(alpha_code, lifted, same)
-    *near, far_got[0] = lax.optimization_barrier((*near, far_got[0]))
+    crossing = send(blocks // 2, far_sum)
     total = own
-    for got in [send(s + 1, near[s]) for s in range(blocks // 2 - 1)] + far_got:
+    for got in [send(s + 1, near[s]) for s in range(blocks // 2 - 1)] + [crossing]:
         total = total + got.astype(jnp.float32)
     return total
 

time: 43.5 us -> 36.5 us (0.84)
  local copies, waits for them, and re-layouts: 2.92 us -> 0 us
  starting transfers between devices: 15 us -> 13.1 us
  Pallas kernels: 18.4 us -> 17.3 us
  waiting for transfers between devices: 5.19 us -> 4.21 us
    unnamed x6 -> x0, local copies, waits for them, and re-layouts: 2.92 us -> none
    ppermute x7, waiting for transfers between devices: 4.56 us -> 2.51 us  [send(): return lax.ppermute(value, 'alpha', [(d, d ^ s) for d in range(blocks)])]
    ppermute x7, starting transfers between devices: 11.9 us -> 9.96 us  [send(): return lax.ppermute(value, 'alpha', [(d, d ^ s) for d in range(blocks)])]
    pallas_call x1, Pallas kernels: 3.37 us -> 2.28 us  [shards(): pl.pallas_call(functools.partial(index_kernel, (rows, cols, nexc, depth,...]
    ppermute x3, waiting for transfers between devices: 0.63 us -> 1.7 us  [shards(): lax.ppermute(civec_bf, 'beta', [(d, d ^ s) for d in range(chunks)])]
  transfers between devices with their start and end apart: 10 -> 10, of which waited for: 5 -> 4; matrix products, arithmetic and copies ran while one was open for 0% -> 0% of each run, Pallas kernels for 12% -> 11%
where the time goes in v5:
time: 36.5 us; the launch traced here: 36.3 us
  Pallas kernels  17.3 us (47%)
  starting transfers between devices  13.1 us (36%)
  waiting for transfers between devices  4.21 us (12%)
  other arithmetic  1.64 us (4%)
    pallas_call x1, Pallas kernels, shards(): pl.pallas_call(functools.partial(far_kernel, sizes), out_shape=[jax.Shape...  13.3 us
    ppermute x7, starting transfers between devices, send(): return lax.ppermute(value, 'alpha', [(d, d ^ s) for d in range(blocks)])  9.96 us
    ppermute x3, starting transfers between devices, shards(): lax.ppermute(civec_bf, 'beta', [(d, d ^ s) for d in range(chunks)])  3.12 us
    ppermute x7, waiting for transfers between devices, send(): return lax.ppermute(value, 'alpha', [(d, d ^ s) for d in range(blocks)])  2.51 us
    pallas_call x1, Pallas kernels, shards(): pl.pallas_call(functools.partial(index_kernel, (rows, cols, nexc, depth,...  2.28 us
    pallas_call x1, Pallas kernels, shards(): pl.pallas_call(functools.partial(near_kernel, (rows, nexc, blocks)), out_...  1.79 us
    ppermute x3, waiting for transfers between devices, shards(): lax.ppermute(civec_bf, 'beta', [(d, d ^ s) for d in range(chunks)])  1.7 us
    convert_element_type x1, other arithmetic, shards(): civec_bf = ci_vector.astype(bf16)  0.91 us
  transfers between devices with their start and end apart: 10, of which 4 were waited for; matrix products, arithmetic and copies ran while one was open for 0% of the time, Pallas kernels for 11%

profile of v5, /device:TPU:0, one launch (start us, length us, event | category | flops | bytes accessed | tf_op | source)
XLA Modules:
  0.0 36.3 jit_solution(15208245096054629755)
XLA Ops:
  0.0 0.9 %convert_element_type.30.rest_0_ = bf16[128,256]{1,0:T(8,128)(2,1)S(1)} convert(f32[128,256]{1,0:T(8,128)} %param.9) | non-fusion elementwise | flops 32768 | bytes 196608 | tf_op jit(solution)/shard_map/convert_element_type | solution.py:207
  0.9 2.4 %collective-permute-start.2 = (bf16[128,256]{1,0:T(8,128)(2,1)S(1)}, bf16[128,256]{1,0:T(8,128)(2,1)S(1)}, u32[]{:S(2)}, u32[]{:S(2)}) collective-permute-start(bf16[128,256]{1,0:T(8,128)(2,1)S(1)} %convert_element_type.30.rest_0_), channel_id=1, source_target_pairs={{0,3},{1,2},{2,1},{3,0},{4,7},{5,6},{6,5},{7,4},{8,11},{9,10},{10,... | collective-permute-start | bytes 196616 | tf_op jit(solution)/shard_map/ppermute | solution.py:209
  3.4 0.6 %collective-permute-start.1 = (bf16[128,256]{1,0:T(8,128)(2,1)S(1)}, bf16[128,256]{1,0:T(8,128)(2,1)S(1)}, u32[]{:S(2)}, u32[]{:S(2)}) collective-permute-start(bf16[128,256]{1,0:T(8,128)(2,1)S(1)} %convert_element_type.30.rest_0_), channel_id=1, source_target_pairs={{0,2},{1,3},{2,0},{3,1},{4,6},{5,7},{6,4},{7,5},{8,10},{9,11},{10,... | collective-permute-start | bytes 196616 | tf_op jit(solution)/shard_map/ppermute | solution.py:209
  4.0 0.0 collective-permute-start
  4.0 2.3 %index_lists.1 = (s32[88,128]{1,0:T(8,128)S(1)}, s32[40,128]{1,0:T(8,128)S(1)}, bf16[6144,128]{1,0:T(8,128)(2,1)S(1)}) custom-call(s32[40,256]{1,0:T(8,128)} %refs_0_.1, s32[40,256]{1,0:T(8,128)} %refs_1_.1, s32[40,256]{1,0:T(8,128)} %refs_2_.1, s32[40,128]{1,0:T(8,128)} %refs_3_.1, s32[40,128]{1,0:T(8,128)} %refs_4_.1, s32[40,128]{1,0:T(8,128)} %refs_5_.1, ...), custom_call_target="tpu_custom_call" | custom-call | flops 402653184 | tf_op jit(solution)/shard_map/index_lists/pallas_call | solution.py:226
  6.3 0.0 collective-permute-done.2.rest_3_
  6.3 1.7 %collective-permute-done.1.rest_2_ = bf16[128,256]{1,0:T(8,128)(2,1)S(1)} collective-permute-done((bf16[128,256]{1,0:T(8,128)(2,1)S(1)}, bf16[128,256]{1,0:T(8,128)(2,1)S(1)}, u32[]{:S(2)}, u32[]{:S(2)}) %collective-permute-start.1) | collective-permute-done | bytes 65568 | tf_op jit(solution)/shard_map/ppermute | solution.py:209
  8.0 0.0 collective-permute-done.rest_1_
  8.0 13.3 %sigma_far.1 = (bf16[5120,256]{1,0:T(8,128)(2,1)S(1)}, f32[128,256]{1,0:T(8,128)S(1)}, bf16[128,256]{1,0:T(8,128)(2,1)S(1)}, bf16[128,256]{1,0:T(8,128)(2,1)S(1)...) custom-call(s32[88,128]{1,0:T(8,128)S(1)} %get-tuple-element.19.beta_ref, ...), custom_call_target="tpu_custom_call" | custom-call | tf_op jit(solution)/shard_map/sigma_far/pallas_call | solution.py:252
  21.3 1.8 %collective-permute-start.6 = (bf16[128,256]{1,0:T(8,128)(2,1)S(1)}, bf16[128,256]{1,0:T(8,128)(2,1)S(1)}, u32[]{:S(2)}, u32[]{:S(2)}) collective-permute-start(bf16[128,256]{1,0:T(8,128)(2,1)S(1)} %get-tuple-element.28), channel_id=1, source_target_pairs={{0,4},{4,0},{8,12},{12,8},{16,20},{20,16},{24,28},{28,24},{1,5},{5... | collective-permute-start | bytes 196616 | tf_op jit(solution)/shard_map/ppermute | solution.py:267
  23.1 1.6 %collective-permute-start.7 = (bf16[128,256]{1,0:T(8,128)(2,1)S(1)}, bf16[128,256]{1,0:T(8,128)(2,1)S(1)}, u32[]{:S(2)}, u32[]{:S(2)}) collective-permute-start(bf16[128,256]{1,0:T(8,128)(2,1)S(1)} %get-tuple-element.29), channel_id=1, source_target_pairs={{0,8},{4,12},{8,0},{12,4},{16,24},{20,28},{24,16},{28,20},{1,9},{5... | collective-permute-start | bytes 196616 | tf_op jit(solution)/shard_map/ppermute | solution.py:267
  24.7 0.2 collective-permute-start.8
  24.9 1.8 %sigma_near.1 = (f32[128,256]{1,0:T(8,128)S(1)}, bf16[128,256]{1,0:T(8,128)(2,1)S(1)}, bf16[128,256]{1,0:T(8,128)(2,1)S(1)}, bf16[128,256]{1,0:T(8,128)(2,1)S(1)}) custom-call(s32[40,128]{1,0:T(8,128)S(1)} %get-tuple-element.18.alpha_ref, bf16[5120,256]{1,0:T(8,128)(2,1)S(1)} %get-tuple-element.21.lifted, f32[128,256]{1,0:T(8,128)S(1)} %get-tuple-element.22.same), custom_call_target="tpu_custom_call" | custom-call | flops 1342177280 | tf_op jit(solution)/shard_map/sigma_near/pallas_call | solution.py:273
  26.7 1.8 %collective-permute-start.3 = (bf16[128,256]{1,0:T(8,128)(2,1)S(1)}, bf16[128,256]{1,0:T(8,128)(2,1)S(1)}, u32[]{:S(2)}, u32[]{:S(2)}) collective-permute-start(bf16[128,256]{1,0:T(8,128)(2,1)S(1)} %get-tuple-element.24), channel_id=1, source_target_pairs={{0,4},{4,0},{8,12},{12,8},{16,20},{20,16},{24,28},{28,24},{1,5},{5... | collective-permute-start | bytes 196616 | tf_op jit(solution)/shard_map/ppermute | solution.py:267
  28.4 1.6 %collective-permute-start.4 = (bf16[128,256]{1,0:T(8,128)(2,1)S(1)}, bf16[128,256]{1,0:T(8,128)(2,1)S(1)}, u32[]{:S(2)}, u32[]{:S(2)}) collective-permute-start(bf16[128,256]{1,0:T(8,128)(2,1)S(1)} %get-tuple-element.25), channel_id=1, source_target_pairs={{0,8},{4,12},{8,0},{12,4},{16,24},{20,28},{24,16},{28,20},{1,9},{5... | collective-permute-start | bytes 196616 | tf_op jit(solution)/shard_map/ppermute | solution.py:267
  30.0 0.0 collective-permute-done.6
  30.0 0.2 collective-permute-start.5
  30.2 0.0 collective-permute-done.7
  30.2 0.0 collective-permute-done.8
  30.3 2.9 %collective-permute-start.9 = (bf16[128,256]{1,0:T(8,128)(2,1)S(1)}, bf16[128,256]{1,0:T(8,128)(2,1)S(1)}, u32[]{:S(2)}, u32[]{:S(2)}) collective-permute-start(bf16[128,256]{1,0:T(8,128)(2,1)S(1)} %add_convert_fusion), channel_id=1, source_target_pairs={{0,16},{4,20},{8,24},{12,28},{16,0},{20,4},{24,8},{28,12},{1,17},{... | collective-permute-start | bytes 196616 | tf_op jit(solution)/shard_map/ppermute | solution.py:267
  33.1 0.0 collective-permute-done.3
  33.1 0.3 collective-permute-done.4
  33.4 1.8 %collective-permute-done.5 = bf16[128,256]{1,0:T(8,128)(2,1)S(1)} collective-permute-done((bf16[128,256]{1,0:T(8,128)(2,1)S(1)}, bf16[128,256]{1,0:T(8,128)(2,1)S(1)}, u32[]{:S(2)}, u32[]{:S(2)}) %collective-permute-start.5) | collective-permute-done | bytes 65568 | tf_op jit(solution)/shard_map/ppermute | solution.py:267
  35.2 0.4 %collective-permute-done.9 = bf16[128,256]{1,0:T(8,128)(2,1)S(1)} collective-permute-done((bf16[128,256]{1,0:T(8,128)(2,1)S(1)}, bf16[128,256]{1,0:T(8,128)(2,1)S(1)}, u32[]{:S(2)}, u32[]{:S(2)}) %collective-permute-start.9) | collective-permute-done | bytes 65568 | tf_op jit(solution)/shard_map/ppermute | solution.py:267
  35.6 0.7 %convert_add_fusion = f32[128,256]{1,0:T(8,128)} fusion(bf16[128,256]{1,0:T(8,128)(2,1)S(1)} %collective-permute-done.9, bf16[128,256]{1,0:T(8,128)(2,1)S(1)} %collective-permute-done.5, bf16[128,256]{1,0:T(8,128)(2,1)S(1)} %collective-permute-done.4, f32[128,256]{1,0:T(8,128)S(1)} %get-tuple-element.23, bf16[128,256]{1,0:T(8,128)(2,1)S(1)} %collective-permute-done.3), kind=kLoop, calls=%fused_computation | loop fusion | flops 262144 | bytes 524288 | tf_op jit(solution)/shard_map/add | solution.py:287
  (1 shorter events, 0.0 us)
Async XLA Ops:
  0.9 5.4 %collective-permute-start.2 = (bf16[128,256]{1,0:T(8,128)(2,1)S(1)}, bf16[128,256]{1,0:T(8,128)(2,1)S(1)}, u32[]{:S(2)}, u32[]{:S(2)}) collective-permute-start(bf16[128,256]{1,0:T(8,128)(2,1)S(1)} %convert_element_type.30.rest_0_), channel_id=1, source_target_pairs={{0,3},{1,2},{2,1},{3,0},{4,7},{5,6},{6,5},{7,4},{8,11},{9,10},{10,... | collective-permute-start | bytes 196616 | tf_op jit(solution)/shard_map/ppermute | solution.py:209
  3.4 4.7 %collective-permute-start.1 = (bf16[128,256]{1,0:T(8,128)(2,1)S(1)}, bf16[128,256]{1,0:T(8,128)(2,1)S(1)}, u32[]{:S(2)}, u32[]{:S(2)}) collective-permute-start(bf16[128,256]{1,0:T(8,128)(2,1)S(1)} %convert_element_type.30.rest_0_), channel_id=1, source_target_pairs={{0,2},{1,3},{2,0},{3,1},{4,6},{5,7},{6,4},{7,5},{8,10},{9,11},{10,... | collective-permute-start | bytes 196616 | tf_op jit(solution)/shard_map/ppermute | solution.py:209
  4.0 4.0 %collective-permute-start = (bf16[128,256]{1,0:T(8,128)(2,1)S(1)}, bf16[128,256]{1,0:T(8,128)(2,1)S(1)}, u32[]{:S(2)}, u32[]{:S(2)}) collective-permute-start(bf16[128,256]{1,0:T(8,128)(2,1)S(1)} %convert_element_type.30.rest_0_), channel_id=1, source_target_pairs={{0,1},{1,0},{2,3},{3,2},{4,5},{5,4},{6,7},{7,6},{8,9},{9,8},{10,11... | collective-permute-start | bytes 196616 | tf_op jit(solution)/shard_map/ppermute | solution.py:209
  21.3 8.7 %collective-permute-start.6 = (bf16[128,256]{1,0:T(8,128)(2,1)S(1)}, bf16[128,256]{1,0:T(8,128)(2,1)S(1)}, u32[]{:S(2)}, u32[]{:S(2)}) collective-permute-start(bf16[128,256]{1,0:T(8,128)(2,1)S(1)} %get-tuple-element.28), channel_id=1, source_target_pairs={{0,4},{4,0},{8,12},{12,8},{16,20},{20,16},{24,28},{28,24},{1,5},{5... | collective-permute-start | bytes 196616 | tf_op jit(solution)/shard_map/ppermute | solution.py:267
  23.1 7.1 %collective-permute-start.7 = (bf16[128,256]{1,0:T(8,128)(2,1)S(1)}, bf16[128,256]{1,0:T(8,128)(2,1)S(1)}, u32[]{:S(2)}, u32[]{:S(2)}) collective-permute-start(bf16[128,256]{1,0:T(8,128)(2,1)S(1)} %get-tuple-element.29), channel_id=1, source_target_pairs={{0,8},{4,12},{8,0},{12,4},{16,24},{20,28},{24,16},{28,20},{1,9},{5... | collective-permute-start | bytes 196616 | tf_op jit(solution)/shard_map/ppermute | solution.py:267
  24.7 5.6 %collective-permute-start.8 = (bf16[128,256]{1,0:T(8,128)(2,1)S(1)}, bf16[128,256]{1,0:T(8,128)(2,1)S(1)}, u32[]{:S(2)}, u32[]{:S(2)}) collective-permute-start(bf16[128,256]{1,0:T(8,128)(2,1)S(1)} %get-tuple-element.30), channel_id=1, source_target_pairs={{0,12},{4,8},{8,4},{12,0},{16,28},{20,24},{24,20},{28,16},{1,13},{... | collective-permute-start | bytes 196616 | tf_op jit(solution)/shard_map/ppermute | solution.py:267
  26.7 6.5 %collective-permute-start.3 = (bf16[128,256]{1,0:T(8,128)(2,1)S(1)}, bf16[128,256]{1,0:T(8,128)(2,1)S(1)}, u32[]{:S(2)}, u32[]{:S(2)}) collective-permute-start(bf16[128,256]{1,0:T(8,128)(2,1)S(1)} %get-tuple-element.24), channel_id=1, source_target_pairs={{0,4},{4,0},{8,12},{12,8},{16,20},{20,16},{24,28},{28,24},{1,5},{5... | collective-permute-start | bytes 196616 | tf_op jit(solution)/shard_map/ppermute | solution.py:267
  28.4 5.0 %collective-permute-start.4 = (bf16[128,256]{1,0:T(8,128)(2,1)S(1)}, bf16[128,256]{1,0:T(8,128)(2,1)S(1)}, u32[]{:S(2)}, u32[]{:S(2)}) collective-permute-start(bf16[128,256]{1,0:T(8,128)(2,1)S(1)} %get-tuple-element.25), channel_id=1, source_target_pairs={{0,8},{4,12},{8,0},{12,4},{16,24},{20,28},{24,16},{28,20},{1,9},{5... | collective-permute-start | bytes 196616 | tf_op jit(solution)/shard_map/ppermute | solution.py:267
  30.0 5.2 %collective-permute-start.5 = (bf16[128,256]{1,0:T(8,128)(2,1)S(1)}, bf16[128,256]{1,0:T(8,128)(2,1)S(1)}, u32[]{:S(2)}, u32[]{:S(2)}) collective-permute-start(bf16[128,256]{1,0:T(8,128)(2,1)S(1)} %get-tuple-element.26), channel_id=1, source_target_pairs={{0,12},{4,8},{8,4},{12,0},{16,28},{20,24},{24,20},{28,16},{1,13},{... | collective-permute-start | bytes 196616 | tf_op jit(solution)/shard_map/ppermute | solution.py:267
  30.3 5.4 %collective-permute-start.9 = (bf16[128,256]{1,0:T(8,128)(2,1)S(1)}, bf16[128,256]{1,0:T(8,128)(2,1)S(1)}, u32[]{:S(2)}, u32[]{:S(2)}) collective-permute-start(bf16[128,256]{1,0:T(8,128)(2,1)S(1)} %add_convert_fusion), channel_id=1, source_target_pairs={{0,16},{4,20},{8,24},{12,28},{16,0},{20,4},{24,8},{28,12},{1,17},{... | collective-permute-start | bytes 196616 | tf_op jit(solution)/shard_map/ppermute | solution.py:267

commit v6 on v5

--- a/solution.py
+++ b/solution.py
@@ -8,15 +8,15 @@
 from jax.sharding import PartitionSpec as P
 
 LANES = 128
-UNROLL = 11
+EARLY = 2
 GROUP = 3
 NT = (((1,), (1,)), ((), ()))
 
 
 def index_kernel(sizes, *refs):
     rows, cols, nexc, depth, tiles, pairs = sizes
-    sources, (beta_ref, alpha_ref, weights_ref) = refs[:8], refs[8:11]
-    staged, (table, turned, arrived) = refs[11:19], refs[19:]
+    sources, (beta_ref, slot_ref, alpha_ref, weights_ref) = refs[:8], refs[8:12]
+    staged, (table, turned, arrived) = refs[12:20], refs[20:]
     copies = [
         pltpu.make_async_copy(source, target, arrived.at[n])
         for n, (source, target) in enumerate(zip(sources, staged))
@@ -71,6 +71,12 @@
         total += pltpu.roll(part, m * per_tile, 1) if m else part
     total = total.astype(jnp.int32)
     beta_ref[...] = total
+    member = lax.div(lax.broadcasted_iota(jnp.int32, (tiles, LANES), 1), per_tile)
+    slot = ((total >> 1) & 127) + LANES * member + 1
+    slot = jnp.where((total & 1) == 1, slot, -slot).astype(f32)
+    turned[:LANES, :] = jnp.zeros((LANES, LANES), f32)
+    turned[:tiles, :] = slot
+    slot_ref[...] = turned[:LANES, :].T.astype(jnp.int32)
 
     code = jnp.concatenate(
         [alpha_target[...], jnp.zeros((LANES - nexc, rows), jnp.int32)], axis=0
@@ -108,54 +114,63 @@
     return total
 
 
-def far_kernel(sizes, beta_ref, alpha_ref, weights, *rest):
+def pick(g, cols, beta_ref, c_refs, first, found):
+    code = jnp.concatenate([beta_ref[2 * g : 2 * g + 1], beta_ref[2 * g + 1 : 2 * g + 2]], axis=1)
+    target = code >> 8
+    low = lax.rem(target, cols)
+    high = lax.div(target, cols) ^ lax.axis_index("beta")
+    j_ids = lax.broadcasted_iota(jnp.int32, (cols, 2 * LANES), 0)
+    hot = jnp.where(j_ids == low, 1.0, 0.0).astype(jnp.bfloat16)
+    for k, c_ref in enumerate(c_refs):
+        here = jnp.dot(c_ref[...], hot, preferred_element_type=jnp.float32)
+        found = here if found is None else jnp.where(high == first + k, here, found)
+    return found
+
+
+def early_kernel(cols, beta_ref, *rest):
+    c_refs, early_ref = rest[:-1], rest[-1]
+    for g in range(early_ref.shape[0]):
+        early_ref[g] = pick(g, cols, beta_ref, c_refs, 0, None)
+
+
+def far_kernel(sizes, beta_ref, slot_ref, alpha_ref, weights, early_ref, *rest):
     chunks, rows, cols, nexc, depth, blocks, stride = sizes
-    c_refs, rest = rest[:chunks], rest[chunks:]
+    c_refs, rest = rest[: chunks - EARLY], rest[chunks - EARLY :]
     lifted, same = rest[:2]
     out_refs, (density, picked) = rest[2:-2], rest[-2:]
     per_tile = LANES // GROUP
     bf16, f32 = jnp.bfloat16, jnp.float32
-    groups = beta_ref.shape[0] // 2
-    my_beta = lax.axis_index("beta")
-
-    def beta_code(g):
-        return jnp.concatenate([beta_ref[pl.ds(2 * g, 1), :], beta_ref[pl.ds(2 * g + 1, 1), :]], axis=1)
-
-    def gather_step(g, carry):
-        target = beta_code(g) >> 8
-        low = lax.rem(target, cols)
-        high = lax.div(target, cols) ^ my_beta
-        j_ids = lax.broadcasted_iota(jnp.int32, (cols, 2 * LANES), 0)
-        hot = jnp.where(j_ids == low, 1.0, 0.0).astype(bf16)
-        found = jnp.dot(c_refs[0][...], hot, preferred_element_type=f32)
-        for k in range(1, chunks):
-            found = jnp.where(
-                high == k, jnp.dot(c_refs[k][...], hot, preferred_element_type=f32), found
-            )
+    groups = early_ref.shape[0]
+
+    for g in range(groups):
+        found = pick(g, cols, beta_ref, c_refs, EARLY, early_ref[g])
         picked[g] = found.astype(bf16)
-        return carry
-
-    lax.fori_loop(0, groups, gather_step, 0, unroll=UNROLL)
-
-    def density_step(g, carry):
-        code = beta_code(g)
-        pair = (code >> 1) & 127
-        sign = (2 * (code & 1) - 1).astype(f32)
-        lane = lax.broadcasted_iota(jnp.int32, (1, 2 * LANES), 1)
-        slot = pair + LANES * lax.div(lane & (LANES - 1), per_tile)
-        for half in range(2):
-            span = slice(half * LANES, (half + 1) * LANES)
-            p_ids = lax.broadcasted_iota(jnp.int32, (GROUP * LANES, LANES), 0)
-            h_t = jnp.where(p_ids == slot[:, span], sign[:, span], 0.0).astype(bf16)
-            d = lax.dot_general(picked[g, :, span], h_t, NT, preferred_element_type=f32)
-            for m in range(GROUP):
-                i = (2 * g + half) * GROUP + m
-                density[pl.ds(pl.multiple_of(i * stride, 8), rows), :] = d[
-                    :, m * LANES : (m + 1) * LANES
-                ]
-        return carry
-
-    lax.fori_loop(0, groups, density_step, 0, unroll=UNROLL)
+
+    ids = lax.broadcasted_iota(jnp.int32, (LANES, LANES), 1) + 1
+    for t in range(2 * groups):
+        slot = jnp.broadcast_to(slot_ref[:, t : t + 1], (LANES, LANES))
+        value = jnp.where(slot > 0, 1.0, -1.0)
+        slot = jnp.abs(slot)
+        hots = []
+        for m in range(GROUP):
+            low = m * per_tile // 16 * 16
+            high = min(-(-(m + 1) * per_tile // 16) * 16, LANES)
+            part = slot[low:high] == ids[low:high] + m * LANES
+            part = [jnp.where(part, value[low:high], 0.0).astype(bf16)]
+            if low:
+                part.insert(0, jnp.zeros((low, LANES), bf16))
+            if high < LANES:
+                part.append(jnp.zeros((LANES - high, LANES), bf16))
+            hots.append(jnp.concatenate(part, axis=0))
+        span = slice(t % 2 * LANES, (t % 2 + 1) * LANES)
+        d = jnp.dot(
+            picked[t // 2, :, span],
+            jnp.concatenate(hots, axis=1),
+            preferred_element_type=f32,
+        )
+        for m in range(GROUP):
+            i = t * GROUP + m
+            density[i * stride : i * stride + rows, :] = d[:, m * LANES : (m + 1) * LANES]
 
     def alpha_step(t, carry):
         parts = []
@@ -171,7 +186,7 @@
         )
         return carry
 
-    lax.fori_loop(0, rows // 2, alpha_step, 0, unroll=8)
+    lax.fori_loop(0, rows // 2, alpha_step, 0, unroll=32)
 
     for s in range(blocks // 2, blocks):
         total = scatter(s, rows, nexc, alpha_ref, lifted)
@@ -211,7 +226,7 @@
     ]
 
     depth = nexc + 8
-    tiles = -(-cols // (2 * GROUP * UNROLL)) * 2 * UNROLL
+    tiles = -(-cols // (2 * GROUP)) * 2
     vmem = pl.BlockSpec(memory_space=pltpu.VMEM)
     lists = (
         beta_target,
@@ -223,15 +238,16 @@
         one_body.reshape(1, pairs),
         pair_integrals,
     )
-    beta_code, alpha_code, weights = pl.pallas_call(
+    beta_code, beta_slot, alpha_code, weights = pl.pallas_call(
         functools.partial(index_kernel, (rows, cols, nexc, depth, tiles, pairs)),
         out_shape=[
             pltpu.VMEM((tiles, LANES), jnp.int32),
+            pltpu.VMEM((LANES, LANES), jnp.int32),
             pltpu.VMEM((rows * nexc // LANES, LANES), jnp.int32),
             pltpu.VMEM((rows * depth, LANES), bf16),
         ],
         in_specs=[pl.BlockSpec(memory_space=pltpu.HBM)] * 8,
-        out_specs=[vmem] * 3,
+        out_specs=[vmem] * 4,
         scratch_shapes=[pltpu.VMEM(x.shape, x.dtype) for x in lists]
         + [
             pltpu.VMEM((LANES, LANES), jnp.float32),
@@ -246,6 +262,17 @@
     )(*[pltpu.with_memory_space_constraint(x, pltpu.HBM) for x in lists])
 
     stride = rows + 8
+    early = pl.pallas_call(
+        functools.partial(early_kernel, cols),
+        out_shape=pltpu.VMEM((tiles // 2, rows, 2 * LANES), jnp.float32),
+        in_specs=[vmem] * (1 + EARLY),
+        out_specs=vmem,
+        compiler_params=pltpu.CompilerParams(vmem_limit_bytes=12 * 1024 * 1024),
+        cost_estimate=pl.CostEstimate(
+            flops=4 * rows * cols * tiles * LANES, bytes_accessed=0, transcendentals=0
+        ),
+        name="gather_early",
+    )(beta_code, *gathered[:EARLY])
     sizes = (chunks, rows, cols, nexc, depth, blocks, stride)
     block = jax.ShapeDtypeStruct((rows, cols), bf16)
     block_f32 = jax.ShapeDtypeStruct((rows, cols), jnp.float32)
@@ -253,7 +280,7 @@
         functools.partial(far_kernel, sizes),
         out_shape=[jax.ShapeDtypeStruct((rows * nexc, cols), bf16), block_f32]
         + [block] * (blocks // 2),
-        in_specs=[vmem] * (3 + chunks),
+        in_specs=[vmem] * (5 + chunks - EARLY),
         out_specs=[vmem] * (2 + blocks // 2),
         scratch_shapes=[
             pltpu.VMEM((tiles * GROUP * stride, LANES), jnp.float32),
@@ -261,7 +288,7 @@
         ],
         compiler_params=pltpu.CompilerParams(vmem_limit_bytes=36 * 1024 * 1024),
         name="sigma_far",
-    )(beta_code, alpha_code, weights, *gathered)
+    )(beta_code, beta_slot, alpha_code, weights, early, *gathered[EARLY:])
 
     def send(s, value):
         return lax.ppermute(value, "alpha", [(d, d ^ s) for d in range(blocks)])

time: 36.5 us -> 32.3 us (0.88)
  Pallas kernels: 17.3 us -> 14.6 us
  waiting for transfers between devices: 4.21 us -> 2.68 us
    pallas_call x1, Pallas kernels: 13.3 us -> 8.77 us  [shards(): pl.pallas_call(functools.partial(far_kernel, sizes), out_shape=[jax.Shape...]
    pallas_call x0 -> x1, Pallas kernels: none -> 1.65 us  [shards(): pl.pallas_call(functools.partial(early_kernel, cols), out_shape=pltpu.VME...]
    ppermute x3, waiting for transfers between devices: 1.7 us -> 0.19 us  [shards(): lax.ppermute(civec_bf, 'beta', [(d, d ^ s) for d in range(chunks)])]
  transfers between devices with their start and end apart: 10 -> 10, of which waited for: 4 -> 5; matrix products, arithmetic and copies ran while one was open for 0% -> 0% of each run, Pallas kernels for 11% -> 18%
where the time goes in v6:
time: 32.3 us; the launch traced here: 32.1 us
  Pallas kernels  14.6 us (45%)
  starting transfers between devices  13.1 us (41%)
  waiting for transfers between devices  2.68 us (8%)
  other arithmetic  1.65 us (5%)
    ppermute x7, starting transfers between devices, send(): return lax.ppermute(value, 'alpha', [(d, d ^ s) for d in range(blocks)])  9.96 us
    pallas_call x1, Pallas kernels, shards(): pl.pallas_call(functools.partial(far_kernel, sizes), out_shape=[jax.Shape...  8.77 us
    ppermute x3, starting transfers between devices, shards(): lax.ppermute(civec_bf, 'beta', [(d, d ^ s) for d in range(chunks)])  3.17 us
    ppermute x7, waiting for transfers between devices, send(): return lax.ppermute(value, 'alpha', [(d, d ^ s) for d in range(blocks)])  2.49 us
    pallas_call x1, Pallas kernels, shards(): pl.pallas_call(functools.partial(index_kernel, (rows, cols, nexc, depth,...  2.35 us
    pallas_call x1, Pallas kernels, shards(): pl.pallas_call(functools.partial(near_kernel, (rows, nexc, blocks)), out_...  1.79 us
    pallas_call x1, Pallas kernels, shards(): pl.pallas_call(functools.partial(early_kernel, cols), out_shape=pltpu.VME...  1.65 us
    convert_element_type x1, other arithmetic, shards(): civec_bf = ci_vector.astype(bf16)  0.91 us
  transfers between devices with their start and end apart: 10, of which 5 were waited for; matrix products, arithmetic and copies ran while one was open for 0% of the time, Pallas kernels for 18%

profile of v6, /device:TPU:0, one launch (start us, length us, event | category | flops | bytes accessed | tf_op | source)
XLA Modules:
  0.0 32.1 jit_solution(2462022687717070229)
XLA Ops:
  0.0 0.9 %convert_element_type.30.rest_0_ = bf16[128,256]{1,0:T(8,128)(2,1)S(1)} convert(f32[128,256]{1,0:T(8,128)} %param.9) | non-fusion elementwise | flops 32768 | bytes 196608 | tf_op jit(solution)/shard_map/convert_element_type | solution.py:222
  0.9 0.5 %collective-permute-start = (bf16[128,256]{1,0:T(8,128)(2,1)S(1)}, bf16[128,256]{1,0:T(8,128)(2,1)S(1)}, u32[]{:S(2)}, u32[]{:S(2)}) collective-permute-start(bf16[128,256]{1,0:T(8,128)(2,1)S(1)} %convert_element_type.30.rest_0_), channel_id=1, source_target_pairs={{0,1},{1,0},{2,3},{3,2},{4,5},{5,4},{6,7},{7,6},{8,9},{9,8},{10,11... | collective-permute-start | bytes 196616 | tf_op jit(solution)/shard_map/ppermute | solution.py:224
  1.4 2.6 %collective-permute-start.2 = (bf16[128,256]{1,0:T(8,128)(2,1)S(1)}, bf16[128,256]{1,0:T(8,128)(2,1)S(1)}, u32[]{:S(2)}, u32[]{:S(2)}) collective-permute-start(bf16[128,256]{1,0:T(8,128)(2,1)S(1)} %convert_element_type.30.rest_0_), channel_id=1, source_target_pairs={{0,3},{1,2},{2,1},{3,0},{4,7},{5,6},{6,5},{7,4},{8,11},{9,10},{10,... | collective-permute-start | bytes 196616 | tf_op jit(solution)/shard_map/ppermute | solution.py:224
  4.0 0.0 collective-permute-start.1
  4.1 2.3 %index_lists.1 = (s32[86,128]{1,0:T(8,128)S(1)}, s32[128,128]{1,0:T(8,128)S(1)}, s32[40,128]{1,0:T(8,128)S(1)}, bf16[6144,128]{1,0:T(8,128)(2,1)S(1)}) custom-call(s32[40,256]{1,0:T(8,128)} %refs_0_.1, s32[40,256]{1,0:T(8,128)} %refs_1_.1, s32[40,256]{1,0:T(8,128)} %refs_2_.1, s32[40,128]{1,0:T(8,128)} %refs_3_.1, s32[40,128]{1,0:T(8,128)} %refs_4_.1, ...), custom_call_target="tpu_custom_call" | custom-call | flops 402653184 | tf_op jit(solution)/shard_map/index_lists/pallas_call | solution.py:241
  6.4 0.0 collective-permute-done.rest_1_
  6.4 1.7 %gather_early.1.early_ref = f32[43,128,256]{2,1,0:T(8,128)S(1)} custom-call(s32[86,128]{1,0:T(8,128)S(1)} %get-tuple-element.20.beta_ref, bf16[128,256]{1,0:T(8,128)(2,1)S(1)} %convert_element_type.30.rest_0_, bf16[128,256]{1,0:T(8,128)(2,1)S(1)} %collective-permute-done.rest_1_), custom_call_target="tpu_custom_call" | custom-call | flops 1442840576 | tf_op jit(solution)/shard_map/gather_early/pallas_call | solution.py:265
  8.1 0.0 collective-permute-done.2.rest_1_
  8.1 0.2 collective-permute-done.1.rest_0_
  8.3 8.8 %sigma_far.1 = (bf16[5120,256]{1,0:T(8,128)(2,1)S(1)}, f32[128,256]{1,0:T(8,128)S(1)}, bf16[128,256]{1,0:T(8,128)(2,1)S(1)}, bf16[128,256]{1,0:T(8,128)(2,1)S(1)...) custom-call(s32[86,128]{1,0:T(8,128)S(1)} %get-tuple-element.20.beta_ref, ...), custom_call_target="tpu_custom_call" | custom-call | tf_op jit(solution)/shard_map/sigma_far/pallas_call | solution.py:279
  17.1 1.9 %collective-permute-start.6 = (bf16[128,256]{1,0:T(8,128)(2,1)S(1)}, bf16[128,256]{1,0:T(8,128)(2,1)S(1)}, u32[]{:S(2)}, u32[]{:S(2)}) collective-permute-start(bf16[128,256]{1,0:T(8,128)(2,1)S(1)} %get-tuple-element.30), channel_id=1, source_target_pairs={{0,4},{4,0},{8,12},{12,8},{16,20},{20,16},{24,28},{28,24},{1,5},{5... | collective-permute-start | bytes 196616 | tf_op jit(solution)/shard_map/ppermute | solution.py:294
  19.0 1.6 %collective-permute-start.7 = (bf16[128,256]{1,0:T(8,128)(2,1)S(1)}, bf16[128,256]{1,0:T(8,128)(2,1)S(1)}, u32[]{:S(2)}, u32[]{:S(2)}) collective-permute-start(bf16[128,256]{1,0:T(8,128)(2,1)S(1)} %get-tuple-element.31), channel_id=1, source_target_pairs={{0,8},{4,12},{8,0},{12,4},{16,24},{20,28},{24,16},{28,20},{1,9},{5... | collective-permute-start | bytes 196616 | tf_op jit(solution)/shard_map/ppermute | solution.py:294
  20.6 0.1 collective-permute-start.8
  20.6 1.8 %sigma_near.1 = (f32[128,256]{1,0:T(8,128)S(1)}, bf16[128,256]{1,0:T(8,128)(2,1)S(1)}, bf16[128,256]{1,0:T(8,128)(2,1)S(1)}, bf16[128,256]{1,0:T(8,128)(2,1)S(1)}) custom-call(s32[40,128]{1,0:T(8,128)S(1)} %get-tuple-element.19.alpha_ref, bf16[5120,256]{1,0:T(8,128)(2,1)S(1)} %get-tuple-element.23.lifted, f32[128,256]{1,0:T(8,128)S(1)} %get-tuple-element.24.same), custom_call_target="tpu_custom_call" | custom-call | flops 1342177280 | tf_op jit(solution)/shard_map/sigma_near/pallas_call | solution.py:300
  22.4 1.9 %collective-permute-start.3 = (bf16[128,256]{1,0:T(8,128)(2,1)S(1)}, bf16[128,256]{1,0:T(8,128)(2,1)S(1)}, u32[]{:S(2)}, u32[]{:S(2)}) collective-permute-start(bf16[128,256]{1,0:T(8,128)(2,1)S(1)} %get-tuple-element.26), channel_id=1, source_target_pairs={{0,4},{4,0},{8,12},{12,8},{16,20},{20,16},{24,28},{28,24},{1,5},{5... | collective-permute-start | bytes 196616 | tf_op jit(solution)/shard_map/ppermute | solution.py:294
  24.3 1.6 %collective-permute-start.4 = (bf16[128,256]{1,0:T(8,128)(2,1)S(1)}, bf16[128,256]{1,0:T(8,128)(2,1)S(1)}, u32[]{:S(2)}, u32[]{:S(2)}) collective-permute-start(bf16[128,256]{1,0:T(8,128)(2,1)S(1)} %get-tuple-element.27), channel_id=1, source_target_pairs={{0,8},{4,12},{8,0},{12,4},{16,24},{20,28},{24,16},{28,20},{1,9},{5... | collective-permute-start | bytes 196616 | tf_op jit(solution)/shard_map/ppermute | solution.py:294
  25.9 0.0 collective-permute-done.6
  25.9 0.1 collective-permute-start.5
  26.0 0.0 collective-permute-done.7
  26.0 0.1 collective-permute-done.8
  26.2 2.9 %collective-permute-start.9 = (bf16[128,256]{1,0:T(8,128)(2,1)S(1)}, bf16[128,256]{1,0:T(8,128)(2,1)S(1)}, u32[]{:S(2)}, u32[]{:S(2)}) collective-permute-start(bf16[128,256]{1,0:T(8,128)(2,1)S(1)} %add_convert_fusion), channel_id=1, source_target_pairs={{0,16},{4,20},{8,24},{12,28},{16,0},{20,4},{24,8},{28,12},{1,17},{... | collective-permute-start | bytes 196616 | tf_op jit(solution)/shard_map/ppermute | solution.py:294
  29.0 0.0 collective-permute-done.3
  29.0 0.3 collective-permute-done.4
  29.3 1.8 %collective-permute-done.5 = bf16[128,256]{1,0:T(8,128)(2,1)S(1)} collective-permute-done((bf16[128,256]{1,0:T(8,128)(2,1)S(1)}, bf16[128,256]{1,0:T(8,128)(2,1)S(1)}, u32[]{:S(2)}, u32[]{:S(2)}) %collective-permute-start.5) | collective-permute-done | bytes 65568 | tf_op jit(solution)/shard_map/ppermute | solution.py:294
  31.1 0.3 collective-permute-done.9
  31.4 0.7 %convert_add_fusion = f32[128,256]{1,0:T(8,128)} fusion(bf16[128,256]{1,0:T(8,128)(2,1)S(1)} %collective-permute-done.9, bf16[128,256]{1,0:T(8,128)(2,1)S(1)} %collective-permute-done.5, bf16[128,256]{1,0:T(8,128)(2,1)S(1)} %collective-permute-done.4, f32[128,256]{1,0:T(8,128)S(1)} %get-tuple-element.25, bf16[128,256]{1,0:T(8,128)(2,1)S(1)} %collective-permute-done.3), kind=kLoop, calls=%fused_computation | loop fusion | flops 262144 | bytes 524288 | tf_op jit(solution)/shard_map/add | solution.py:314
  (1 shorter events, 0.0 us)
Async XLA Ops:
  0.9 5.5 %collective-permute-start = (bf16[128,256]{1,0:T(8,128)(2,1)S(1)}, bf16[128,256]{1,0:T(8,128)(2,1)S(1)}, u32[]{:S(2)}, u32[]{:S(2)}) collective-permute-start(bf16[128,256]{1,0:T(8,128)(2,1)S(1)} %convert_element_type.30.rest_0_), channel_id=1, source_target_pairs={{0,1},{1,0},{2,3},{3,2},{4,5},{5,4},{6,7},{7,6},{8,9},{9,8},{10,11... | collective-permute-start | bytes 196616 | tf_op jit(solution)/shard_map/ppermute | solution.py:224
  1.4 6.7 %collective-permute-start.2 = (bf16[128,256]{1,0:T(8,128)(2,1)S(1)}, bf16[128,256]{1,0:T(8,128)(2,1)S(1)}, u32[]{:S(2)}, u32[]{:S(2)}) collective-permute-start(bf16[128,256]{1,0:T(8,128)(2,1)S(1)} %convert_element_type.30.rest_0_), channel_id=1, source_target_pairs={{0,3},{1,2},{2,1},{3,0},{4,7},{5,6},{6,5},{7,4},{8,11},{9,10},{10,... | collective-permute-start | bytes 196616 | tf_op jit(solution)/shard_map/ppermute | solution.py:224
  4.0 4.3 %collective-permute-start.1 = (bf16[128,256]{1,0:T(8,128)(2,1)S(1)}, bf16[128,256]{1,0:T(8,128)(2,1)S(1)}, u32[]{:S(2)}, u32[]{:S(2)}) collective-permute-start(bf16[128,256]{1,0:T(8,128)(2,1)S(1)} %convert_element_type.30.rest_0_), channel_id=1, source_target_pairs={{0,2},{1,3},{2,0},{3,1},{4,6},{5,7},{6,4},{7,5},{8,10},{9,11},{10,... | collective-permute-start | bytes 196616 | tf_op jit(solution)/shard_map/ppermute | solution.py:224
  17.1 8.8 %collective-permute-start.6 = (bf16[128,256]{1,0:T(8,128)(2,1)S(1)}, bf16[128,256]{1,0:T(8,128)(2,1)S(1)}, u32[]{:S(2)}, u32[]{:S(2)}) collective-permute-start(bf16[128,256]{1,0:T(8,128)(2,1)S(1)} %get-tuple-element.30), channel_id=1, source_target_pairs={{0,4},{4,0},{8,12},{12,8},{16,20},{20,16},{24,28},{28,24},{1,5},{5... | collective-permute-start | bytes 196616 | tf_op jit(solution)/shard_map/ppermute | solution.py:294
  19.0 7.0 %collective-permute-start.7 = (bf16[128,256]{1,0:T(8,128)(2,1)S(1)}, bf16[128,256]{1,0:T(8,128)(2,1)S(1)}, u32[]{:S(2)}, u32[]{:S(2)}) collective-permute-start(bf16[128,256]{1,0:T(8,128)(2,1)S(1)} %get-tuple-element.31), channel_id=1, source_target_pairs={{0,8},{4,12},{8,0},{12,4},{16,24},{20,28},{24,16},{28,20},{1,9},{5... | collective-permute-start | bytes 196616 | tf_op jit(solution)/shard_map/ppermute | solution.py:294
  20.6 5.5 %collective-permute-start.8 = (bf16[128,256]{1,0:T(8,128)(2,1)S(1)}, bf16[128,256]{1,0:T(8,128)(2,1)S(1)}, u32[]{:S(2)}, u32[]{:S(2)}) collective-permute-start(bf16[128,256]{1,0:T(8,128)(2,1)S(1)} %get-tuple-element.32), channel_id=1, source_target_pairs={{0,12},{4,8},{8,4},{12,0},{16,28},{20,24},{24,20},{28,16},{1,13},{... | collective-permute-start | bytes 196616 | tf_op jit(solution)/shard_map/ppermute | solution.py:294
  22.4 6.6 %collective-permute-start.3 = (bf16[128,256]{1,0:T(8,128)(2,1)S(1)}, bf16[128,256]{1,0:T(8,128)(2,1)S(1)}, u32[]{:S(2)}, u32[]{:S(2)}) collective-permute-start(bf16[128,256]{1,0:T(8,128)(2,1)S(1)} %get-tuple-element.26), channel_id=1, source_target_pairs={{0,4},{4,0},{8,12},{12,8},{16,20},{20,16},{24,28},{28,24},{1,5},{5... | collective-permute-start | bytes 196616 | tf_op jit(solution)/shard_map/ppermute | solution.py:294
  24.3 5.0 %collective-permute-start.4 = (bf16[128,256]{1,0:T(8,128)(2,1)S(1)}, bf16[128,256]{1,0:T(8,128)(2,1)S(1)}, u32[]{:S(2)}, u32[]{:S(2)}) collective-permute-start(bf16[128,256]{1,0:T(8,128)(2,1)S(1)} %get-tuple-element.27), channel_id=1, source_target_pairs={{0,8},{4,12},{8,0},{12,4},{16,24},{20,28},{24,16},{28,20},{1,9},{5... | collective-permute-start | bytes 196616 | tf_op jit(solution)/shard_map/ppermute | solution.py:294
  25.9 5.2 %collective-permute-start.5 = (bf16[128,256]{1,0:T(8,128)(2,1)S(1)}, bf16[128,256]{1,0:T(8,128)(2,1)S(1)}, u32[]{:S(2)}, u32[]{:S(2)}) collective-permute-start(bf16[128,256]{1,0:T(8,128)(2,1)S(1)} %get-tuple-element.28), channel_id=1, source_target_pairs={{0,12},{4,8},{8,4},{12,0},{16,28},{20,24},{24,20},{28,16},{1,13},{... | collective-permute-start | bytes 196616 | tf_op jit(solution)/shard_map/ppermute | solution.py:294
  26.2 5.2 %collective-permute-start.9 = (bf16[128,256]{1,0:T(8,128)(2,1)S(1)}, bf16[128,256]{1,0:T(8,128)(2,1)S(1)}, u32[]{:S(2)}, u32[]{:S(2)}) collective-permute-start(bf16[128,256]{1,0:T(8,128)(2,1)S(1)} %add_convert_fusion), channel_id=1, source_target_pairs={{0,16},{4,20},{8,24},{12,28},{16,0},{20,4},{24,8},{28,12},{1,17},{... | collective-permute-start | bytes 196616 | tf_op jit(solution)/shard_map/ppermute | solution.py:294

commit v7 on v6

--- a/solution.py
+++ b/solution.py
@@ -8,6 +8,7 @@
 from jax.sharding import PartitionSpec as P
 
 LANES = 128
+BATCH = 32
 EARLY = 2
 GROUP = 3
 NT = (((1,), (1,)), ((), ()))
@@ -96,22 +97,21 @@
         alpha_ref[8 * w : 8 * w + 8, :] = found[w].astype(jnp.int32)
 
 
-def scatter(s, rows, nexc, alpha_ref, lifted):
+def scatter(s, first, last, sizes, alpha_ref, lifted):
+    rows, nexc = sizes[1], sizes[3]
     base = (lax.axis_index("alpha") ^ s) * rows
-    total = jnp.zeros((rows, lifted.shape[1]), jnp.float32)
     period = rows * nexc // LANES // 8
-    for t in range(8):
-        hots = []
-        for w in range(period):
-            target = alpha_ref[8 * w + t : 8 * w + t + 1, :] - base
-            b_ids = lax.broadcasted_iota(jnp.int32, (rows, LANES), 0)
-            hots.append(jnp.where(b_ids == target, 1.0, 0.0).astype(jnp.bfloat16))
-        total += jnp.dot(
-            jnp.concatenate(hots, axis=1),
-            lifted[period * t * LANES : period * (t + 1) * LANES, :],
-            preferred_element_type=jnp.float32,
-        )
-    return total
+    b_ids = lax.broadcasted_iota(jnp.int32, (rows, LANES), 0)
+    hots = []
+    for tile in range(first * nexc // LANES, last * nexc // LANES):
+        row = 8 * (tile % period) + tile // period
+        target = alpha_ref[row : row + 1, :] - base
+        hots.append(jnp.where(b_ids == target, 1.0, 0.0).astype(jnp.bfloat16))
+    return jnp.dot(
+        jnp.concatenate(hots, axis=1),
+        lifted[first * nexc : last * nexc, :],
+        preferred_element_type=jnp.float32,
+    )
 
 
 def pick(g, cols, beta_ref, c_refs, first, found):
@@ -137,7 +137,7 @@
     chunks, rows, cols, nexc, depth, blocks, stride = sizes
     c_refs, rest = rest[: chunks - EARLY], rest[chunks - EARLY :]
     lifted, same = rest[:2]
-    out_refs, (density, picked) = rest[2:-2], rest[-2:]
+    out_refs, (density, picked, sums) = rest[2:-3], rest[-3:]
     per_tile = LANES // GROUP
     bf16, f32 = jnp.bfloat16, jnp.float32
     groups = early_ref.shape[0]
@@ -172,33 +172,34 @@
             i = t * GROUP + m
             density[i * stride : i * stride + rows, :] = d[:, m * LANES : (m + 1) * LANES]
 
-    def alpha_step(t, carry):
-        parts = []
-        for m in range(2):
-            a = 2 * t + m
-            d = density[pl.ds(a, cols, stride=stride), :].astype(bf16)
-            u = weights[pl.ds(pl.multiple_of(a * depth, 16), depth), :]
-            l = lax.dot_general(u, d, NT, preferred_element_type=f32)
-            same[pl.ds(a, 1), :] = l[nexc : nexc + 1] + l[nexc + 1 : nexc + 2]
-            parts.append(l[:nexc])
-        lifted[pl.ds(pl.multiple_of(t * 2 * nexc, 2 * nexc), 2 * nexc), :] = (
-            jnp.concatenate(parts, axis=0).astype(bf16)
-        )
-        return carry
-
-    lax.fori_loop(0, rows // 2, alpha_step, 0, unroll=32)
-
-    for s in range(blocks // 2, blocks):
-        total = scatter(s, rows, nexc, alpha_ref, lifted)
-        out_refs[s - blocks // 2][...] = total.astype(bf16)
-
-
-def near_kernel(sizes, alpha_ref, lifted, same, own_ref, *out_refs):
-    rows, nexc, blocks = sizes
-    for s in range(1, blocks // 2):
-        total = scatter(s, rows, nexc, alpha_ref, lifted)
-        out_refs[s - 1][...] = total.astype(jnp.bfloat16)
-    own_ref[...] = scatter(0, rows, nexc, alpha_ref, lifted) + same[...]
+    for first in range(0, rows, BATCH):
+        for a in range(first, first + BATCH, 2):
+            parts = []
+            for m in range(2):
+                d = density[pl.ds(a + m, cols, stride=stride), :].T.astype(bf16)
+                u = weights[(a + m) * depth : (a + m + 1) * depth, :]
+                l = jnp.dot(u, d, preferred_element_type=f32)
+                same[a + m : a + m + 1, :] = l[nexc : nexc + 1] + l[nexc + 1 : nexc + 2]
+                parts.append(l[:nexc])
+            lifted[a * nexc : (a + 2) * nexc, :] = jnp.concatenate(parts, axis=0).astype(bf16)
+        for s in range(blocks // 2):
+            part = scatter(blocks // 2 + s, first, first + BATCH, sizes, alpha_ref, lifted)
+            if first:
+                part += sums[s]
+            if first + BATCH < rows:
+                sums[s] = part
+            else:
+                out_refs[s][...] = part.astype(bf16)
+
+
+def near_kernel(sizes, alpha_ref, lifted, *out_refs):
+    for s, out_ref in enumerate(out_refs):
+        total = scatter(s + 1, 0, sizes[1], sizes, alpha_ref, lifted)
+        out_ref[...] = total.astype(jnp.bfloat16)
+
+
+def own_kernel(sizes, alpha_ref, lifted, same, own_ref):
+    own_ref[...] = scatter(0, 0, sizes[1], sizes, alpha_ref, lifted) + same[...]
 
 
 def shards(
@@ -261,7 +262,7 @@
         name="index_lists",
     )(*[pltpu.with_memory_space_constraint(x, pltpu.HBM) for x in lists])
 
-    stride = rows + 8
+    stride = rows + 4
     early = pl.pallas_call(
         functools.partial(early_kernel, cols),
         out_shape=pltpu.VMEM((tiles // 2, rows, 2 * LANES), jnp.float32),
@@ -285,6 +286,7 @@
         scratch_shapes=[
             pltpu.VMEM((tiles * GROUP * stride, LANES), jnp.float32),
             pltpu.VMEM((tiles // 2, rows, 2 * LANES), bf16),
+            pltpu.VMEM((blocks // 2, rows, cols), jnp.float32),
         ],
         compiler_params=pltpu.CompilerParams(vmem_limit_bytes=36 * 1024 * 1024),
         name="sigma_far",
@@ -294,19 +296,30 @@
         return lax.ppermute(value, "alpha", [(d, d ^ s) for d in range(blocks)])
 
     far_sum = far[0].astype(jnp.float32)
-    for s in range(1, blocks // 2):
+    for s in reversed(range(1, blocks // 2)):
         far_sum = far_sum + send(s, far[s]).astype(jnp.float32)
     far_sum = far_sum.astype(bf16)
-    own, *near = pl.pallas_call(
-        functools.partial(near_kernel, (rows, nexc, blocks)),
-        out_shape=[block_f32] + [block] * (blocks // 2 - 1),
-        in_specs=[vmem] * 3,
-        out_specs=[vmem] * (blocks // 2),
+    near = pl.pallas_call(
+        functools.partial(near_kernel, sizes),
+        out_shape=[block] * (blocks // 2 - 1),
+        in_specs=[vmem] * 2,
+        out_specs=[vmem] * (blocks // 2 - 1),
         compiler_params=pltpu.CompilerParams(vmem_limit_bytes=8 * 1024 * 1024),
         cost_estimate=pl.CostEstimate(
-            flops=blocks * rows * rows * nexc * cols, bytes_accessed=0, transcendentals=0
+            flops=(blocks - 2) * rows * rows * nexc * cols, bytes_accessed=0, transcendentals=0
         ),
         name="sigma_near",
+    )(alpha_code, lifted)
+    own = pl.pallas_call(
+        functools.partial(own_kernel, sizes),
+        out_shape=block_f32,
+        in_specs=[vmem] * 3,
+        out_specs=vmem,
+        compiler_params=pltpu.CompilerParams(vmem_limit_bytes=4 * 1024 * 1024),
+        cost_estimate=pl.CostEstimate(
+            flops=2 * rows * rows * nexc * cols, bytes_accessed=0, transcendentals=0
+        ),
+        name="sigma_own",
     )(alpha_code, lifted, same)
     crossing = send(blocks // 2, far_sum)
     total = own

time: 32.3 us -> 30.4 us (0.941)
  Pallas kernels: 14.6 us -> 13.3 us
  waiting for transfers between devices: 2.68 us -> 1.94 us
    pallas_call x1, Pallas kernels: 8.77 us -> 7.63 us  [shards(): pl.pallas_call(functools.partial(far_kernel, sizes), out_shape=[jax.Shape...]
    ppermute x7, waiting for transfers between devices: 2.49 us -> 1.75 us  [send(): return lax.ppermute(value, 'alpha', [(d, d ^ s) for d in range(blocks)])]
    pallas_call x1 -> x2, Pallas kernels: 1.79 us -> 1.69 us  [the longest x1 1.19 us: shards(): pl.pallas_call(functools.partial(near_kernel, sizes), out_shape=[block] *...]
  transfers between devices with their start and end apart: 10 -> 10, of which waited for: 5 -> 3; matrix products, arithmetic and copies ran while one was open for 0% -> 0% of each run, Pallas kernels for 18% -> 19%
where the time goes in v7:
time: 30.4 us; the launch traced here: 30.2 us
  starting transfers between devices  13.3 us (44%)
  Pallas kernels  13.3 us (44%)
  waiting for transfers between devices  1.94 us (6%)
  other arithmetic  1.64 us (5%)
    ppermute x7, starting transfers between devices, send(): return lax.ppermute(value, 'alpha', [(d, d ^ s) for d in range(blocks)])  10.1 us
    pallas_call x1, Pallas kernels, shards(): pl.pallas_call(functools.partial(far_kernel, sizes), out_shape=[jax.Shape...  7.63 us
    ppermute x3, starting transfers between devices, shards(): lax.ppermute(civec_bf, 'beta', [(d, d ^ s) for d in range(chunks)])  3.17 us
    pallas_call x1, Pallas kernels, shards(): pl.pallas_call(functools.partial(index_kernel, (rows, cols, nexc, depth,...  2.35 us
    ppermute x7, waiting for transfers between devices, send(): return lax.ppermute(value, 'alpha', [(d, d ^ s) for d in range(blocks)])  1.75 us
    pallas_call x1, Pallas kernels, shards(): pl.pallas_call(functools.partial(early_kernel, cols), out_shape=pltpu.VME...  1.66 us
    pallas_call x1, Pallas kernels, shards(): pl.pallas_call(functools.partial(near_kernel, sizes), out_shape=[block] *...  1.19 us
    convert_element_type x1, other arithmetic, shards(): civec_bf = ci_vector.astype(bf16)  0.91 us
  transfers between devices with their start and end apart: 10, of which 3 were waited for; matrix products, arithmetic and copies ran while one was open for 0% of the time, Pallas kernels for 19%

profile of v7, /device:TPU:0, one launch (start us, length us, event | category | flops | bytes accessed | tf_op | source)
XLA Modules:
  0.0 30.2 jit_solution(17194509798502194632)
XLA Ops:
  0.0 0.9 %convert_element_type.30.rest_0_ = bf16[128,256]{1,0:T(8,128)(2,1)S(1)} convert(f32[128,256]{1,0:T(8,128)} %param.9) | non-fusion elementwise | flops 32768 | bytes 196608 | tf_op jit(solution)/shard_map/convert_element_type | solution.py:223
  0.9 0.5 %collective-permute-start = (bf16[128,256]{1,0:T(8,128)(2,1)S(1)}, bf16[128,256]{1,0:T(8,128)(2,1)S(1)}, u32[]{:S(2)}, u32[]{:S(2)}) collective-permute-start(bf16[128,256]{1,0:T(8,128)(2,1)S(1)} %convert_element_type.30.rest_0_), channel_id=1, source_target_pairs={{0,1},{1,0},{2,3},{3,2},{4,5},{5,4},{6,7},{7,6},{8,9},{9,8},{10,11... | collective-permute-start | bytes 196616 | tf_op jit(solution)/shard_map/ppermute | solution.py:225
  1.4 2.6 %collective-permute-start.2 = (bf16[128,256]{1,0:T(8,128)(2,1)S(1)}, bf16[128,256]{1,0:T(8,128)(2,1)S(1)}, u32[]{:S(2)}, u32[]{:S(2)}) collective-permute-start(bf16[128,256]{1,0:T(8,128)(2,1)S(1)} %convert_element_type.30.rest_0_), channel_id=1, source_target_pairs={{0,3},{1,2},{2,1},{3,0},{4,7},{5,6},{6,5},{7,4},{8,11},{9,10},{10,... | collective-permute-start | bytes 196616 | tf_op jit(solution)/shard_map/ppermute | solution.py:225
  4.0 0.0 collective-permute-start.1
  4.1 2.3 %index_lists.1 = (s32[86,128]{1,0:T(8,128)S(1)}, s32[128,128]{1,0:T(8,128)S(1)}, s32[40,128]{1,0:T(8,128)S(1)}, bf16[6144,128]{1,0:T(8,128)(2,1)S(1)}) custom-call(s32[40,256]{1,0:T(8,128)} %refs_0_.1, s32[40,256]{1,0:T(8,128)} %refs_1_.1, s32[40,256]{1,0:T(8,128)} %refs_2_.1, s32[40,128]{1,0:T(8,128)} %refs_3_.1, s32[40,128]{1,0:T(8,128)} %refs_4_.1, ...), custom_call_target="tpu_custom_call" | custom-call | flops 402653184 | tf_op jit(solution)/shard_map/index_lists/pallas_call | solution.py:242
  6.4 0.0 collective-permute-done.rest_1_
  6.4 1.7 %gather_early.1.early_ref = f32[43,128,256]{2,1,0:T(8,128)S(1)} custom-call(s32[86,128]{1,0:T(8,128)S(1)} %get-tuple-element.19.beta_ref, bf16[128,256]{1,0:T(8,128)(2,1)S(1)} %convert_element_type.30.rest_0_, bf16[128,256]{1,0:T(8,128)(2,1)S(1)} %collective-permute-done.rest_1_), custom_call_target="tpu_custom_call" | custom-call | flops 1442840576 | tf_op jit(solution)/shard_map/gather_early/pallas_call | solution.py:266
  8.1 0.0 collective-permute-done.2.rest_1_
  8.1 0.2 collective-permute-done.1.rest_0_
  8.3 7.6 %sigma_far.1 = (bf16[5120,256]{1,0:T(8,128)(2,1)S(1)}, f32[128,256]{1,0:T(8,128)S(1)}, bf16[128,256]{1,0:T(8,128)(2,1)S(1)}, bf16[128,256]{1,0:T(8,128)(2,1)S(1)...) custom-call(s32[86,128]{1,0:T(8,128)S(1)} %get-tuple-element.19.beta_ref, ...), custom_call_target="tpu_custom_call" | custom-call | tf_op jit(solution)/shard_map/sigma_far/pallas_call | solution.py:280
  15.9 2.9 %collective-permute-start.6 = (bf16[128,256]{1,0:T(8,128)(2,1)S(1)}, bf16[128,256]{1,0:T(8,128)(2,1)S(1)}, u32[]{:S(2)}, u32[]{:S(2)}) collective-permute-start(bf16[128,256]{1,0:T(8,128)(2,1)S(1)} %get-tuple-element.28), channel_id=1, source_target_pairs={{0,12},{4,8},{8,4},{12,0},{16,28},{20,24},{24,20},{28,16},{1,13},{... | collective-permute-start | bytes 196616 | tf_op jit(solution)/shard_map/ppermute | solution.py:296
  18.9 0.4 %collective-permute-start.7 = (bf16[128,256]{1,0:T(8,128)(2,1)S(1)}, bf16[128,256]{1,0:T(8,128)(2,1)S(1)}, u32[]{:S(2)}, u32[]{:S(2)}) collective-permute-start(bf16[128,256]{1,0:T(8,128)(2,1)S(1)} %get-tuple-element.29), channel_id=1, source_target_pairs={{0,8},{4,12},{8,0},{12,4},{16,24},{20,28},{24,16},{28,20},{1,9},{5... | collective-permute-start | bytes 196616 | tf_op jit(solution)/shard_map/ppermute | solution.py:296
  19.3 0.2 collective-permute-start.8
  19.5 1.2 %sigma_near.1 = (bf16[128,256]{1,0:T(8,128)(2,1)S(1)}, bf16[128,256]{1,0:T(8,128)(2,1)S(1)}, bf16[128,256]{1,0:T(8,128)(2,1)S(1)}) custom-call(s32[40,128]{1,0:T(8,128)S(1)} %get-tuple-element.18.alpha_ref, bf16[5120,256]{1,0:T(8,128)(2,1)S(1)} %get-tuple-element.22.lifted), custom_call_target="tpu_custom_call" | custom-call | flops 1006632960 | tf_op jit(solution)/shard_map/sigma_near/pallas_call | solution.py:302
  20.7 1.9 %collective-permute-start.3 = (bf16[128,256]{1,0:T(8,128)(2,1)S(1)}, bf16[128,256]{1,0:T(8,128)(2,1)S(1)}, u32[]{:S(2)}, u32[]{:S(2)}) collective-permute-start(bf16[128,256]{1,0:T(8,128)(2,1)S(1)} %get-tuple-element.24), channel_id=1, source_target_pairs={{0,4},{4,0},{8,12},{12,8},{16,20},{20,16},{24,28},{28,24},{1,5},{5... | collective-permute-start | bytes 196616 | tf_op jit(solution)/shard_map/ppermute | solution.py:296
  22.6 1.6 %collective-permute-start.4 = (bf16[128,256]{1,0:T(8,128)(2,1)S(1)}, bf16[128,256]{1,0:T(8,128)(2,1)S(1)}, u32[]{:S(2)}, u32[]{:S(2)}) collective-permute-start(bf16[128,256]{1,0:T(8,128)(2,1)S(1)} %get-tuple-element.25), channel_id=1, source_target_pairs={{0,8},{4,12},{8,0},{12,4},{16,24},{20,28},{24,16},{28,20},{1,9},{5... | collective-permute-start | bytes 196616 | tf_op jit(solution)/shard_map/ppermute | solution.py:296
  24.2 0.0 collective-permute-done.6
  24.2 0.1 collective-permute-start.5
  24.3 0.0 collective-permute-done.7
  24.3 0.0 collective-permute-done.8
  24.3 3.0 %collective-permute-start.9 = (bf16[128,256]{1,0:T(8,128)(2,1)S(1)}, bf16[128,256]{1,0:T(8,128)(2,1)S(1)}, u32[]{:S(2)}, u32[]{:S(2)}) collective-permute-start(bf16[128,256]{1,0:T(8,128)(2,1)S(1)} %add_convert_fusion), channel_id=1, source_target_pairs={{0,16},{4,20},{8,24},{12,28},{16,0},{20,4},{24,8},{28,12},{1,17},{... | collective-permute-start | bytes 196616 | tf_op jit(solution)/shard_map/ppermute | solution.py:296
  27.3 0.5 %sigma_own.1 = f32[128,256]{1,0:T(8,128)S(1)} custom-call(s32[40,128]{1,0:T(8,128)S(1)} %get-tuple-element.18.alpha_ref, bf16[5120,256]{1,0:T(8,128)(2,1)S(1)} %get-tuple-element.22.lifted, f32[128,256]{1,0:T(8,128)S(1)} %get-tuple-element.23.same), custom_call_target="tpu_custom_call" | custom-call | flops 335544320 | tf_op jit(solution)/shard_map/sigma_own/pallas_call | solution.py:313
  27.8 0.0 collective-permute-done.3
  27.8 0.0 collective-permute-done.4
  27.8 1.5 %collective-permute-done.5 = bf16[128,256]{1,0:T(8,128)(2,1)S(1)} collective-permute-done((bf16[128,256]{1,0:T(8,128)(2,1)S(1)}, bf16[128,256]{1,0:T(8,128)(2,1)S(1)}, u32[]{:S(2)}, u32[]{:S(2)}) %collective-permute-start.5) | collective-permute-done | bytes 65568 | tf_op jit(solution)/shard_map/ppermute | solution.py:296
  29.3 0.2 collective-permute-done.9
  29.6 0.7 %convert_add_fusion = f32[128,256]{1,0:T(8,128)} fusion(bf16[128,256]{1,0:T(8,128)(2,1)S(1)} %collective-permute-done.9, bf16[128,256]{1,0:T(8,128)(2,1)S(1)} %collective-permute-done.5, bf16[128,256]{1,0:T(8,128)(2,1)S(1)} %collective-permute-done.4, f32[128,256]{1,0:T(8,128)S(1)} %sigma_own.1, bf16[128,256]{1,0:T(8,128)(2,1)S(1)} %collective-permute-done.3), kind=kLoop, calls=%fused_computation | loop fusion | flops 262144 | bytes 524288 | tf_op jit(solution)/shard_map/add | solution.py:327
  (1 shorter events, 0.0 us)
Async XLA Ops:
  0.9 5.5 %collective-permute-start = (bf16[128,256]{1,0:T(8,128)(2,1)S(1)}, bf16[128,256]{1,0:T(8,128)(2,1)S(1)}, u32[]{:S(2)}, u32[]{:S(2)}) collective-permute-start(bf16[128,256]{1,0:T(8,128)(2,1)S(1)} %convert_element_type.30.rest_0_), channel_id=1, source_target_pairs={{0,1},{1,0},{2,3},{3,2},{4,5},{5,4},{6,7},{7,6},{8,9},{9,8},{10,11... | collective-permute-start | bytes 196616 | tf_op jit(solution)/shard_map/ppermute | solution.py:225
  1.4 6.7 %collective-permute-start.2 = (bf16[128,256]{1,0:T(8,128)(2,1)S(1)}, bf16[128,256]{1,0:T(8,128)(2,1)S(1)}, u32[]{:S(2)}, u32[]{:S(2)}) collective-permute-start(bf16[128,256]{1,0:T(8,128)(2,1)S(1)} %convert_element_type.30.rest_0_), channel_id=1, source_target_pairs={{0,3},{1,2},{2,1},{3,0},{4,7},{5,6},{6,5},{7,4},{8,11},{9,10},{10,... | collective-permute-start | bytes 196616 | tf_op jit(solution)/shard_map/ppermute | solution.py:225
  4.0 4.3 %collective-permute-start.1 = (bf16[128,256]{1,0:T(8,128)(2,1)S(1)}, bf16[128,256]{1,0:T(8,128)(2,1)S(1)}, u32[]{:S(2)}, u32[]{:S(2)}) collective-permute-start(bf16[128,256]{1,0:T(8,128)(2,1)S(1)} %convert_element_type.30.rest_0_), channel_id=1, source_target_pairs={{0,2},{1,3},{2,0},{3,1},{4,6},{5,7},{6,4},{7,5},{8,10},{9,11},{10,... | collective-permute-start | bytes 196616 | tf_op jit(solution)/shard_map/ppermute | solution.py:225
  15.9 8.2 %collective-permute-start.6 = (bf16[128,256]{1,0:T(8,128)(2,1)S(1)}, bf16[128,256]{1,0:T(8,128)(2,1)S(1)}, u32[]{:S(2)}, u32[]{:S(2)}) collective-permute-start(bf16[128,256]{1,0:T(8,128)(2,1)S(1)} %get-tuple-element.28), channel_id=1, source_target_pairs={{0,12},{4,8},{8,4},{12,0},{16,28},{20,24},{24,20},{28,16},{1,13},{... | collective-permute-start | bytes 196616 | tf_op jit(solution)/shard_map/ppermute | solution.py:296
  18.9 5.4 %collective-permute-start.7 = (bf16[128,256]{1,0:T(8,128)(2,1)S(1)}, bf16[128,256]{1,0:T(8,128)(2,1)S(1)}, u32[]{:S(2)}, u32[]{:S(2)}) collective-permute-start(bf16[128,256]{1,0:T(8,128)(2,1)S(1)} %get-tuple-element.29), channel_id=1, source_target_pairs={{0,8},{4,12},{8,0},{12,4},{16,24},{20,28},{24,16},{28,20},{1,9},{5... | collective-permute-start | bytes 196616 | tf_op jit(solution)/shard_map/ppermute | solution.py:296
  19.3 5.0 %collective-permute-start.8 = (bf16[128,256]{1,0:T(8,128)(2,1)S(1)}, bf16[128,256]{1,0:T(8,128)(2,1)S(1)}, u32[]{:S(2)}, u32[]{:S(2)}) collective-permute-start(bf16[128,256]{1,0:T(8,128)(2,1)S(1)} %get-tuple-element.30), channel_id=1, source_target_pairs={{0,4},{4,0},{8,12},{12,8},{16,20},{20,16},{24,28},{28,24},{1,5},{5... | collective-permute-start | bytes 196616 | tf_op jit(solution)/shard_map/ppermute | solution.py:296
  20.7 7.1 %collective-permute-start.3 = (bf16[128,256]{1,0:T(8,128)(2,1)S(1)}, bf16[128,256]{1,0:T(8,128)(2,1)S(1)}, u32[]{:S(2)}, u32[]{:S(2)}) collective-permute-start(bf16[128,256]{1,0:T(8,128)(2,1)S(1)} %get-tuple-element.24), channel_id=1, source_target_pairs={{0,4},{4,0},{8,12},{12,8},{16,20},{20,16},{24,28},{28,24},{1,5},{5... | collective-permute-start | bytes 196616 | tf_op jit(solution)/shard_map/ppermute | solution.py:296
  22.6 5.2 %collective-permute-start.4 = (bf16[128,256]{1,0:T(8,128)(2,1)S(1)}, bf16[128,256]{1,0:T(8,128)(2,1)S(1)}, u32[]{:S(2)}, u32[]{:S(2)}) collective-permute-start(bf16[128,256]{1,0:T(8,128)(2,1)S(1)} %get-tuple-element.25), channel_id=1, source_target_pairs={{0,8},{4,12},{8,0},{12,4},{16,24},{20,28},{24,16},{28,20},{1,9},{5... | collective-permute-start | bytes 196616 | tf_op jit(solution)/shard_map/ppermute | solution.py:296
  24.2 5.2 %collective-permute-start.5 = (bf16[128,256]{1,0:T(8,128)(2,1)S(1)}, bf16[128,256]{1,0:T(8,128)(2,1)S(1)}, u32[]{:S(2)}, u32[]{:S(2)}) collective-permute-start(bf16[128,256]{1,0:T(8,128)(2,1)S(1)} %get-tuple-element.26), channel_id=1, source_target_pairs={{0,12},{4,8},{8,4},{12,0},{16,28},{20,24},{24,20},{28,16},{1,13},{... | collective-permute-start | bytes 196616 | tf_op jit(solution)/shard_map/ppermute | solution.py:296
  24.3 5.2 %collective-permute-start.9 = (bf16[128,256]{1,0:T(8,128)(2,1)S(1)}, bf16[128,256]{1,0:T(8,128)(2,1)S(1)}, u32[]{:S(2)}, u32[]{:S(2)}) collective-permute-start(bf16[128,256]{1,0:T(8,128)(2,1)S(1)} %add_convert_fusion), channel_id=1, source_target_pairs={{0,16},{4,20},{8,24},{12,28},{16,0},{20,4},{24,8},{28,12},{1,17},{... | collective-permute-start | bytes 196616 | tf_op jit(solution)/shard_map/ppermute | solution.py:296

commit v8 on v7

--- a/solution.py
+++ b/solution.py
@@ -14,20 +14,39 @@
 NT = (((1,), (1,)), ((), ()))
 
 
-def index_kernel(sizes, *refs):
-    rows, cols, nexc, depth, tiles, pairs = sizes
-    sources, (beta_ref, slot_ref, alpha_ref, weights_ref) = refs[:8], refs[8:12]
-    staged, (table, turned, arrived) = refs[12:20], refs[20:]
+def stage_kernel(count, *refs):
+    sources, (civec_ref, *staged) = refs[: count + 1], refs[count + 1 : 2 * count + 2]
+    landing, arrived = refs[2 * count + 2 :]
     copies = [
         pltpu.make_async_copy(source, target, arrived.at[n])
-        for n, (source, target) in enumerate(zip(sources, staged))
+        for n, (source, target) in enumerate(zip(sources, [landing, *staged]))
     ]
     for copy in copies:
         copy.start()
-    for copy in copies:
+    copies[0].wait()
+    civec_ref[...] = landing[...].astype(jnp.bfloat16)
+    for copy in copies[1:]:
         copy.wait()
-    beta_target, beta_pair, beta_sign, alpha_target, alpha_pair, alpha_sign = staged[:6]
-    one_body, integrals = staged[6:]
+
+
+def index_kernel(
+    sizes,
+    beta_target,
+    beta_pair,
+    beta_sign,
+    alpha_target,
+    alpha_pair,
+    alpha_sign,
+    one_body,
+    integrals,
+    beta_ref,
+    slot_ref,
+    alpha_ref,
+    weights_ref,
+    table,
+    turned,
+):
+    rows, cols, nexc, depth, tiles, pairs = sizes
     bf16, f32 = jnp.bfloat16, jnp.float32
     per_tile = LANES // GROUP
     lane = lax.broadcasted_iota(jnp.int32, (8, LANES), 1)
@@ -220,15 +239,6 @@
     chunks = lax.axis_size("beta")
     bf16 = jnp.bfloat16
 
-    civec_bf = ci_vector.astype(bf16)
-    gathered = [civec_bf] + [
-        lax.ppermute(civec_bf, "beta", [(d, d ^ s) for d in range(chunks)])
-        for s in range(1, chunks)
-    ]
-
-    depth = nexc + 8
-    tiles = -(-cols // (2 * GROUP)) * 2
-    vmem = pl.BlockSpec(memory_space=pltpu.VMEM)
     lists = (
         beta_target,
         beta_pair,
@@ -239,6 +249,26 @@
         one_body.reshape(1, pairs),
         pair_integrals,
     )
+    vmem = pl.BlockSpec(memory_space=pltpu.VMEM)
+    civec_bf, *lists = pl.pallas_call(
+        functools.partial(stage_kernel, len(lists)),
+        out_shape=[pltpu.VMEM((rows, cols), bf16)] + [pltpu.VMEM(x.shape, x.dtype) for x in lists],
+        in_specs=[pl.BlockSpec(memory_space=pltpu.HBM)] * (1 + len(lists)),
+        out_specs=[vmem] * (1 + len(lists)),
+        scratch_shapes=[
+            pltpu.VMEM((rows, cols), jnp.float32),
+            pltpu.SemaphoreType.DMA((1 + len(lists),)),
+        ],
+        compiler_params=pltpu.CompilerParams(vmem_limit_bytes=4 * 1024 * 1024),
+        name="stage",
+    )(*[pltpu.with_memory_space_constraint(x, pltpu.HBM) for x in (ci_vector, *lists)])
+    gathered = [civec_bf] + [
+        lax.ppermute(civec_bf, "beta", [(d, d ^ s) for d in range(chunks)])
+        for s in range(1, chunks)
+    ]
+
+    depth = nexc + 8
+    tiles = -(-cols // (2 * GROUP)) * 2
     beta_code, beta_slot, alpha_code, weights = pl.pallas_call(
         functools.partial(index_kernel, (rows, cols, nexc, depth, tiles, pairs)),
         out_shape=[
@@ -247,20 +277,18 @@
             pltpu.VMEM((rows * nexc // LANES, LANES), jnp.int32),
             pltpu.VMEM((rows * depth, LANES), bf16),
         ],
-        in_specs=[pl.BlockSpec(memory_space=pltpu.HBM)] * 8,
+        in_specs=[vmem] * 8,
         out_specs=[vmem] * 4,
-        scratch_shapes=[pltpu.VMEM(x.shape, x.dtype) for x in lists]
-        + [
+        scratch_shapes=[
             pltpu.VMEM((LANES, LANES), jnp.float32),
             pltpu.VMEM((tiles * GROUP, LANES), jnp.float32),
-            pltpu.SemaphoreType.DMA((len(lists),)),
         ],
         cost_estimate=pl.CostEstimate(
             flops=4 * rows * depth * LANES * LANES, bytes_accessed=0, transcendentals=0
         ),
         compiler_params=pltpu.CompilerParams(vmem_limit_bytes=16 * 1024 * 1024),
         name="index_lists",
-    )(*[pltpu.with_memory_space_constraint(x, pltpu.HBM) for x in lists])
+    )(*lists)
 
     stride = rows + 4
     early = pl.pallas_call(

time: 30.4 us -> 30.5 us (level)
  waiting for transfers between devices: 1.94 us -> 3.19 us
  other arithmetic: 1.64 us -> 0.73 us
  starting transfers between devices: 13.3 us -> 12.9 us
    pallas_call x0 -> x1, Pallas kernels: none -> 1.01 us  [shards(): pl.pallas_call(functools.partial(stage_kernel, len(lists)), out_shape=[pl...]
    ppermute x3, waiting for transfers between devices: 0.19 us -> 1.14 us  [shards(): lax.ppermute(civec_bf, 'beta', [(d, d ^ s) for d in range(chunks)])]
    pallas_call x1, Pallas kernels: 2.35 us -> 1.4 us  [shards(): pl.pallas_call(functools.partial(index_kernel, (rows, cols, nexc, depth,...]
    convert_element_type x1 -> x0, other arithmetic: 0.91 us -> none  [shards(): civec_bf = ci_vector.astype(bf16)]
    ppermute x7, starting transfers between devices: 10.1 us -> 9.76 us  [send(): return lax.ppermute(value, 'alpha', [(d, d ^ s) for d in range(blocks)])]
  transfers between devices with their start and end apart: 10 -> 10, of which waited for: 3 -> 3; matrix products, arithmetic and copies ran while one was open for 0% -> 0% of each run, Pallas kernels for 19% -> 16%
where the time goes in v8:
time: 30.5 us; the launch traced here: 30.3 us
  Pallas kernels  13.4 us (44%)
  starting transfers between devices  12.9 us (42%)
  waiting for transfers between devices  3.19 us (10%)
  other arithmetic  0.73 us (2%)
    ppermute x7, starting transfers between devices, send(): return lax.ppermute(value, 'alpha', [(d, d ^ s) for d in range(blocks)])  9.76 us
    pallas_call x1, Pallas kernels, shards(): pl.pallas_call(functools.partial(far_kernel, sizes), out_shape=[jax.Shape...  7.63 us
    ppermute x3, starting transfers between devices, shards(): lax.ppermute(civec_bf, 'beta', [(d, d ^ s) for d in range(chunks)])  3.17 us
    ppermute x7, waiting for transfers between devices, send(): return lax.ppermute(value, 'alpha', [(d, d ^ s) for d in range(blocks)])  2.05 us
    pallas_call x1, Pallas kernels, shards(): pl.pallas_call(functools.partial(early_kernel, cols), out_shape=pltpu.VME...  1.65 us
    pallas_call x1, Pallas kernels, shards(): pl.pallas_call(functools.partial(index_kernel, (rows, cols, nexc, depth,...  1.4 us
    pallas_call x1, Pallas kernels, shards(): pl.pallas_call(functools.partial(near_kernel, sizes), out_shape=[block] *...  1.18 us
    ppermute x3, waiting for transfers between devices, shards(): lax.ppermute(civec_bf, 'beta', [(d, d ^ s) for d in range(chunks)])  1.14 us
  transfers between devices with their start and end apart: 10, of which 3 were waited for; matrix products, arithmetic and copies ran while one was open for 0% of the time, Pallas kernels for 16%

profile of v8, /device:TPU:0, one launch (start us, length us, event | category | flops | bytes accessed | tf_op | source)
XLA Modules:
  0.0 30.3 jit_solution(6715092604787143496)
XLA Ops:
  0.0 1.0 %stage.1 = (bf16[128,256]{1,0:T(8,128)(2,1)S(1)}, s32[40,256]{1,0:T(8,128)S(1)}, s32[40,256]{1,0:T(8,128)S(1)}, s32[40,256]{1,0:T(8,128)S(1)}, s32[40,128]{1,0:T...) custom-call(f32[128,256]{1,0:T(8,128)} %refs_0_.1, ...), custom_call_target="tpu_custom_call" | custom-call | tf_op jit(solution)/shard_map/stage/pallas_call | solution.py:253
  1.0 0.5 %collective-permute-start = (bf16[128,256]{1,0:T(8,128)(2,1)S(1)}, bf16[128,256]{1,0:T(8,128)(2,1)S(1)}, u32[]{:S(2)}, u32[]{:S(2)}) collective-permute-start(bf16[128,256]{1,0:T(8,128)(2,1)S(1)} %get-tuple-element.39.rest_0_), channel_id=1, source_target_pairs={{0,1},{1,0},{2,3},{3,2},{4,5},{5,4},{6,7},{7,6},{8,9},{9,8},{10,11... | collective-permute-start | bytes 196616 | tf_op jit(solution)/shard_map/ppermute | solution.py:266
  1.5 2.6 %collective-permute-start.2 = (bf16[128,256]{1,0:T(8,128)(2,1)S(1)}, bf16[128,256]{1,0:T(8,128)(2,1)S(1)}, u32[]{:S(2)}, u32[]{:S(2)}) collective-permute-start(bf16[128,256]{1,0:T(8,128)(2,1)S(1)} %get-tuple-element.39.rest_0_), channel_id=1, source_target_pairs={{0,3},{1,2},{2,1},{3,0},{4,7},{5,6},{6,5},{7,4},{8,11},{9,10},{10,... | collective-permute-start | bytes 196616 | tf_op jit(solution)/shard_map/ppermute | solution.py:266
  4.1 0.0 collective-permute-start.1
  4.2 1.4 %index_lists.1 = (s32[86,128]{1,0:T(8,128)S(1)}, s32[128,128]{1,0:T(8,128)S(1)}, s32[40,128]{1,0:T(8,128)S(1)}, bf16[6144,128]{1,0:T(8,128)(2,1)S(1)}) custom-call(s32[40,256]{1,0:T(8,128)S(1)} %get-tuple-element.27.beta_target, s32[40,256]{1,0:T(8,128)S(1)} %get-tuple-element.28.beta_pair, s32[40,256]{1,0:T(8,128)S(1)} %get-tuple-element.29.beta_sign, ...), custom_call_target="tpu_custom_call" | custom-call | flops 402653184 | tf_op jit(solution)/shard_map/index_lists/pallas_call | solution.py:272
  5.6 0.0 collective-permute-done.rest_1_
  5.6 1.7 %gather_early.1.early_ref = f32[43,128,256]{2,1,0:T(8,128)S(1)} custom-call(s32[86,128]{1,0:T(8,128)S(1)} %get-tuple-element.36.beta_ref, bf16[128,256]{1,0:T(8,128)(2,1)S(1)} %get-tuple-element.39.rest_0_, bf16[128,256]{1,0:T(8,128)(2,1)S(1)} %collective-permute-done.rest_1_), custom_call_target="tpu_custom_call" | custom-call | flops 1442840576 | tf_op jit(solution)/shard_map/gather_early/pallas_call | solution.py:294
  7.3 0.0 collective-permute-done.2.rest_1_
  7.3 1.1 %collective-permute-done.1.rest_0_ = bf16[128,256]{1,0:T(8,128)(2,1)S(1)} collective-permute-done((bf16[128,256]{1,0:T(8,128)(2,1)S(1)}, bf16[128,256]{1,0:T(8,128)(2,1)S(1)}, u32[]{:S(2)}, u32[]{:S(2)}) %collective-permute-start.1) | collective-permute-done | bytes 65568 | tf_op jit(solution)/shard_map/ppermute | solution.py:266
  8.4 7.6 %sigma_far.1 = (bf16[5120,256]{1,0:T(8,128)(2,1)S(1)}, f32[128,256]{1,0:T(8,128)S(1)}, bf16[128,256]{1,0:T(8,128)(2,1)S(1)}, bf16[128,256]{1,0:T(8,128)(2,1)S(1)...) custom-call(s32[86,128]{1,0:T(8,128)S(1)} %get-tuple-element.36.beta_ref, ...), custom_call_target="tpu_custom_call" | custom-call | tf_op jit(solution)/shard_map/sigma_far/pallas_call | solution.py:308
  16.1 2.6 %collective-permute-start.6 = (bf16[128,256]{1,0:T(8,128)(2,1)S(1)}, bf16[128,256]{1,0:T(8,128)(2,1)S(1)}, u32[]{:S(2)}, u32[]{:S(2)}) collective-permute-start(bf16[128,256]{1,0:T(8,128)(2,1)S(1)} %get-tuple-element.46), channel_id=1, source_target_pairs={{0,12},{4,8},{8,4},{12,0},{16,28},{20,24},{24,20},{28,16},{1,13},{... | collective-permute-start | bytes 196616 | tf_op jit(solution)/shard_map/ppermute | solution.py:324
  18.7 0.4 %collective-permute-start.7 = (bf16[128,256]{1,0:T(8,128)(2,1)S(1)}, bf16[128,256]{1,0:T(8,128)(2,1)S(1)}, u32[]{:S(2)}, u32[]{:S(2)}) collective-permute-start(bf16[128,256]{1,0:T(8,128)(2,1)S(1)} %get-tuple-element.47), channel_id=1, source_target_pairs={{0,8},{4,12},{8,0},{12,4},{16,24},{20,28},{24,16},{28,20},{1,9},{5... | collective-permute-start | bytes 196616 | tf_op jit(solution)/shard_map/ppermute | solution.py:324
  19.1 0.5 %collective-permute-start.8 = (bf16[128,256]{1,0:T(8,128)(2,1)S(1)}, bf16[128,256]{1,0:T(8,128)(2,1)S(1)}, u32[]{:S(2)}, u32[]{:S(2)}) collective-permute-start(bf16[128,256]{1,0:T(8,128)(2,1)S(1)} %get-tuple-element.48), channel_id=1, source_target_pairs={{0,4},{4,0},{8,12},{12,8},{16,20},{20,16},{24,28},{28,24},{1,5},{5... | collective-permute-start | bytes 196616 | tf_op jit(solution)/shard_map/ppermute | solution.py:324
  19.6 1.2 %sigma_near.1 = (bf16[128,256]{1,0:T(8,128)(2,1)S(1)}, bf16[128,256]{1,0:T(8,128)(2,1)S(1)}, bf16[128,256]{1,0:T(8,128)(2,1)S(1)}) custom-call(s32[40,128]{1,0:T(8,128)S(1)} %get-tuple-element.35.alpha_ref, bf16[5120,256]{1,0:T(8,128)(2,1)S(1)} %get-tuple-element.40.lifted), custom_call_target="tpu_custom_call" | custom-call | flops 1006632960 | tf_op jit(solution)/shard_map/sigma_near/pallas_call | solution.py:330
  20.8 1.6 %collective-permute-start.3 = (bf16[128,256]{1,0:T(8,128)(2,1)S(1)}, bf16[128,256]{1,0:T(8,128)(2,1)S(1)}, u32[]{:S(2)}, u32[]{:S(2)}) collective-permute-start(bf16[128,256]{1,0:T(8,128)(2,1)S(1)} %get-tuple-element.42), channel_id=1, source_target_pairs={{0,4},{4,0},{8,12},{12,8},{16,20},{20,16},{24,28},{28,24},{1,5},{5... | collective-permute-start | bytes 196616 | tf_op jit(solution)/shard_map/ppermute | solution.py:324
  22.4 1.6 %collective-permute-start.4 = (bf16[128,256]{1,0:T(8,128)(2,1)S(1)}, bf16[128,256]{1,0:T(8,128)(2,1)S(1)}, u32[]{:S(2)}, u32[]{:S(2)}) collective-permute-start(bf16[128,256]{1,0:T(8,128)(2,1)S(1)} %get-tuple-element.43), channel_id=1, source_target_pairs={{0,8},{4,12},{8,0},{12,4},{16,24},{20,28},{24,16},{28,20},{1,9},{5... | collective-permute-start | bytes 196616 | tf_op jit(solution)/shard_map/ppermute | solution.py:324
  24.0 0.0 collective-permute-done.6
  24.0 0.4 %collective-permute-start.5 = (bf16[128,256]{1,0:T(8,128)(2,1)S(1)}, bf16[128,256]{1,0:T(8,128)(2,1)S(1)}, u32[]{:S(2)}, u32[]{:S(2)}) collective-permute-start(bf16[128,256]{1,0:T(8,128)(2,1)S(1)} %get-tuple-element.44), channel_id=1, source_target_pairs={{0,12},{4,8},{8,4},{12,0},{16,28},{20,24},{24,20},{28,16},{1,13},{... | collective-permute-start | bytes 196616 | tf_op jit(solution)/shard_map/ppermute | solution.py:324
  24.4 0.0 collective-permute-done.7
  24.4 0.0 collective-permute-done.8
  24.4 2.7 %collective-permute-start.9 = (bf16[128,256]{1,0:T(8,128)(2,1)S(1)}, bf16[128,256]{1,0:T(8,128)(2,1)S(1)}, u32[]{:S(2)}, u32[]{:S(2)}) collective-permute-start(bf16[128,256]{1,0:T(8,128)(2,1)S(1)} %add_convert_fusion), channel_id=1, source_target_pairs={{0,16},{4,20},{8,24},{12,28},{16,0},{20,4},{24,8},{28,12},{1,17},{... | collective-permute-start | bytes 196616 | tf_op jit(solution)/shard_map/ppermute | solution.py:324
  27.1 0.5 %sigma_own.1 = f32[128,256]{1,0:T(8,128)S(1)} custom-call(s32[40,128]{1,0:T(8,128)S(1)} %get-tuple-element.35.alpha_ref, bf16[5120,256]{1,0:T(8,128)(2,1)S(1)} %get-tuple-element.40.lifted, f32[128,256]{1,0:T(8,128)S(1)} %get-tuple-element.41.same), custom_call_target="tpu_custom_call" | custom-call | flops 335544320 | tf_op jit(solution)/shard_map/sigma_own/pallas_call | solution.py:341
  27.6 0.0 collective-permute-done.3
  27.6 0.0 collective-permute-done.4
  27.6 1.5 %collective-permute-done.5 = bf16[128,256]{1,0:T(8,128)(2,1)S(1)} collective-permute-done((bf16[128,256]{1,0:T(8,128)(2,1)S(1)}, bf16[128,256]{1,0:T(8,128)(2,1)S(1)}, u32[]{:S(2)}, u32[]{:S(2)}) %collective-permute-start.5) | collective-permute-done | bytes 65568 | tf_op jit(solution)/shard_map/ppermute | solution.py:324
  29.1 0.5 %collective-permute-done.9 = bf16[128,256]{1,0:T(8,128)(2,1)S(1)} collective-permute-done((bf16[128,256]{1,0:T(8,128)(2,1)S(1)}, bf16[128,256]{1,0:T(8,128)(2,1)S(1)}, u32[]{:S(2)}, u32[]{:S(2)}) %collective-permute-start.9) | collective-permute-done | bytes 65568 | tf_op jit(solution)/shard_map/ppermute | solution.py:324
  29.6 0.7 %convert_add_fusion = f32[128,256]{1,0:T(8,128)} fusion(bf16[128,256]{1,0:T(8,128)(2,1)S(1)} %collective-permute-done.9, bf16[128,256]{1,0:T(8,128)(2,1)S(1)} %collective-permute-done.5, bf16[128,256]{1,0:T(8,128)(2,1)S(1)} %collective-permute-done.4, f32[128,256]{1,0:T(8,128)S(1)} %sigma_own.1, bf16[128,256]{1,0:T(8,128)(2,1)S(1)} %collective-permute-done.3), kind=kLoop, calls=%fused_computation | loop fusion | flops 262144 | bytes 524288 | tf_op jit(solution)/shard_map/add | solution.py:355
  (1 shorter events, 0.0 us)
Async XLA Ops:
  1.0 4.6 %collective-permute-start = (bf16[128,256]{1,0:T(8,128)(2,1)S(1)}, bf16[128,256]{1,0:T(8,128)(2,1)S(1)}, u32[]{:S(2)}, u32[]{:S(2)}) collective-permute-start(bf16[128,256]{1,0:T(8,128)(2,1)S(1)} %get-tuple-element.39.rest_0_), channel_id=1, source_target_pairs={{0,1},{1,0},{2,3},{3,2},{4,5},{5,4},{6,7},{7,6},{8,9},{9,8},{10,11... | collective-permute-start | bytes 196616 | tf_op jit(solution)/shard_map/ppermute | solution.py:266
  1.5 5.7 %collective-permute-start.2 = (bf16[128,256]{1,0:T(8,128)(2,1)S(1)}, bf16[128,256]{1,0:T(8,128)(2,1)S(1)}, u32[]{:S(2)}, u32[]{:S(2)}) collective-permute-start(bf16[128,256]{1,0:T(8,128)(2,1)S(1)} %get-tuple-element.39.rest_0_), channel_id=1, source_target_pairs={{0,3},{1,2},{2,1},{3,0},{4,7},{5,6},{6,5},{7,4},{8,11},{9,10},{10,... | collective-permute-start | bytes 196616 | tf_op jit(solution)/shard_map/ppermute | solution.py:266
  4.1 4.3 %collective-permute-start.1 = (bf16[128,256]{1,0:T(8,128)(2,1)S(1)}, bf16[128,256]{1,0:T(8,128)(2,1)S(1)}, u32[]{:S(2)}, u32[]{:S(2)}) collective-permute-start(bf16[128,256]{1,0:T(8,128)(2,1)S(1)} %get-tuple-element.39.rest_0_), channel_id=1, source_target_pairs={{0,2},{1,3},{2,0},{3,1},{4,6},{5,7},{6,4},{7,5},{8,10},{9,11},{10,... | collective-permute-start | bytes 196616 | tf_op jit(solution)/shard_map/ppermute | solution.py:266
  16.1 7.9 %collective-permute-start.6 = (bf16[128,256]{1,0:T(8,128)(2,1)S(1)}, bf16[128,256]{1,0:T(8,128)(2,1)S(1)}, u32[]{:S(2)}, u32[]{:S(2)}) collective-permute-start(bf16[128,256]{1,0:T(8,128)(2,1)S(1)} %get-tuple-element.46), channel_id=1, source_target_pairs={{0,12},{4,8},{8,4},{12,0},{16,28},{20,24},{24,20},{28,16},{1,13},{... | collective-permute-start | bytes 196616 | tf_op jit(solution)/shard_map/ppermute | solution.py:324
  18.7 5.7 %collective-permute-start.7 = (bf16[128,256]{1,0:T(8,128)(2,1)S(1)}, bf16[128,256]{1,0:T(8,128)(2,1)S(1)}, u32[]{:S(2)}, u32[]{:S(2)}) collective-permute-start(bf16[128,256]{1,0:T(8,128)(2,1)S(1)} %get-tuple-element.47), channel_id=1, source_target_pairs={{0,8},{4,12},{8,0},{12,4},{16,24},{20,28},{24,16},{28,20},{1,9},{5... | collective-permute-start | bytes 196616 | tf_op jit(solution)/shard_map/ppermute | solution.py:324
  19.1 5.3 %collective-permute-start.8 = (bf16[128,256]{1,0:T(8,128)(2,1)S(1)}, bf16[128,256]{1,0:T(8,128)(2,1)S(1)}, u32[]{:S(2)}, u32[]{:S(2)}) collective-permute-start(bf16[128,256]{1,0:T(8,128)(2,1)S(1)} %get-tuple-element.48), channel_id=1, source_target_pairs={{0,4},{4,0},{8,12},{12,8},{16,20},{20,16},{24,28},{28,24},{1,5},{5... | collective-permute-start | bytes 196616 | tf_op jit(solution)/shard_map/ppermute | solution.py:324
  20.8 6.8 %collective-permute-start.3 = (bf16[128,256]{1,0:T(8,128)(2,1)S(1)}, bf16[128,256]{1,0:T(8,128)(2,1)S(1)}, u32[]{:S(2)}, u32[]{:S(2)}) collective-permute-start(bf16[128,256]{1,0:T(8,128)(2,1)S(1)} %get-tuple-element.42), channel_id=1, source_target_pairs={{0,4},{4,0},{8,12},{12,8},{16,20},{20,16},{24,28},{28,24},{1,5},{5... | collective-permute-start | bytes 196616 | tf_op jit(solution)/shard_map/ppermute | solution.py:324
  22.4 5.2 %collective-permute-start.4 = (bf16[128,256]{1,0:T(8,128)(2,1)S(1)}, bf16[128,256]{1,0:T(8,128)(2,1)S(1)}, u32[]{:S(2)}, u32[]{:S(2)}) collective-permute-start(bf16[128,256]{1,0:T(8,128)(2,1)S(1)} %get-tuple-element.43), channel_id=1, source_target_pairs={{0,8},{4,12},{8,0},{12,4},{16,24},{20,28},{24,16},{28,20},{1,9},{5... | collective-permute-start | bytes 196616 | tf_op jit(solution)/shard_map/ppermute | solution.py:324
  24.0 5.2 %collective-permute-start.5 = (bf16[128,256]{1,0:T(8,128)(2,1)S(1)}, bf16[128,256]{1,0:T(8,128)(2,1)S(1)}, u32[]{:S(2)}, u32[]{:S(2)}) collective-permute-start(bf16[128,256]{1,0:T(8,128)(2,1)S(1)} %get-tuple-element.44), channel_id=1, source_target_pairs={{0,12},{4,8},{8,4},{12,0},{16,28},{20,24},{24,20},{28,16},{1,13},{... | collective-permute-start | bytes 196616 | tf_op jit(solution)/shard_map/ppermute | solution.py:324
  24.4 5.2 %collective-permute-start.9 = (bf16[128,256]{1,0:T(8,128)(2,1)S(1)}, bf16[128,256]{1,0:T(8,128)(2,1)S(1)}, u32[]{:S(2)}, u32[]{:S(2)}) collective-permute-start(bf16[128,256]{1,0:T(8,128)(2,1)S(1)} %add_convert_fusion), channel_id=1, source_target_pairs={{0,16},{4,20},{8,24},{12,28},{16,0},{20,4},{24,8},{28,12},{1,17},{... | collective-permute-start | bytes 196616 | tf_op jit(solution)/shard_map/ppermute | solution.py:324

commit v9 on v8

--- a/solution.py
+++ b/solution.py
@@ -195,9 +195,12 @@
         for a in range(first, first + BATCH, 2):
             parts = []
             for m in range(2):
-                d = density[pl.ds(a + m, cols, stride=stride), :].T.astype(bf16)
+                d = density[pl.ds(a + m, cols, stride=stride), :]
                 u = weights[(a + m) * depth : (a + m + 1) * depth, :]
-                l = jnp.dot(u, d, preferred_element_type=f32)
+                if m and a % 4:
+                    l = lax.dot_general(u, d.astype(bf16), NT, preferred_element_type=f32)
+                else:
+                    l = jnp.dot(u, d.T.astype(bf16), preferred_element_type=f32)
                 same[a + m : a + m + 1, :] = l[nexc : nexc + 1] + l[nexc + 1 : nexc + 2]
                 parts.append(l[:nexc])
             lifted[a * nexc : (a + 2) * nexc, :] = jnp.concatenate(parts, axis=0).astype(bf16)

time: 30.5 us -> 30.3 us (level)
  no operation moved by 1% of the time
where the time goes in v9:
time: 30.3 us; the launch traced here: 30.2 us
  Pallas kernels  13.2 us (44%)
  starting transfers between devices  12.9 us (43%)
  waiting for transfers between devices  3.19 us (11%)
  other arithmetic  0.73 us (2%)
    ppermute x7, starting transfers between devices, send(): return lax.ppermute(value, 'alpha', [(d, d ^ s) for d in range(blocks)])  9.76 us
    pallas_call x1, Pallas kernels, shards(): pl.pallas_call(functools.partial(far_kernel, sizes), out_shape=[jax.Shape...  7.45 us
    ppermute x3, starting transfers between devices, shards(): lax.ppermute(civec_bf, 'beta', [(d, d ^ s) for d in range(chunks)])  3.17 us
    ppermute x7, waiting for transfers between devices, send(): return lax.ppermute(value, 'alpha', [(d, d ^ s) for d in range(blocks)])  2.05 us
    pallas_call x1, Pallas kernels, shards(): pl.pallas_call(functools.partial(early_kernel, cols), out_shape=pltpu.VME...  1.65 us
    pallas_call x1, Pallas kernels, shards(): pl.pallas_call(functools.partial(index_kernel, (rows, cols, nexc, depth,...  1.4 us
    pallas_call x1, Pallas kernels, shards(): pl.pallas_call(functools.partial(near_kernel, sizes), out_shape=[block] *...  1.19 us
    ppermute x3, waiting for transfers between devices, shards(): lax.ppermute(civec_bf, 'beta', [(d, d ^ s) for d in range(chunks)])  1.14 us
  transfers between devices with their start and end apart: 10, of which 3 were waited for; matrix products, arithmetic and copies ran while one was open for 0% of the time, Pallas kernels for 16%

profile of v9, /device:TPU:0, one launch (start us, length us, event | category | flops | bytes accessed | tf_op | source)
XLA Modules:
  0.0 30.2 jit_solution(40671123562070594)
XLA Ops:
  0.0 1.0 %stage.1 = (bf16[128,256]{1,0:T(8,128)(2,1)S(1)}, s32[40,256]{1,0:T(8,128)S(1)}, s32[40,256]{1,0:T(8,128)S(1)}, s32[40,256]{1,0:T(8,128)S(1)}, s32[40,128]{1,0:T...) custom-call(f32[128,256]{1,0:T(8,128)} %refs_0_.1, ...), custom_call_target="tpu_custom_call" | custom-call | tf_op jit(solution)/shard_map/stage/pallas_call | solution.py:256
  1.0 0.5 %collective-permute-start = (bf16[128,256]{1,0:T(8,128)(2,1)S(1)}, bf16[128,256]{1,0:T(8,128)(2,1)S(1)}, u32[]{:S(2)}, u32[]{:S(2)}) collective-permute-start(bf16[128,256]{1,0:T(8,128)(2,1)S(1)} %get-tuple-element.39.rest_0_), channel_id=1, source_target_pairs={{0,1},{1,0},{2,3},{3,2},{4,5},{5,4},{6,7},{7,6},{8,9},{9,8},{10,11... | collective-permute-start | bytes 196616 | tf_op jit(solution)/shard_map/ppermute | solution.py:269
  1.5 2.6 %collective-permute-start.2 = (bf16[128,256]{1,0:T(8,128)(2,1)S(1)}, bf16[128,256]{1,0:T(8,128)(2,1)S(1)}, u32[]{:S(2)}, u32[]{:S(2)}) collective-permute-start(bf16[128,256]{1,0:T(8,128)(2,1)S(1)} %get-tuple-element.39.rest_0_), channel_id=1, source_target_pairs={{0,3},{1,2},{2,1},{3,0},{4,7},{5,6},{6,5},{7,4},{8,11},{9,10},{10,... | collective-permute-start | bytes 196616 | tf_op jit(solution)/shard_map/ppermute | solution.py:269
  4.1 0.0 collective-permute-start.1
  4.2 1.4 %index_lists.1 = (s32[86,128]{1,0:T(8,128)S(1)}, s32[128,128]{1,0:T(8,128)S(1)}, s32[40,128]{1,0:T(8,128)S(1)}, bf16[6144,128]{1,0:T(8,128)(2,1)S(1)}) custom-call(s32[40,256]{1,0:T(8,128)S(1)} %get-tuple-element.27.beta_target, s32[40,256]{1,0:T(8,128)S(1)} %get-tuple-element.28.beta_pair, s32[40,256]{1,0:T(8,128)S(1)} %get-tuple-element.29.beta_sign, ...), custom_call_target="tpu_custom_call" | custom-call | flops 402653184 | tf_op jit(solution)/shard_map/index_lists/pallas_call | solution.py:275
  5.6 0.0 collective-permute-done.rest_1_
  5.6 1.7 %gather_early.1.early_ref = f32[43,128,256]{2,1,0:T(8,128)S(1)} custom-call(s32[86,128]{1,0:T(8,128)S(1)} %get-tuple-element.36.beta_ref, bf16[128,256]{1,0:T(8,128)(2,1)S(1)} %get-tuple-element.39.rest_0_, bf16[128,256]{1,0:T(8,128)(2,1)S(1)} %collective-permute-done.rest_1_), custom_call_target="tpu_custom_call" | custom-call | flops 1442840576 | tf_op jit(solution)/shard_map/gather_early/pallas_call | solution.py:297
  7.3 0.0 collective-permute-done.2.rest_1_
  7.3 1.1 %collective-permute-done.1.rest_0_ = bf16[128,256]{1,0:T(8,128)(2,1)S(1)} collective-permute-done((bf16[128,256]{1,0:T(8,128)(2,1)S(1)}, bf16[128,256]{1,0:T(8,128)(2,1)S(1)}, u32[]{:S(2)}, u32[]{:S(2)}) %collective-permute-start.1) | collective-permute-done | bytes 65568 | tf_op jit(solution)/shard_map/ppermute | solution.py:269
  8.4 7.5 %sigma_far.1 = (bf16[5120,256]{1,0:T(8,128)(2,1)S(1)}, f32[128,256]{1,0:T(8,128)S(1)}, bf16[128,256]{1,0:T(8,128)(2,1)S(1)}, bf16[128,256]{1,0:T(8,128)(2,1)S(1)...) custom-call(s32[86,128]{1,0:T(8,128)S(1)} %get-tuple-element.36.beta_ref, ...), custom_call_target="tpu_custom_call" | custom-call | tf_op jit(solution)/shard_map/sigma_far/pallas_call | solution.py:311
  15.9 2.6 %collective-permute-start.6 = (bf16[128,256]{1,0:T(8,128)(2,1)S(1)}, bf16[128,256]{1,0:T(8,128)(2,1)S(1)}, u32[]{:S(2)}, u32[]{:S(2)}) collective-permute-start(bf16[128,256]{1,0:T(8,128)(2,1)S(1)} %get-tuple-element.46), channel_id=1, source_target_pairs={{0,12},{4,8},{8,4},{12,0},{16,28},{20,24},{24,20},{28,16},{1,13},{... | collective-permute-start | bytes 196616 | tf_op jit(solution)/shard_map/ppermute | solution.py:327
  18.5 0.4 %collective-permute-start.7 = (bf16[128,256]{1,0:T(8,128)(2,1)S(1)}, bf16[128,256]{1,0:T(8,128)(2,1)S(1)}, u32[]{:S(2)}, u32[]{:S(2)}) collective-permute-start(bf16[128,256]{1,0:T(8,128)(2,1)S(1)} %get-tuple-element.47), channel_id=1, source_target_pairs={{0,8},{4,12},{8,0},{12,4},{16,24},{20,28},{24,16},{28,20},{1,9},{5... | collective-permute-start | bytes 196616 | tf_op jit(solution)/shard_map/ppermute | solution.py:327
  18.9 0.5 %collective-permute-start.8 = (bf16[128,256]{1,0:T(8,128)(2,1)S(1)}, bf16[128,256]{1,0:T(8,128)(2,1)S(1)}, u32[]{:S(2)}, u32[]{:S(2)}) collective-permute-start(bf16[128,256]{1,0:T(8,128)(2,1)S(1)} %get-tuple-element.48), channel_id=1, source_target_pairs={{0,4},{4,0},{8,12},{12,8},{16,20},{20,16},{24,28},{28,24},{1,5},{5... | collective-permute-start | bytes 196616 | tf_op jit(solution)/shard_map/ppermute | solution.py:327
  19.4 1.2 %sigma_near.1 = (bf16[128,256]{1,0:T(8,128)(2,1)S(1)}, bf16[128,256]{1,0:T(8,128)(2,1)S(1)}, bf16[128,256]{1,0:T(8,128)(2,1)S(1)}) custom-call(s32[40,128]{1,0:T(8,128)S(1)} %get-tuple-element.35.alpha_ref, bf16[5120,256]{1,0:T(8,128)(2,1)S(1)} %get-tuple-element.40.lifted), custom_call_target="tpu_custom_call" | custom-call | flops 1006632960 | tf_op jit(solution)/shard_map/sigma_near/pallas_call | solution.py:333
  20.6 1.6 %collective-permute-start.3 = (bf16[128,256]{1,0:T(8,128)(2,1)S(1)}, bf16[128,256]{1,0:T(8,128)(2,1)S(1)}, u32[]{:S(2)}, u32[]{:S(2)}) collective-permute-start(bf16[128,256]{1,0:T(8,128)(2,1)S(1)} %get-tuple-element.42), channel_id=1, source_target_pairs={{0,4},{4,0},{8,12},{12,8},{16,20},{20,16},{24,28},{28,24},{1,5},{5... | collective-permute-start | bytes 196616 | tf_op jit(solution)/shard_map/ppermute | solution.py:327
  22.2 1.6 %collective-permute-start.4 = (bf16[128,256]{1,0:T(8,128)(2,1)S(1)}, bf16[128,256]{1,0:T(8,128)(2,1)S(1)}, u32[]{:S(2)}, u32[]{:S(2)}) collective-permute-start(bf16[128,256]{1,0:T(8,128)(2,1)S(1)} %get-tuple-element.43), channel_id=1, source_target_pairs={{0,8},{4,12},{8,0},{12,4},{16,24},{20,28},{24,16},{28,20},{1,9},{5... | collective-permute-start | bytes 196616 | tf_op jit(solution)/shard_map/ppermute | solution.py:327
  23.8 0.0 collective-permute-done.6
  23.8 0.4 %collective-permute-start.5 = (bf16[128,256]{1,0:T(8,128)(2,1)S(1)}, bf16[128,256]{1,0:T(8,128)(2,1)S(1)}, u32[]{:S(2)}, u32[]{:S(2)}) collective-permute-start(bf16[128,256]{1,0:T(8,128)(2,1)S(1)} %get-tuple-element.44), channel_id=1, source_target_pairs={{0,12},{4,8},{8,4},{12,0},{16,28},{20,24},{24,20},{28,16},{1,13},{... | collective-permute-start | bytes 196616 | tf_op jit(solution)/shard_map/ppermute | solution.py:327
  24.2 0.0 collective-permute-done.7
  24.2 0.0 collective-permute-done.8
  24.2 2.7 %collective-permute-start.9 = (bf16[128,256]{1,0:T(8,128)(2,1)S(1)}, bf16[128,256]{1,0:T(8,128)(2,1)S(1)}, u32[]{:S(2)}, u32[]{:S(2)}) collective-permute-start(bf16[128,256]{1,0:T(8,128)(2,1)S(1)} %add_convert_fusion), channel_id=1, source_target_pairs={{0,16},{4,20},{8,24},{12,28},{16,0},{20,4},{24,8},{28,12},{1,17},{... | collective-permute-start | bytes 196616 | tf_op jit(solution)/shard_map/ppermute | solution.py:327
  26.9 0.5 %sigma_own.1 = f32[128,256]{1,0:T(8,128)S(1)} custom-call(s32[40,128]{1,0:T(8,128)S(1)} %get-tuple-element.35.alpha_ref, bf16[5120,256]{1,0:T(8,128)(2,1)S(1)} %get-tuple-element.40.lifted, f32[128,256]{1,0:T(8,128)S(1)} %get-tuple-element.41.same), custom_call_target="tpu_custom_call" | custom-call | flops 335544320 | tf_op jit(solution)/shard_map/sigma_own/pallas_call | solution.py:344
  27.4 0.0 collective-permute-done.3
  27.4 0.0 collective-permute-done.4
  27.4 1.5 %collective-permute-done.5 = bf16[128,256]{1,0:T(8,128)(2,1)S(1)} collective-permute-done((bf16[128,256]{1,0:T(8,128)(2,1)S(1)}, bf16[128,256]{1,0:T(8,128)(2,1)S(1)}, u32[]{:S(2)}, u32[]{:S(2)}) %collective-permute-start.5) | collective-permute-done | bytes 65568 | tf_op jit(solution)/shard_map/ppermute | solution.py:327
  29.0 0.5 %collective-permute-done.9 = bf16[128,256]{1,0:T(8,128)(2,1)S(1)} collective-permute-done((bf16[128,256]{1,0:T(8,128)(2,1)S(1)}, bf16[128,256]{1,0:T(8,128)(2,1)S(1)}, u32[]{:S(2)}, u32[]{:S(2)}) %collective-permute-start.9) | collective-permute-done | bytes 65568 | tf_op jit(solution)/shard_map/ppermute | solution.py:327
  29.5 0.7 %convert_add_fusion = f32[128,256]{1,0:T(8,128)} fusion(bf16[128,256]{1,0:T(8,128)(2,1)S(1)} %collective-permute-done.9, bf16[128,256]{1,0:T(8,128)(2,1)S(1)} %collective-permute-done.5, bf16[128,256]{1,0:T(8,128)(2,1)S(1)} %collective-permute-done.4, f32[128,256]{1,0:T(8,128)S(1)} %sigma_own.1, bf16[128,256]{1,0:T(8,128)(2,1)S(1)} %collective-permute-done.3), kind=kLoop, calls=%fused_computation | loop fusion | flops 262144 | bytes 524288 | tf_op jit(solution)/shard_map/add | solution.py:358
  (1 shorter events, 0.0 us)
Async XLA Ops:
  1.0 4.6 %collective-permute-start = (bf16[128,256]{1,0:T(8,128)(2,1)S(1)}, bf16[128,256]{1,0:T(8,128)(2,1)S(1)}, u32[]{:S(2)}, u32[]{:S(2)}) collective-permute-start(bf16[128,256]{1,0:T(8,128)(2,1)S(1)} %get-tuple-element.39.rest_0_), channel_id=1, source_target_pairs={{0,1},{1,0},{2,3},{3,2},{4,5},{5,4},{6,7},{7,6},{8,9},{9,8},{10,11... | collective-permute-start | bytes 196616 | tf_op jit(solution)/shard_map/ppermute | solution.py:269
  1.5 5.7 %collective-permute-start.2 = (bf16[128,256]{1,0:T(8,128)(2,1)S(1)}, bf16[128,256]{1,0:T(8,128)(2,1)S(1)}, u32[]{:S(2)}, u32[]{:S(2)}) collective-permute-start(bf16[128,256]{1,0:T(8,128)(2,1)S(1)} %get-tuple-element.39.rest_0_), channel_id=1, source_target_pairs={{0,3},{1,2},{2,1},{3,0},{4,7},{5,6},{6,5},{7,4},{8,11},{9,10},{10,... | collective-permute-start | bytes 196616 | tf_op jit(solution)/shard_map/ppermute | solution.py:269
  4.1 4.3 %collective-permute-start.1 = (bf16[128,256]{1,0:T(8,128)(2,1)S(1)}, bf16[128,256]{1,0:T(8,128)(2,1)S(1)}, u32[]{:S(2)}, u32[]{:S(2)}) collective-permute-start(bf16[128,256]{1,0:T(8,128)(2,1)S(1)} %get-tuple-element.39.rest_0_), channel_id=1, source_target_pairs={{0,2},{1,3},{2,0},{3,1},{4,6},{5,7},{6,4},{7,5},{8,10},{9,11},{10,... | collective-permute-start | bytes 196616 | tf_op jit(solution)/shard_map/ppermute | solution.py:269
  15.9 7.9 %collective-permute-start.6 = (bf16[128,256]{1,0:T(8,128)(2,1)S(1)}, bf16[128,256]{1,0:T(8,128)(2,1)S(1)}, u32[]{:S(2)}, u32[]{:S(2)}) collective-permute-start(bf16[128,256]{1,0:T(8,128)(2,1)S(1)} %get-tuple-element.46), channel_id=1, source_target_pairs={{0,12},{4,8},{8,4},{12,0},{16,28},{20,24},{24,20},{28,16},{1,13},{... | collective-permute-start | bytes 196616 | tf_op jit(solution)/shard_map/ppermute | solution.py:327
  18.5 5.7 %collective-permute-start.7 = (bf16[128,256]{1,0:T(8,128)(2,1)S(1)}, bf16[128,256]{1,0:T(8,128)(2,1)S(1)}, u32[]{:S(2)}, u32[]{:S(2)}) collective-permute-start(bf16[128,256]{1,0:T(8,128)(2,1)S(1)} %get-tuple-element.47), channel_id=1, source_target_pairs={{0,8},{4,12},{8,0},{12,4},{16,24},{20,28},{24,16},{28,20},{1,9},{5... | collective-permute-start | bytes 196616 | tf_op jit(solution)/shard_map/ppermute | solution.py:327
  18.9 5.3 %collective-permute-start.8 = (bf16[128,256]{1,0:T(8,128)(2,1)S(1)}, bf16[128,256]{1,0:T(8,128)(2,1)S(1)}, u32[]{:S(2)}, u32[]{:S(2)}) collective-permute-start(bf16[128,256]{1,0:T(8,128)(2,1)S(1)} %get-tuple-element.48), channel_id=1, source_target_pairs={{0,4},{4,0},{8,12},{12,8},{16,20},{20,16},{24,28},{28,24},{1,5},{5... | collective-permute-start | bytes 196616 | tf_op jit(solution)/shard_map/ppermute | solution.py:327
  20.6 6.8 %collective-permute-start.3 = (bf16[128,256]{1,0:T(8,128)(2,1)S(1)}, bf16[128,256]{1,0:T(8,128)(2,1)S(1)}, u32[]{:S(2)}, u32[]{:S(2)}) collective-permute-start(bf16[128,256]{1,0:T(8,128)(2,1)S(1)} %get-tuple-element.42), channel_id=1, source_target_pairs={{0,4},{4,0},{8,12},{12,8},{16,20},{20,16},{24,28},{28,24},{1,5},{5... | collective-permute-start | bytes 196616 | tf_op jit(solution)/shard_map/ppermute | solution.py:327
  22.2 5.2 %collective-permute-start.4 = (bf16[128,256]{1,0:T(8,128)(2,1)S(1)}, bf16[128,256]{1,0:T(8,128)(2,1)S(1)}, u32[]{:S(2)}, u32[]{:S(2)}) collective-permute-start(bf16[128,256]{1,0:T(8,128)(2,1)S(1)} %get-tuple-element.43), channel_id=1, source_target_pairs={{0,8},{4,12},{8,0},{12,4},{16,24},{20,28},{24,16},{28,20},{1,9},{5... | collective-permute-start | bytes 196616 | tf_op jit(solution)/shard_map/ppermute | solution.py:327
  23.8 5.2 %collective-permute-start.5 = (bf16[128,256]{1,0:T(8,128)(2,1)S(1)}, bf16[128,256]{1,0:T(8,128)(2,1)S(1)}, u32[]{:S(2)}, u32[]{:S(2)}) collective-permute-start(bf16[128,256]{1,0:T(8,128)(2,1)S(1)} %get-tuple-element.44), channel_id=1, source_target_pairs={{0,12},{4,8},{8,4},{12,0},{16,28},{20,24},{24,20},{28,16},{1,13},{... | collective-permute-start | bytes 196616 | tf_op jit(solution)/shard_map/ppermute | solution.py:327
  24.2 5.2 %collective-permute-start.9 = (bf16[128,256]{1,0:T(8,128)(2,1)S(1)}, bf16[128,256]{1,0:T(8,128)(2,1)S(1)}, u32[]{:S(2)}, u32[]{:S(2)}) collective-permute-start(bf16[128,256]{1,0:T(8,128)(2,1)S(1)} %add_convert_fusion), channel_id=1, source_target_pairs={{0,16},{4,20},{8,24},{12,28},{16,0},{20,4},{24,8},{28,12},{1,17},{... | collective-permute-start | bytes 196616 | tf_op jit(solution)/shard_map/ppermute | solution.py:327

commit v10 on v9

--- a/solution.py
+++ b/solution.py
@@ -149,7 +149,7 @@
 def early_kernel(cols, beta_ref, *rest):
     c_refs, early_ref = rest[:-1], rest[-1]
     for g in range(early_ref.shape[0]):
-        early_ref[g] = pick(g, cols, beta_ref, c_refs, 0, None)
+        early_ref[g] = pick(g, cols, beta_ref, c_refs, 0, None).astype(jnp.bfloat16)
 
 
 def far_kernel(sizes, beta_ref, slot_ref, alpha_ref, weights, early_ref, *rest):
@@ -162,7 +162,7 @@
     groups = early_ref.shape[0]
 
     for g in range(groups):
-        found = pick(g, cols, beta_ref, c_refs, EARLY, early_ref[g])
+        found = pick(g, cols, beta_ref, c_refs, EARLY, early_ref[g].astype(f32))
         picked[g] = found.astype(bf16)
 
     ids = lax.broadcasted_iota(jnp.int32, (LANES, LANES), 1) + 1
@@ -296,7 +296,7 @@
     stride = rows + 4
     early = pl.pallas_call(
         functools.partial(early_kernel, cols),
-        out_shape=pltpu.VMEM((tiles // 2, rows, 2 * LANES), jnp.float32),
+        out_shape=pltpu.VMEM((tiles // 2, rows, 2 * LANES), bf16),
         in_specs=[vmem] * (1 + EARLY),
         out_specs=vmem,
         compiler_params=pltpu.CompilerParams(vmem_limit_bytes=12 * 1024 * 1024),

time: 30.3 us -> 30.4 us (level)
  no operation moved by 1% of the time
where the time goes in v10:
time: 30.4 us; the launch traced here: 30.2 us
  Pallas kernels  13.3 us (44%)
  starting transfers between devices  12.9 us (42%)
  waiting for transfers between devices  3.17 us (10%)
  other arithmetic  0.73 us (2%)
    ppermute x7, starting transfers between devices, send(): return lax.ppermute(value, 'alpha', [(d, d ^ s) for d in range(blocks)])  9.77 us
    pallas_call x1, Pallas kernels, shards(): pl.pallas_call(functools.partial(far_kernel, sizes), out_shape=[jax.Shape...  7.54 us
    ppermute x3, starting transfers between devices, shards(): lax.ppermute(civec_bf, 'beta', [(d, d ^ s) for d in range(chunks)])  3.17 us
    ppermute x7, waiting for transfers between devices, send(): return lax.ppermute(value, 'alpha', [(d, d ^ s) for d in range(blocks)])  2.03 us
    pallas_call x1, Pallas kernels, shards(): pl.pallas_call(functools.partial(early_kernel, cols), out_shape=pltpu.VME...  1.66 us
    pallas_call x1, Pallas kernels, shards(): pl.pallas_call(functools.partial(index_kernel, (rows, cols, nexc, depth,...  1.4 us
    pallas_call x1, Pallas kernels, shards(): pl.pallas_call(functools.partial(near_kernel, sizes), out_shape=[block] *...  1.18 us
    ppermute x3, waiting for transfers between devices, shards(): lax.ppermute(civec_bf, 'beta', [(d, d ^ s) for d in range(chunks)])  1.13 us
  transfers between devices with their start and end apart: 10, of which 3 were waited for; matrix products, arithmetic and copies ran while one was open for 0% of the time, Pallas kernels for 16%

profile of v10, /device:TPU:0, one launch (start us, length us, event | category | flops | bytes accessed | tf_op | source)
XLA Modules:
  0.0 30.2 jit_solution(3966486537008262648)
XLA Ops:
  0.0 1.0 %stage.1 = (bf16[128,256]{1,0:T(8,128)(2,1)S(1)}, s32[40,256]{1,0:T(8,128)S(1)}, s32[40,256]{1,0:T(8,128)S(1)}, s32[40,256]{1,0:T(8,128)S(1)}, s32[40,128]{1,0:T...) custom-call(f32[128,256]{1,0:T(8,128)} %refs_0_.1, ...), custom_call_target="tpu_custom_call" | custom-call | tf_op jit(solution)/shard_map/stage/pallas_call | solution.py:256
  1.0 0.5 %collective-permute-start = (bf16[128,256]{1,0:T(8,128)(2,1)S(1)}, bf16[128,256]{1,0:T(8,128)(2,1)S(1)}, u32[]{:S(2)}, u32[]{:S(2)}) collective-permute-start(bf16[128,256]{1,0:T(8,128)(2,1)S(1)} %get-tuple-element.39.rest_0_), channel_id=1, source_target_pairs={{0,1},{1,0},{2,3},{3,2},{4,5},{5,4},{6,7},{7,6},{8,9},{9,8},{10,11... | collective-permute-start | bytes 196616 | tf_op jit(solution)/shard_map/ppermute | solution.py:269
  1.5 2.6 %collective-permute-start.2 = (bf16[128,256]{1,0:T(8,128)(2,1)S(1)}, bf16[128,256]{1,0:T(8,128)(2,1)S(1)}, u32[]{:S(2)}, u32[]{:S(2)}) collective-permute-start(bf16[128,256]{1,0:T(8,128)(2,1)S(1)} %get-tuple-element.39.rest_0_), channel_id=1, source_target_pairs={{0,3},{1,2},{2,1},{3,0},{4,7},{5,6},{6,5},{7,4},{8,11},{9,10},{10,... | collective-permute-start | bytes 196616 | tf_op jit(solution)/shard_map/ppermute | solution.py:269
  4.1 0.0 collective-permute-start.1
  4.2 1.4 %index_lists.1 = (s32[86,128]{1,0:T(8,128)S(1)}, s32[128,128]{1,0:T(8,128)S(1)}, s32[40,128]{1,0:T(8,128)S(1)}, bf16[6144,128]{1,0:T(8,128)(2,1)S(1)}) custom-call(s32[40,256]{1,0:T(8,128)S(1)} %get-tuple-element.27.beta_target, s32[40,256]{1,0:T(8,128)S(1)} %get-tuple-element.28.beta_pair, s32[40,256]{1,0:T(8,128)S(1)} %get-tuple-element.29.beta_sign, ...), custom_call_target="tpu_custom_call" | custom-call | flops 402653184 | tf_op jit(solution)/shard_map/index_lists/pallas_call | solution.py:275
  5.6 0.0 collective-permute-done.rest_1_
  5.6 1.7 %gather_early.1.early_ref = bf16[43,128,256]{2,1,0:T(8,128)(2,1)S(1)} custom-call(s32[86,128]{1,0:T(8,128)S(1)} %get-tuple-element.36.beta_ref, bf16[128,256]{1,0:T(8,128)(2,1)S(1)} %get-tuple-element.39.rest_0_, bf16[128,256]{1,0:T(8,128)(2,1)S(1)} %collective-permute-done.rest_1_), custom_call_target="tpu_custom_call" | custom-call | flops 1442840576 | tf_op jit(solution)/shard_map/gather_early/pallas_call | solution.py:297
  7.3 0.0 collective-permute-done.2.rest_1_
  7.3 1.1 %collective-permute-done.1.rest_0_ = bf16[128,256]{1,0:T(8,128)(2,1)S(1)} collective-permute-done((bf16[128,256]{1,0:T(8,128)(2,1)S(1)}, bf16[128,256]{1,0:T(8,128)(2,1)S(1)}, u32[]{:S(2)}, u32[]{:S(2)}) %collective-permute-start.1) | collective-permute-done | bytes 65568 | tf_op jit(solution)/shard_map/ppermute | solution.py:269
  8.4 7.5 %sigma_far.1 = (bf16[5120,256]{1,0:T(8,128)(2,1)S(1)}, f32[128,256]{1,0:T(8,128)S(1)}, bf16[128,256]{1,0:T(8,128)(2,1)S(1)}, bf16[128,256]{1,0:T(8,128)(2,1)S(1)...) custom-call(s32[86,128]{1,0:T(8,128)S(1)} %get-tuple-element.36.beta_ref, ...), custom_call_target="tpu_custom_call" | custom-call | tf_op jit(solution)/shard_map/sigma_far/pallas_call | solution.py:311
  16.0 2.6 %collective-permute-start.6 = (bf16[128,256]{1,0:T(8,128)(2,1)S(1)}, bf16[128,256]{1,0:T(8,128)(2,1)S(1)}, u32[]{:S(2)}, u32[]{:S(2)}) collective-permute-start(bf16[128,256]{1,0:T(8,128)(2,1)S(1)} %get-tuple-element.46), channel_id=1, source_target_pairs={{0,12},{4,8},{8,4},{12,0},{16,28},{20,24},{24,20},{28,16},{1,13},{... | collective-permute-start | bytes 196616 | tf_op jit(solution)/shard_map/ppermute | solution.py:327
  18.6 0.5 %collective-permute-start.7 = (bf16[128,256]{1,0:T(8,128)(2,1)S(1)}, bf16[128,256]{1,0:T(8,128)(2,1)S(1)}, u32[]{:S(2)}, u32[]{:S(2)}) collective-permute-start(bf16[128,256]{1,0:T(8,128)(2,1)S(1)} %get-tuple-element.47), channel_id=1, source_target_pairs={{0,8},{4,12},{8,0},{12,4},{16,24},{20,28},{24,16},{28,20},{1,9},{5... | collective-permute-start | bytes 196616 | tf_op jit(solution)/shard_map/ppermute | solution.py:327
  19.0 0.5 %collective-permute-start.8 = (bf16[128,256]{1,0:T(8,128)(2,1)S(1)}, bf16[128,256]{1,0:T(8,128)(2,1)S(1)}, u32[]{:S(2)}, u32[]{:S(2)}) collective-permute-start(bf16[128,256]{1,0:T(8,128)(2,1)S(1)} %get-tuple-element.48), channel_id=1, source_target_pairs={{0,4},{4,0},{8,12},{12,8},{16,20},{20,16},{24,28},{28,24},{1,5},{5... | collective-permute-start | bytes 196616 | tf_op jit(solution)/shard_map/ppermute | solution.py:327
  19.5 1.2 %sigma_near.1 = (bf16[128,256]{1,0:T(8,128)(2,1)S(1)}, bf16[128,256]{1,0:T(8,128)(2,1)S(1)}, bf16[128,256]{1,0:T(8,128)(2,1)S(1)}) custom-call(s32[40,128]{1,0:T(8,128)S(1)} %get-tuple-element.35.alpha_ref, bf16[5120,256]{1,0:T(8,128)(2,1)S(1)} %get-tuple-element.40.lifted), custom_call_target="tpu_custom_call" | custom-call | flops 1006632960 | tf_op jit(solution)/shard_map/sigma_near/pallas_call | solution.py:333
  20.7 1.6 %collective-permute-start.3 = (bf16[128,256]{1,0:T(8,128)(2,1)S(1)}, bf16[128,256]{1,0:T(8,128)(2,1)S(1)}, u32[]{:S(2)}, u32[]{:S(2)}) collective-permute-start(bf16[128,256]{1,0:T(8,128)(2,1)S(1)} %get-tuple-element.42), channel_id=1, source_target_pairs={{0,4},{4,0},{8,12},{12,8},{16,20},{20,16},{24,28},{28,24},{1,5},{5... | collective-permute-start | bytes 196616 | tf_op jit(solution)/shard_map/ppermute | solution.py:327
  22.3 1.6 %collective-permute-start.4 = (bf16[128,256]{1,0:T(8,128)(2,1)S(1)}, bf16[128,256]{1,0:T(8,128)(2,1)S(1)}, u32[]{:S(2)}, u32[]{:S(2)}) collective-permute-start(bf16[128,256]{1,0:T(8,128)(2,1)S(1)} %get-tuple-element.43), channel_id=1, source_target_pairs={{0,8},{4,12},{8,0},{12,4},{16,24},{20,28},{24,16},{28,20},{1,9},{5... | collective-permute-start | bytes 196616 | tf_op jit(solution)/shard_map/ppermute | solution.py:327
  23.9 0.0 collective-permute-done.6
  23.9 0.4 %collective-permute-start.5 = (bf16[128,256]{1,0:T(8,128)(2,1)S(1)}, bf16[128,256]{1,0:T(8,128)(2,1)S(1)}, u32[]{:S(2)}, u32[]{:S(2)}) collective-permute-start(bf16[128,256]{1,0:T(8,128)(2,1)S(1)} %get-tuple-element.44), channel_id=1, source_target_pairs={{0,12},{4,8},{8,4},{12,0},{16,28},{20,24},{24,20},{28,16},{1,13},{... | collective-permute-start | bytes 196616 | tf_op jit(solution)/shard_map/ppermute | solution.py:327
  24.3 0.0 collective-permute-done.7
  24.3 0.0 collective-permute-done.8
  24.3 2.7 %collective-permute-start.9 = (bf16[128,256]{1,0:T(8,128)(2,1)S(1)}, bf16[128,256]{1,0:T(8,128)(2,1)S(1)}, u32[]{:S(2)}, u32[]{:S(2)}) collective-permute-start(bf16[128,256]{1,0:T(8,128)(2,1)S(1)} %add_convert_fusion), channel_id=1, source_target_pairs={{0,16},{4,20},{8,24},{12,28},{16,0},{20,4},{24,8},{28,12},{1,17},{... | collective-permute-start | bytes 196616 | tf_op jit(solution)/shard_map/ppermute | solution.py:327
  27.0 0.5 %sigma_own.1 = f32[128,256]{1,0:T(8,128)S(1)} custom-call(s32[40,128]{1,0:T(8,128)S(1)} %get-tuple-element.35.alpha_ref, bf16[5120,256]{1,0:T(8,128)(2,1)S(1)} %get-tuple-element.40.lifted, f32[128,256]{1,0:T(8,128)S(1)} %get-tuple-element.41.same), custom_call_target="tpu_custom_call" | custom-call | flops 335544320 | tf_op jit(solution)/shard_map/sigma_own/pallas_call | solution.py:344
  27.5 0.0 collective-permute-done.3
  27.5 0.0 collective-permute-done.4
  27.5 1.5 %collective-permute-done.5 = bf16[128,256]{1,0:T(8,128)(2,1)S(1)} collective-permute-done((bf16[128,256]{1,0:T(8,128)(2,1)S(1)}, bf16[128,256]{1,0:T(8,128)(2,1)S(1)}, u32[]{:S(2)}, u32[]{:S(2)}) %collective-permute-start.5) | collective-permute-done | bytes 65568 | tf_op jit(solution)/shard_map/ppermute | solution.py:327
  29.0 0.5 %collective-permute-done.9 = bf16[128,256]{1,0:T(8,128)(2,1)S(1)} collective-permute-done((bf16[128,256]{1,0:T(8,128)(2,1)S(1)}, bf16[128,256]{1,0:T(8,128)(2,1)S(1)}, u32[]{:S(2)}, u32[]{:S(2)}) %collective-permute-start.9) | collective-permute-done | bytes 65568 | tf_op jit(solution)/shard_map/ppermute | solution.py:327
  29.5 0.7 %convert_add_fusion = f32[128,256]{1,0:T(8,128)} fusion(bf16[128,256]{1,0:T(8,128)(2,1)S(1)} %collective-permute-done.9, bf16[128,256]{1,0:T(8,128)(2,1)S(1)} %collective-permute-done.5, bf16[128,256]{1,0:T(8,128)(2,1)S(1)} %collective-permute-done.4, f32[128,256]{1,0:T(8,128)S(1)} %sigma_own.1, bf16[128,256]{1,0:T(8,128)(2,1)S(1)} %collective-permute-done.3), kind=kLoop, calls=%fused_computation | loop fusion | flops 262144 | bytes 524288 | tf_op jit(solution)/shard_map/add | solution.py:358
  (1 shorter events, 0.0 us)
Async XLA Ops:
  1.0 4.6 %collective-permute-start = (bf16[128,256]{1,0:T(8,128)(2,1)S(1)}, bf16[128,256]{1,0:T(8,128)(2,1)S(1)}, u32[]{:S(2)}, u32[]{:S(2)}) collective-permute-start(bf16[128,256]{1,0:T(8,128)(2,1)S(1)} %get-tuple-element.39.rest_0_), channel_id=1, source_target_pairs={{0,1},{1,0},{2,3},{3,2},{4,5},{5,4},{6,7},{7,6},{8,9},{9,8},{10,11... | collective-permute-start | bytes 196616 | tf_op jit(solution)/shard_map/ppermute | solution.py:269
  1.5 5.7 %collective-permute-start.2 = (bf16[128,256]{1,0:T(8,128)(2,1)S(1)}, bf16[128,256]{1,0:T(8,128)(2,1)S(1)}, u32[]{:S(2)}, u32[]{:S(2)}) collective-permute-start(bf16[128,256]{1,0:T(8,128)(2,1)S(1)} %get-tuple-element.39.rest_0_), channel_id=1, source_target_pairs={{0,3},{1,2},{2,1},{3,0},{4,7},{5,6},{6,5},{7,4},{8,11},{9,10},{10,... | collective-permute-start | bytes 196616 | tf_op jit(solution)/shard_map/ppermute | solution.py:269
  4.1 4.3 %collective-permute-start.1 = (bf16[128,256]{1,0:T(8,128)(2,1)S(1)}, bf16[128,256]{1,0:T(8,128)(2,1)S(1)}, u32[]{:S(2)}, u32[]{:S(2)}) collective-permute-start(bf16[128,256]{1,0:T(8,128)(2,1)S(1)} %get-tuple-element.39.rest_0_), channel_id=1, source_target_pairs={{0,2},{1,3},{2,0},{3,1},{4,6},{5,7},{6,4},{7,5},{8,10},{9,11},{10,... | collective-permute-start | bytes 196616 | tf_op jit(solution)/shard_map/ppermute | solution.py:269
  16.0 7.9 %collective-permute-start.6 = (bf16[128,256]{1,0:T(8,128)(2,1)S(1)}, bf16[128,256]{1,0:T(8,128)(2,1)S(1)}, u32[]{:S(2)}, u32[]{:S(2)}) collective-permute-start(bf16[128,256]{1,0:T(8,128)(2,1)S(1)} %get-tuple-element.46), channel_id=1, source_target_pairs={{0,12},{4,8},{8,4},{12,0},{16,28},{20,24},{24,20},{28,16},{1,13},{... | collective-permute-start | bytes 196616 | tf_op jit(solution)/shard_map/ppermute | solution.py:327
  18.6 5.7 %collective-permute-start.7 = (bf16[128,256]{1,0:T(8,128)(2,1)S(1)}, bf16[128,256]{1,0:T(8,128)(2,1)S(1)}, u32[]{:S(2)}, u32[]{:S(2)}) collective-permute-start(bf16[128,256]{1,0:T(8,128)(2,1)S(1)} %get-tuple-element.47), channel_id=1, source_target_pairs={{0,8},{4,12},{8,0},{12,4},{16,24},{20,28},{24,16},{28,20},{1,9},{5... | collective-permute-start | bytes 196616 | tf_op jit(solution)/shard_map/ppermute | solution.py:327
  19.0 5.3 %collective-permute-start.8 = (bf16[128,256]{1,0:T(8,128)(2,1)S(1)}, bf16[128,256]{1,0:T(8,128)(2,1)S(1)}, u32[]{:S(2)}, u32[]{:S(2)}) collective-permute-start(bf16[128,256]{1,0:T(8,128)(2,1)S(1)} %get-tuple-element.48), channel_id=1, source_target_pairs={{0,4},{4,0},{8,12},{12,8},{16,20},{20,16},{24,28},{28,24},{1,5},{5... | collective-permute-start | bytes 196616 | tf_op jit(solution)/shard_map/ppermute | solution.py:327
  20.7 6.8 %collective-permute-start.3 = (bf16[128,256]{1,0:T(8,128)(2,1)S(1)}, bf16[128,256]{1,0:T(8,128)(2,1)S(1)}, u32[]{:S(2)}, u32[]{:S(2)}) collective-permute-start(bf16[128,256]{1,0:T(8,128)(2,1)S(1)} %get-tuple-element.42), channel_id=1, source_target_pairs={{0,4},{4,0},{8,12},{12,8},{16,20},{20,16},{24,28},{28,24},{1,5},{5... | collective-permute-start | bytes 196616 | tf_op jit(solution)/shard_map/ppermute | solution.py:327
  22.3 5.2 %collective-permute-start.4 = (bf16[128,256]{1,0:T(8,128)(2,1)S(1)}, bf16[128,256]{1,0:T(8,128)(2,1)S(1)}, u32[]{:S(2)}, u32[]{:S(2)}) collective-permute-start(bf16[128,256]{1,0:T(8,128)(2,1)S(1)} %get-tuple-element.43), channel_id=1, source_target_pairs={{0,8},{4,12},{8,0},{12,4},{16,24},{20,28},{24,16},{28,20},{1,9},{5... | collective-permute-start | bytes 196616 | tf_op jit(solution)/shard_map/ppermute | solution.py:327
  23.9 5.2 %collective-permute-start.5 = (bf16[128,256]{1,0:T(8,128)(2,1)S(1)}, bf16[128,256]{1,0:T(8,128)(2,1)S(1)}, u32[]{:S(2)}, u32[]{:S(2)}) collective-permute-start(bf16[128,256]{1,0:T(8,128)(2,1)S(1)} %get-tuple-element.44), channel_id=1, source_target_pairs={{0,12},{4,8},{8,4},{12,0},{16,28},{20,24},{24,20},{28,16},{1,13},{... | collective-permute-start | bytes 196616 | tf_op jit(solution)/shard_map/ppermute | solution.py:327
  24.3 5.2 %collective-permute-start.9 = (bf16[128,256]{1,0:T(8,128)(2,1)S(1)}, bf16[128,256]{1,0:T(8,128)(2,1)S(1)}, u32[]{:S(2)}, u32[]{:S(2)}) collective-permute-start(bf16[128,256]{1,0:T(8,128)(2,1)S(1)} %add_convert_fusion), channel_id=1, source_target_pairs={{0,16},{4,20},{8,24},{12,28},{16,0},{20,4},{24,8},{28,12},{1,17},{... | collective-permute-start | bytes 196616 | tf_op jit(solution)/shard_map/ppermute | solution.py:327
